TPU v7x, 512 devices: a whole 4x8x8 slice. The times are simulated.
512 devices in a mesh: span: 4 (over y_lo), head: 8 (over x, core), seq: 16 (over z, y_hi).
Axes of the slice: x: 4, y: 8 (y_hi: 2, y_lo: 4; y = y_hi * 4 + y_lo), z: 8, core: 2. Of those that a mesh axis runs over, the one named last changes fastest.
Arguments:
- queries: bfloat16 [3072, 5120], P(('span', 'seq'), 'head'), may hold values from -8 to 8
- keys: bfloat16 [3072, 5120], P(('span', 'seq'), 'head'), may hold values from -8 to 8
- values: bfloat16 [3072, 5120], P(('span', 'seq'), 'head'), may hold values from -6 to 6
- out_weight: bfloat16 [5120, 5120], P('head', 'seq'), may hold values from -0.078125 to 0.078125
- gate_table: float32 [50, 5120], P(None, 'seq'), may hold values from 0.25 to 2
- noise_level: int32 [4], replicated, may hold values from 0 to 49
- span_order: int32 [4], replicated, may hold values from 0 to 3, each once
Outputs:
- branch: bfloat16 [3072, 5120], P(('span', 'head'), 'seq')
All inputs are finite; a program needn't handle non-finite values.
Results may differ from a plain program's by a relative error of at most 0.035.
Values may be sent and summed in bfloat16 or wider, within the bound.
No kernel may reach another device: no remote copies, remote signals or barrier semaphores. Data moves between devices by JAX's collectives and lax.ppermute only.
A program may use at most 64 MiB of HBM per device.

v0:
```python
import math

import jax
import jax.numpy as jnp
from jax import lax
from jax.sharding import PartitionSpec as P

HEAD_DIM = 128


key_block = 512


def block_update(carry, query_heads, key_rows, value_rows, scale):
    run_max, run_sum, accum = carry
    scores = (
        jnp.einsum("qhd,khd->hqk", query_heads, key_rows, preferred_element_type=jnp.float32)
        * scale
    )
    new_max = jnp.maximum(run_max, jnp.max(scores, axis=2))
    keeping = jnp.exp(run_max - new_max)
    weights = jnp.exp(scores - new_max[..., None])
    run_sum = run_sum * keeping + jnp.sum(weights, axis=2)
    accum = accum * keeping[..., None] + jnp.einsum(
        "hqk,khd->hqd", weights.astype(jnp.bfloat16), value_rows, preferred_element_type=jnp.float32
    )
    return (new_max, run_sum, accum)


def sweep_rows(carry, query_heads, key_piece, value_piece, scale):
    row_total = key_piece.shape[0]
    for begin in range(0, row_total, key_block):
        finish = min(row_total, begin + key_block)
        carry = block_update(
            carry, query_heads, key_piece[begin:finish], value_piece[begin:finish], scale
        )
    return carry


def keep_state(carry):
    return carry


def shards(queries, keys, values, out_weight, gate_table, noise_level, span_order):
    tok_rows = queries.shape[0]
    head_count = queries.shape[1] // HEAD_DIM
    span_count = lax.axis_size("span")
    my_span = lax.axis_index("span")
    my_place = span_order[my_span]
    scale = 1.0 / math.sqrt(HEAD_DIM)
    query_heads = queries.reshape(tok_rows, head_count, HEAD_DIM)
    gathered_keys, gathered_values = (
        lax.all_gather(keys, "span", axis=0, tiled=True),
        lax.all_gather(values, "span", axis=0, tiled=True),
    )
    stacked_keys = gathered_keys.reshape(span_count, tok_rows, head_count * HEAD_DIM)
    stacked_values = gathered_values.reshape(span_count, tok_rows, head_count * HEAD_DIM)
    visible = span_order <= my_place
    start_state = (
        jnp.full((head_count, tok_rows), -jnp.inf, jnp.float32),
        jnp.zeros((head_count, tok_rows), jnp.float32),
        jnp.zeros((head_count, tok_rows, HEAD_DIM), jnp.float32),
    )
    carry = start_state
    key_piece = lax.all_gather(stacked_keys, "seq", axis=1, tiled=True)
    value_piece = lax.all_gather(stacked_values, "seq", axis=1, tiled=True)
    row_total = key_piece.shape[1]
    key_piece = key_piece.reshape(span_count, row_total, head_count, HEAD_DIM)
    value_piece = value_piece.reshape(span_count, row_total, head_count, HEAD_DIM)
    for source in range(span_count):
        key_span = key_piece[source]
        value_span = value_piece[source]

        def update(state):
            return sweep_rows(state, query_heads, key_span, value_span, scale)

        carry = lax.cond(visible[source], update, keep_state, carry)
    run_max, run_sum, accum = carry
    attended = accum / run_sum[..., None]
    attended_local = (
        attended.transpose(1, 0, 2).reshape(tok_rows, head_count * HEAD_DIM).astype(jnp.bfloat16)
    )
    head_terms = jnp.dot(
        lax.all_gather(attended_local, "seq", axis=0, tiled=True),
        out_weight,
        preferred_element_type=jnp.float32,
    )
    summed = lax.psum_scatter(
        head_terms.astype(jnp.bfloat16), "head", scatter_dimension=0, tiled=True
    ).astype(jnp.float32)
    gate_row = lax.dynamic_index_in_dim(gate_table, noise_level[my_span], 0, keepdims=False)
    return (summed * gate_row[None, :]).astype(jnp.bfloat16)


def solution(mesh):
    return jax.shard_map(
        shards,
        mesh=mesh,
        in_specs=(
            P(("span", "seq"), "head"),
            P(("span", "seq"), "head"),
            P(("span", "seq"), "head"),
            P("head", "seq"),
            P(None, "seq"),
            P(),
            P(),
        ),
        out_specs=P(("span", "head"), "seq"),
        check_vma=False,
    )
```

profile of v0, /device:TPU:8, one launch (start us, length us, event | category | flops | bytes accessed | tf_op | source)
XLA Modules:
  0.0 454.3 jit_solution(5472718091321877179)
XLA Ops:
  6.5 18.8 %all_gather.15 = bf16[192,640]{1,0:T(8,128)(2,1)} all-gather(bf16[48,640]{1,0:T(8,128)(2,1)} %param.16), channel_id=1, replica_groups=mesh['span'=4,'head'=8,'seq'=16] {'span'}, dimensions={0}, use_global_device_ids=true | all-gather | bytes 307200 | tf_op jit(solution)/shard_map/all_gather | solution.py:53
  25.4 14.8 %all_gather.17 = bf16[192,640]{1,0:T(8,128)(2,1)} all-gather(bf16[48,640]{1,0:T(8,128)(2,1)} %param.17), channel_id=1, replica_groups=mesh['span'=4,'head'=8,'seq'=16] {'span'}, dimensions={0}, use_global_device_ids=true | all-gather | bytes 307200 | tf_op jit(solution)/shard_map/all_gather | solution.py:54
  40.3 1.2 dynamic_slice.10
  41.5 1.3 broadcast_compare_fusion
  46.9 108.8 %all-gather.3.cloned.1.call-done = bf16[4,768,640]{2,1,0:T(8,128)(2,1)} async-done(((bf16[4,48,640]{2,1,0:T(8,128)(2,1)}), bf16[4,768,640]{2,1,0:T(8,128)(2,1)}) %all-gather.3.cloned.1.call-update) | async-done | bytes 3932176 | tf_op jit(solution)/shard_map/all_gather | solution.py:65
  155.7 1.7 fusion.73
  157.4 1.4 copy.37
  158.8 123.9 %all-gather.5.cloned.1.call-done = bf16[4,768,640]{2,1,0:T(8,128)(2,1)} async-done(((bf16[4,48,640]{2,1,0:T(8,128)(2,1)}), bf16[4,768,640]{2,1,0:T(8,128)(2,1)}) %all-gather.5.cloned.1.call-update) | async-done | bytes 3932176 | tf_op jit(solution)/shard_map/all_gather | solution.py:66
  282.8 2.6 fusion.72
  285.4 1.4 copy.38
  287.4 2.3 copy.43
  289.7 7.6 %conditional.4 = (f32[5,48]{1,0:T(8,128)}, f32[5,48]{1,0:T(8,128)S(1)}, f32[5,48,128]{2,1,0:T(8,128)S(1)}) conditional(s32[]{:T(128)} %bitcast.12, () %tuple.32, (bf16[768,5,128]{0,2,1:T(8,128)(2,1)}, bf16[48,5,128]{2,1,0:T(8,128)(2,1)S(1)}, bf16[768,5,128]{0,2,1:T(8,128)(2,1)}) %tuple.95), branch_computations={%region_0.0_spmd, %region_1.0_spmd} | conditional | flops 95570640 | bytes 8703960 | solution.py:77
  289.7 1.6 copy.39
  294.4 1.6 copy.41
  297.3 6.0 %conditional.5 = ((f32[5,48]{1,0:T(8,128)}, f32[5,48]{1,0:T(8,128)S(1)}, f32[5,48,128]{2,1,0:T(8,128)S(1)})) conditional(s32[]{:T(128)} %bitcast.11, (f32[5,48]{1,0:T(8,128)}, f32[5,48]{1,0:T(8,128)S(1)}, f32[5,48,128]{2,1,0:T(8,128)S(1)}) %conditional.4, (bf16[768,5,128]{0,2,1:T(8,128)(2,1)S(1)}, bf16[48,5,128]{2,1,0:T(8,128)(2,1)S(1)}, ...), branch_computations={%region_6.0_spmd, %region_7.0_spmd} | conditional | flops 95601600 | bytes 8835744 | solution.py:77
  301.1 1.6 copy.46
  303.3 20.5 %conditional.6 = ((f32[5,48]{1,0:T(8,128)}, f32[5,48]{1,0:T(8,128)S(1)}, f32[5,48,128]{2,1,0:T(8,128)S(1)})) conditional(s32[]{:T(128)} %bitcast.10, (f32[5,48]{1,0:T(8,128)}, f32[5,48]{1,0:T(8,128)S(1)}, f32[5,48,128]{2,1,0:T(8,128)S(1)}) %get-tuple-element.229, (bf16[4,768,640]{2,1,0:T(8,128)(2,1)}, bf16[48,5,128]{2,1,0:T(8,128)(2,1)S(1)}, ...), branch_computations={%region_12.0_spmd, %region_13.0_spmd} | conditional | flops 95601600 | bytes 24478112 | solution.py:77
  303.3 6.3 %copy.47 = bf16[4,768,640]{1,2,0:T(8,128)(2,1)} copy(bf16[4,768,640]{2,1,0:T(8,128)(2,1)} %get-tuple-element.153) | data formatting | bytes 7864320 | tf_op jit(solution)/shard_map
  309.6 1.0 slice.137
  310.8 1.1 slice.136
  314.7 6.3 %copy.49 = bf16[4,768,640]{1,2,0:T(8,128)(2,1)} copy(bf16[4,768,640]{2,1,0:T(8,128)(2,1)} %get-tuple-element.158) | data formatting | bytes 7864320 | tf_op jit(solution)/shard_map
  321.0 1.0 slice.139
  322.2 1.2 slice.138
  323.8 19.9 %conditional.7 = ((f32[5,48]{1,0:T(8,128)S(1)}, f32[5,48,128]{2,1,0:T(8,128)S(1)})) conditional(s32[]{:T(128)} %bitcast.9, (f32[5,48]{1,0:T(8,128)S(1)}, f32[5,48,128]{2,1,0:T(8,128)S(1)}) %tuple.36, (bf16[4,768,640]{2,1,0:T(8,128)(2,1)}, bf16[48,5,128]{2,1,0:T(8,128)(2,1)S(1)}, f32[5,48]{1,0:T(8,128)}, f32[5,48]{1,0:T(8,128)S(1)}, ...), branch_computations={%region_18.0_spmd, %region_19.0_spmd} | conditional | flops 95601600 | bytes 24476184 | solution.py:77
  323.8 6.3 %copy.50 = bf16[4,768,640]{1,2,0:T(8,128)(2,1)} copy(bf16[4,768,640]{2,1,0:T(8,128)(2,1)} %get-tuple-element.159) | data formatting | bytes 7864320 | tf_op jit(solution)/shard_map
  331.3 1.1 slice.140
  334.6 6.3 %copy.52 = bf16[4,768,640]{1,2,0:T(8,128)(2,1)} copy(bf16[4,768,640]{2,1,0:T(8,128)(2,1)} %get-tuple-element.164) | data formatting | bytes 7864320 | tf_op jit(solution)/shard_map
  342.1 1.2 slice.142
  343.8 66.6 %all_gather.19 = bf16[768,640]{1,0:T(8,128)(2,1)S(1)} all-gather(bf16[48,640]{1,0:T(8,128)(2,1)S(1)} %copy_bitcast_fusion), channel_id=1, replica_groups=mesh['span'=4,'head'=8,'seq'=16] {'seq'}, dimensions={0}, use_global_device_ids=true | all-gather | bytes 1044480 | tf_op jit(solution)/shard_map/all_gather | solution.py:84
  410.5 1.5 convolution_convert_fusion
  415.3 30.9 %reduce-scatter.2.cloned.1.call-done = bf16[96,320]{1,0:T(8,128)(2,1)} async-done(((bf16[768,320]{1,0:T(8,128)(2,1)}), bf16[96,320]{1,0:T(8,128)(2,1)}) %reduce-scatter.2.cloned.1.call-update) | async-done | bytes 61456 | tf_op jit(solution)/shard_map/reduce_scatter | solution.py:88
  446.2 1.5 multiply_convert_fusion
  (53 shorter events, 21.1 us)
Async XLA Ops:
  6.5 403.9 %copy-start = (bf16[640,320]{0,1:T(8,128)(2,1)S(1)}, bf16[640,320]{0,1:T(8,128)(2,1)}, u32[]{:S(2)}) copy-start(bf16[640,320]{0,1:T(8,128)(2,1)} %param.18) | copy-start | bytes 1228804
  6.5 149.2 %all-gather.3.cloned.1.call-start = ((), (), s32[]{:S(2)}) async-start(), calls=%async_computation.1 | async-start | bytes 4177920 | tf_op jit(solution)/shard_map/all_gather | solution.py:65
  25.4 257.4 %all-gather.5.cloned.1.call-start = ((), (), s32[]{:S(2)}) async-start(), calls=%async_computation.2 | async-start | bytes 4177920 | tf_op jit(solution)/shard_map/all_gather | solution.py:66
  40.2 406.0 %reduce-scatter.2.cloned.1.call-start = ((), (), s32[]{:S(2)}) async-start(), calls=%async_computation.3 | async-start | bytes 663552 | tf_op jit(solution)/shard_map/reduce_scatter | solution.py:88
  343.7 68.3 %copy-start.1 = (s32[4]{0:T(128)S(1)}, s32[4]{0:T(128)}, u32[]{:S(2)}) copy-start(s32[4]{0:T(128)} %param.20) | copy-start | bytes 52
Sparse Core Ops, SparseCore 0:
  25.5 130.1 all-gather.2
  158.9 123.7 all-gather.4
  412.1 34.0 reduce-scatter.1
where the time goes:
time: 450 us; the launch traced here: 454 us
  waiting for transfers between devices  264 us (59%)
  blocking collectives  100 us (22%)
  local copies, waits for them, and re-layouts  54.5 us (12%)
  between operations  17.6 us (4%)
  other arithmetic  10.7 us (2%)
  matrix products  7.23 us (2%)
    all_gather x1, waiting for transfers between devices, shards(): value_piece = lax.all_gather(stacked_values, 'seq', axis=1, tiled=True)  124 us
    all_gather x1, waiting for transfers between devices, shards(): key_piece = lax.all_gather(stacked_keys, 'seq', axis=1, tiled=True)  109 us
    all_gather x1, blocking collectives, shards(): lax.all_gather(attended_local, 'seq', axis=0, tiled=True)  66.6 us
    reduce_scatter x1, waiting for transfers between devices, shards(): lax.psum_scatter(head_terms.astype(jnp.bfloat16), 'head', scatter_dimensi...  30.9 us
    another operation x8, local copies, waits for them, and re-layouts  30.6 us
    all_gather x1, blocking collectives, shards(): lax.all_gather(keys, 'span', axis=0, tiled=True)  18.8 us
    all_gather x1, blocking collectives, shards(): lax.all_gather(values, 'span', axis=0, tiled=True)  14.8 us
  transfers between devices with their start and end apart: 3, of which 3 were waited for; matrix products, arithmetic and copies ran while one was open for 2% of the time, Pallas kernels for 0%

commit v1 on v0

v1 whole, which is shorter than its diff:
```python
import functools
import math

import jax
import jax.numpy as jnp
from jax import lax
from jax.experimental import pallas as pl
from jax.experimental.pallas import tpu as pltpu
from jax.sharding import PartitionSpec as P

HEAD_DIM = 128
SPANS = 4
GROUPS = 8
HEADS_HERE = 5
BLOCKS = 3
PLACES = 16
ROWS = 48
QROWS = ROWS // BLOCKS
SPAN_ROWS = PLACES * ROWS
QBLOCK = PLACES * QROWS
PIECE = QBLOCK // GROUPS
STATS = 8
HIDDEN = -1.0e30
EXP2_SCALE = math.log2(math.e) / math.sqrt(HEAD_DIM)
VMEM = pl.BlockSpec(memory_space=pltpu.VMEM)
SMEM = pl.BlockSpec(memory_space=pltpu.SMEM)


def params(mib=24):
    return pltpu.CompilerParams(vmem_limit_bytes=mib * 2**20)


def pack_kernel(q_ref, k_ref, v_ref, out_ref):
    for head in range(HEADS_HERE):
        cols = slice(head * HEAD_DIM, (head + 1) * HEAD_DIM)
        key_rows = k_ref[:, cols]
        value_rows = v_ref[:, cols]
        for block in range(BLOCKS):
            place = head * BLOCKS + block
            out_ref[place, :QROWS, :] = q_ref[block * QROWS : (block + 1) * QROWS, cols]
            out_ref[place, QROWS : QROWS + ROWS, :] = key_rows
            out_ref[place, QROWS + ROWS :, :] = value_rows
    for place in range(HEADS_HERE * BLOCKS, PLACES):
        out_ref[place] = jnp.zeros(out_ref.shape[1:], out_ref.dtype)


def split_three(x):
    high = x.astype(jnp.bfloat16)
    rest = x - high.astype(jnp.float32)
    middle = rest.astype(jnp.bfloat16)
    low = (rest - middle.astype(jnp.float32)).astype(jnp.bfloat16)
    return high, middle, low


def attend_kernel(order_ref, me_ref, rows_ref, q_ref, out_ref):
    my_place = order_ref[me_ref[0]]
    keys = rows_ref[:, QROWS : QROWS + ROWS, :].reshape(SPAN_ROWS, HEAD_DIM)
    values = rows_ref[:, QROWS + ROWS :, :].reshape(SPAN_ROWS, HEAD_DIM)

    for span in range(SPANS):
        seen = my_place <= order_ref[span]

        @pl.when(seen)
        def _():
            scores = lax.dot_general(
                q_ref[span], keys, (((1,), (1,)), ((), ())), preferred_element_type=jnp.float32
            )
            scores = scores * EXP2_SCALE
            highest = jnp.max(scores, axis=1, keepdims=True)
            weights = jnp.exp2(scores - highest)
            total = jnp.sum(weights, axis=1, keepdims=True)
            mixed = jnp.dot(
                weights.astype(jnp.bfloat16), values, preferred_element_type=jnp.float32
            )
            mixed = (mixed / total).astype(jnp.bfloat16)
            logsum = highest + jnp.log2(total)
            wide = jnp.transpose(jnp.broadcast_to(logsum, (QBLOCK, HEAD_DIM)))
            terms = split_three(wide[:STATS])
            for group in range(GROUPS):
                piece = span * GROUPS + group
                out_ref[piece, :PIECE, :] = mixed[group * PIECE : (group + 1) * PIECE]
                half = group * PIECE // HEAD_DIM
                lanes = slice(half * HEAD_DIM, (half + 1) * HEAD_DIM)
                which = lax.broadcasted_iota(jnp.int32, (STATS, HEAD_DIM), 0)
                high, middle, low = (t[:, lanes].astype(jnp.float32) for t in terms)
                stat = jnp.where(which == 0, high, jnp.where(which == 1, middle, low))
                out_ref[piece, PIECE:, :] = stat.astype(jnp.bfloat16)

        @pl.when(jnp.logical_not(seen))
        def _():
            for group in range(GROUPS):
                piece = span * GROUPS + group
                out_ref[piece, :PIECE, :] = jnp.zeros((PIECE, HEAD_DIM), jnp.bfloat16)
                out_ref[piece, PIECE:, :] = jnp.full((STATS, HEAD_DIM), HIDDEN, jnp.bfloat16)


def merge_kernel(group_ref, parts_ref, out_ref, turn_ref):
    stats = parts_ref[:, PIECE:, :].astype(jnp.float32)
    logsum = stats[:, 0, :] + stats[:, 1, :] + stats[:, 2, :]
    pad = jnp.zeros((HEAD_DIM - SPANS * GROUPS, HEAD_DIM), jnp.float32)
    turn_ref[...] = jnp.transpose(jnp.concatenate([logsum, pad], axis=0))
    begin = lax.rem(group_ref[0], HEAD_DIM // PIECE) * PIECE
    mine = turn_ref[pl.ds(pl.multiple_of(begin, PIECE), PIECE), :]
    for group in range(GROUPS):
        cols = [mine[:, s * GROUPS + group : s * GROUPS + group + 1] for s in range(SPANS)]
        highest = functools.reduce(jnp.maximum, cols)
        shares = [jnp.exp2(c - highest) for c in cols]
        total = functools.reduce(jnp.add, shares)
        mixed = jnp.zeros((PIECE, HEAD_DIM), jnp.float32)
        for s in range(SPANS):
            part = parts_ref[s * GROUPS + group, :PIECE, :].astype(jnp.float32)
            mixed = mixed + part * (shares[s] / total)
        mixed = mixed.astype(jnp.bfloat16)
        for place in range(PLACES):
            out_ref[place, :, group * HEAD_DIM : (group + 1) * HEAD_DIM] = mixed


def project_kernel(level_ref, rows_ref, weight_ref, gate_ref, out_ref):
    acc = jnp.zeros((BLOCKS * PIECE, out_ref.shape[1]), jnp.float32)
    width = HEADS_HERE * HEAD_DIM
    for head in range(HEADS_HERE):
        for pair in range(GROUPS // 2):
            lanes = slice(2 * pair * HEAD_DIM, 2 * (pair + 1) * HEAD_DIM)
            left = jnp.concatenate(
                [rows_ref[head * BLOCKS + b, :, lanes] for b in range(BLOCKS)], axis=0
            )
            first = 2 * pair * width + head * HEAD_DIM
            right = jnp.concatenate(
                [
                    weight_ref[first : first + HEAD_DIM, :],
                    weight_ref[first + width : first + width + HEAD_DIM, :],
                ],
                axis=0,
            )
            acc = acc + jnp.dot(left, right, preferred_element_type=jnp.float32)
    gated = (acc * gate_ref[pl.ds(level_ref[0], 1), :]).astype(jnp.bfloat16)
    for block in range(BLOCKS):
        for side in range(2):
            source = block * PIECE + side * QROWS
            target = side * ROWS + block * QROWS
            out_ref[target : target + QROWS, :] = gated[source : source + QROWS]


def shards(queries, keys, values, out_weight, gate_table, noise_level, span_order):
    my_span = lax.axis_index("span")
    my_group = lax.axis_index("head")
    weight = lax.all_gather(out_weight, "head", axis=0, tiled=True)
    packed = pl.pallas_call(
        pack_kernel,
        out_shape=jax.ShapeDtypeStruct((PLACES, QROWS + 2 * ROWS, HEAD_DIM), jnp.bfloat16),
        in_specs=[VMEM] * 3,
        out_specs=VMEM,
        compiler_params=params(),
        name="pack",
    )(queries, keys, values)
    rows = lax.all_to_all(packed, "seq", 0, 0, tiled=True)
    own = rows[:, :QROWS, :].reshape(QBLOCK, HEAD_DIM)
    q_all = lax.all_gather(own, "span", axis=0, tiled=False)
    parts = pl.pallas_call(
        attend_kernel,
        out_shape=jax.ShapeDtypeStruct((SPANS * GROUPS, PIECE + STATS, HEAD_DIM), jnp.bfloat16),
        in_specs=[SMEM, SMEM, VMEM, VMEM],
        out_specs=VMEM,
        compiler_params=params(),
        name="attend",
    )(span_order, my_span.reshape(1), rows, q_all)
    parts = lax.all_to_all(parts, ("span", "head"), 0, 0, tiled=True)
    merged = pl.pallas_call(
        merge_kernel,
        out_shape=jax.ShapeDtypeStruct((PLACES, PIECE, GROUPS * HEAD_DIM), jnp.bfloat16),
        in_specs=[SMEM, VMEM],
        out_specs=VMEM,
        scratch_shapes=[pltpu.VMEM((HEAD_DIM, HEAD_DIM), jnp.float32)],
        compiler_params=params(),
        name="merge",
    )(my_group.reshape(1), parts)
    merged = lax.all_to_all(merged, "seq", 0, 0, tiled=True)
    level = lax.dynamic_slice(noise_level, (my_span,), (1,))
    return pl.pallas_call(
        project_kernel,
        out_shape=jax.ShapeDtypeStruct((BLOCKS * PIECE, out_weight.shape[1]), jnp.bfloat16),
        in_specs=[SMEM, VMEM, VMEM, VMEM],
        out_specs=VMEM,
        compiler_params=params(),
        name="project",
    )(level, merged, weight, gate_table)


def solution(mesh):
    return jax.shard_map(
        shards,
        mesh=mesh,
        in_specs=(
            P(("span", "seq"), "head"),
            P(("span", "seq"), "head"),
            P(("span", "seq"), "head"),
            P("head", "seq"),
            P(None, "seq"),
            P(),
            P(),
        ),
        out_specs=P(("span", "head"), "seq"),
        check_vma=False,
    )
```

time: 450 us -> 149 us (0.33)
  the two profiles are of different devices: /device:TPU:8 before, /device:TPU:42 now
where the time goes in v1:
time: 149 us; the launch traced here: 148 us
  waiting for transfers between devices  74.5 us (50%)
  starting transfers between devices  32.2 us (22%)
  between operations  13.4 us (9%)
  blocking collectives  12.5 us (8%)
  local copies, waits for them, and re-layouts  7.89 us (5%)
  Pallas kernels  7.85 us (5%)
    all_to_all x1, waiting for transfers between devices, shards(): merged = lax.all_to_all(merged, 'seq', 0, 0, tiled=True)  48.8 us
    all_to_all x1, waiting for transfers between devices, shards(): rows = lax.all_to_all(packed, 'seq', 0, 0, tiled=True)  15.8 us
    all_to_all x1, starting transfers between devices, shards(): rows = lax.all_to_all(packed, 'seq', 0, 0, tiled=True)  15.7 us
    all_gather x1, blocking collectives, shards(): q_all = lax.all_gather(own, 'span', axis=0, tiled=False)  12.5 us
    all_to_all x1, waiting for transfers between devices, shards(): parts = lax.all_to_all(parts, ('span', 'head'), 0, 0, tiled=True)  9.84 us
    all_to_all x1, starting transfers between devices, shards(): merged = lax.all_to_all(merged, 'seq', 0, 0, tiled=True)  9.12 us
    all_to_all x1, starting transfers between devices, shards(): parts = lax.all_to_all(parts, ('span', 'head'), 0, 0, tiled=True)  7.38 us
    unnamed x15, local copies, waits for them, and re-layouts  7.28 us
  transfers between devices with their start and end apart: 4, of which 3 were waited for; matrix products, arithmetic and copies ran while one was open for 0% of the time, Pallas kernels for 4%

profile of v1, /device:TPU:42, one launch (start us, length us, event | category | flops | bytes accessed | tf_op | source)
XLA Modules:
  0.0 148.3 jit_solution(9429571717538572025)
XLA Ops:
  6.5 0.0 all-gather.2.cloned.1.call-start
  6.5 2.0 %copy.9 = bf16[640,320]{1,0:T(8,128)(2,1)} copy(bf16[640,320]{0,1:T(8,128)(2,1)} %param.10) | data formatting | bytes 819200 | tf_op args[3]
  8.5 0.0 copy-start.6
  8.5 0.0 copy-start.1
  8.5 0.0 all-gather.2.cloned.1.call-update
  8.6 0.0 copy-start.2
  8.6 0.9 copy-done.2
  9.4 0.0 copy-start.3
  9.4 0.8 copy-done.3
  10.3 0.0 copy-start.4
  10.3 0.8 copy-done.4
  11.1 0.8 pack.1
  11.9 15.7 %all-to-all-start = ((bf16[16,112,128]{2,1,0:T(8,128)(2,1)}), bf16[16,112,128]{2,1,0:T(8,128)(2,1)S(1)}, u32[]{:S(2)}, u32[]{:S(2)}) async-start(bf16[16,112,128]{2,1,0:T(8,128)(2,1)} %pack.1), calls=%async_computation | async-start | bytes 917504 | tf_op jit(solution)/shard_map/all_to_all | solution.py:156
  27.6 15.8 %all-to-all-done.rows_ref = bf16[16,112,128]{2,1,0:T(8,128)(2,1)S(1)} async-done(((bf16[16,112,128]{2,1,0:T(8,128)(2,1)}), bf16[16,112,128]{2,1,0:T(8,128)(2,1)S(1)}, u32[]{:S(2)}, u32[]{:S(2)}) %all-to-all-start) | async-done | bytes 458784 | tf_op jit(solution)/shard_map/all_to_all | solution.py:156
  43.4 12.5 %all_gather.6.q_ref = bf16[4,256,128]{2,1,0:T(8,128)(2,1)S(1)} all-gather(bf16[1,256,128]{2,1,0:T(8,128)(2,1)S(1)} %bitcast.3), channel_id=1, replica_groups=mesh['span'=4,'head'=8,'seq'=16] {'span'}, dimensions={0}, use_global_device_ids=true | all-gather | bytes 327680 | tf_op jit(solution)/shard_map/all_gather | solution.py:158
  55.9 0.0 copy-start.5
  55.9 0.7 copy-done.5
  56.6 3.2 %attend.1 = bf16[32,40,128]{2,1,0:T(8,128)(2,1)} custom-call(s32[4]{0:T(128)S(1)} %copy-done.5, s32[1]{0:T(128)} %bitcast.1.me_ref, bf16[16,112,128]{2,1,0:T(8,128)(2,1)S(1)} %all-to-all-done.rows_ref, bf16[4,256,128]{2,1,0:T(8,128)(2,1)S(1)} %all_gather.6.q_ref), custom_call_target="tpu_custom_call" | custom-call | tf_op jit(solution)/shard_map/attend/pallas_call | solution.py:159
  59.8 7.4 %all-to-all-start.1 = ((bf16[32,40,128]{2,1,0:T(8,128)(2,1)}), bf16[32,40,128]{2,1,0:T(8,128)(2,1)S(1)}, u32[]{:S(2)}, u32[]{:S(2)}) async-start(bf16[32,40,128]{2,1,0:T(8,128)(2,1)} %attend.1), calls=%async_computation.1 | async-start | bytes 655360 | tf_op jit(solution)/shard_map/all_to_all | solution.py:167
  67.2 9.8 %all-to-all-done.1.parts_ref = bf16[32,40,128]{2,1,0:T(8,128)(2,1)S(1)} async-done(((bf16[32,40,128]{2,1,0:T(8,128)(2,1)}), bf16[32,40,128]{2,1,0:T(8,128)(2,1)S(1)}, u32[]{:S(2)}, u32[]{:S(2)}) %all-to-all-start.1) | async-done | bytes 327712 | tf_op jit(solution)/shard_map/all_to_all | solution.py:167
  77.0 1.7 %merge.1 = bf16[16,32,1024]{2,1,0:T(8,128)(2,1)} custom-call(s32[1]{0:T(128)} %bitcast.group_ref, bf16[32,40,128]{2,1,0:T(8,128)(2,1)S(1)} %all-to-all-done.1.parts_ref), custom_call_target="tpu_custom_call" | custom-call | tf_op jit(solution)/shard_map/merge/pallas_call | solution.py:168
  78.7 9.1 %all-to-all-start.2 = ((bf16[16,32,1024]{2,1,0:T(8,128)(2,1)}), bf16[16,32,1024]{2,1,0:T(8,128)(2,1)S(1)}, u32[]{:S(2)}, u32[]{:S(2)}) async-start(bf16[16,32,1024]{2,1,0:T(8,128)(2,1)} %merge.1), calls=%async_computation.2 | async-start | bytes 2097152 | tf_op jit(solution)/shard_map/all_to_all | solution.py:177
  87.8 0.0 copy-done.6
  87.8 0.6 dynamic_slice.3.level_ref
  88.4 48.8 %all-to-all-done.2.rows_ref = bf16[16,32,1024]{2,1,0:T(8,128)(2,1)S(1)} async-done(((bf16[16,32,1024]{2,1,0:T(8,128)(2,1)}), bf16[16,32,1024]{2,1,0:T(8,128)(2,1)S(1)}, u32[]{:S(2)}, u32[]{:S(2)}) %all-to-all-start.2) | async-done | bytes 1048608 | tf_op jit(solution)/shard_map/all_to_all | solution.py:177
  137.3 0.0 all-gather.2.cloned.1.call-done.weight_ref
  137.3 0.0 copy-done.1
  137.3 0.0 copy-start
  137.3 2.1 %copy-done = bf16[5120,320]{1,0:T(8,128)(2,1)S(1)} copy-done((bf16[5120,320]{1,0:T(8,128)(2,1)S(1)}, bf16[5120,320]{1,0:T(8,128)(2,1)}, u32[]{:S(2)}) %copy-start) | copy-done | bytes 3276824
  139.4 2.1 %project.1 = bf16[96,320]{1,0:T(8,128)(2,1)} custom-call(s32[1]{0:T(128)} %dynamic_slice.3.level_ref, bf16[16,32,1024]{2,1,0:T(8,128)(2,1)S(1)} %all-to-all-done.2.rows_ref, bf16[5120,320]{1,0:T(8,128)(2,1)S(1)} %copy-done, f32[50,320]{1,0:T(8,128)S(1)} %copy-done.1), custom_call_target="tpu_custom_call" | custom-call | tf_op jit(solution)/shard_map/project/pallas_call | solution.py:179
  (1 shorter events, 0.0 us)
Async XLA Ops:
  6.5 130.7 %all-gather.2.cloned.1.call-start = ((), (), s32[]{:S(2)}) async-start(), calls=%async_computation.3 | async-start | bytes 4423680 | tf_op jit(solution)/shard_map/all_gather | solution.py:147
  8.5 79.3 %copy-start.6 = (s32[4]{0:T(128)S(1)}, s32[4]{0:T(128)}, u32[]{:S(2)}) copy-start(s32[4]{0:T(128)} %param.12) | copy-start | bytes 52
  8.5 128.7 %copy-start.1 = (f32[50,320]{1,0:T(8,128)S(1)}, f32[50,320]{1,0:T(8,128)}, u32[]{:S(2)}) copy-start(f32[50,320]{1,0:T(8,128)} %gate_ref.1) | copy-start | bytes 192004
  8.6 0.9 copy-start.2
  9.4 0.8 copy-start.3
  10.3 0.8 copy-start.4
  11.9 31.5 %all-to-all-start = ((bf16[16,112,128]{2,1,0:T(8,128)(2,1)}), bf16[16,112,128]{2,1,0:T(8,128)(2,1)S(1)}, u32[]{:S(2)}, u32[]{:S(2)}) async-start(bf16[16,112,128]{2,1,0:T(8,128)(2,1)} %pack.1), calls=%async_computation | async-start | bytes 917504 | tf_op jit(solution)/shard_map/all_to_all | solution.py:156
  55.9 0.7 copy-start.5
  59.8 17.2 %all-to-all-start.1 = ((bf16[32,40,128]{2,1,0:T(8,128)(2,1)}), bf16[32,40,128]{2,1,0:T(8,128)(2,1)S(1)}, u32[]{:S(2)}, u32[]{:S(2)}) async-start(bf16[32,40,128]{2,1,0:T(8,128)(2,1)} %attend.1), calls=%async_computation.1 | async-start | bytes 655360 | tf_op jit(solution)/shard_map/all_to_all | solution.py:167
  78.7 58.5 %all-to-all-start.2 = ((bf16[16,32,1024]{2,1,0:T(8,128)(2,1)}), bf16[16,32,1024]{2,1,0:T(8,128)(2,1)S(1)}, u32[]{:S(2)}, u32[]{:S(2)}) async-start(bf16[16,32,1024]{2,1,0:T(8,128)(2,1)} %merge.1), calls=%async_computation.2 | async-start | bytes 2097152 | tf_op jit(solution)/shard_map/all_to_all | solution.py:177
  137.3 2.1 %copy-start = (bf16[5120,320]{1,0:T(8,128)(2,1)S(1)}, bf16[5120,320]{1,0:T(8,128)(2,1)}, u32[]{:S(2)}) copy-start(bf16[5120,320]{1,0:T(8,128)(2,1)} %all-gather.2.cloned.1.call-done.weight_ref) | copy-start | bytes 9830404
Sparse Core Ops, SparseCore 0:
  9.5 39.4 all-gather.1

commit v2 on v1

v2 whole, which is shorter than its diff:
```python
import functools
import math

import jax
import jax.numpy as jnp
from jax import lax
from jax.experimental import pallas as pl
from jax.experimental.pallas import tpu as pltpu
from jax.sharding import PartitionSpec as P

HEAD_DIM = 128
SPANS = 4
GROUPS = 8
HEADS_HERE = 5
BLOCKS = 3
PLACES = 16
ROWS = 48
QROWS = ROWS // BLOCKS
KROWS = ROWS // SPANS
KBLOCK = PLACES * KROWS
QBLOCK = PLACES * QROWS
PIECE = QBLOCK // GROUPS
STATS = 8
EXP2_SCALE = math.log2(math.e) / math.sqrt(HEAD_DIM)
VMEM = pl.BlockSpec(memory_space=pltpu.VMEM)
ANY = pl.BlockSpec(memory_space=pl.ANY)
SMEM = pl.BlockSpec(memory_space=pltpu.SMEM)


def params(mib=24):
    return pltpu.CompilerParams(vmem_limit_bytes=mib * 2**20)


def pack_kernel(q_hbm, k_hbm, v_hbm, out_ref, q_ref, k_ref, v_ref, kv_ref, sems):
    copies = [
        pltpu.make_async_copy(source, target, sems.at[i])
        for i, (source, target) in enumerate(((q_hbm, q_ref), (k_hbm, k_ref), (v_hbm, v_ref)))
    ]
    for copy in copies:
        copy.start()
    for span in range(SPANS):
        for place in range(HEADS_HERE * BLOCKS, PLACES):
            out_ref[span * PLACES + place] = jnp.zeros(out_ref.shape[1:], out_ref.dtype)
    copies[0].wait()
    for head in range(HEADS_HERE):
        cols = slice(head * HEAD_DIM, (head + 1) * HEAD_DIM)
        for block in range(BLOCKS):
            part = q_ref[block * QROWS : (block + 1) * QROWS, cols]
            for span in range(SPANS):
                out_ref[span * PLACES + head * BLOCKS + block, :QROWS, :] = part
    copies[1].wait()
    copies[2].wait()
    key_rows = k_ref[...].astype(jnp.float32)
    value_rows = v_ref[...].astype(jnp.float32)
    for span in range(SPANS):
        kv_ref[span, :KROWS, :] = key_rows[span * KROWS : (span + 1) * KROWS]
        kv_ref[span, KROWS:, :] = value_rows[span * KROWS : (span + 1) * KROWS]
    for span in range(SPANS):
        both = kv_ref[span].astype(jnp.bfloat16)
        for head in range(HEADS_HERE):
            part = both[:, head * HEAD_DIM : (head + 1) * HEAD_DIM]
            for block in range(BLOCKS):
                out_ref[span * PLACES + head * BLOCKS + block, QROWS:, :] = part


def split_three(x):
    high = x.astype(jnp.bfloat16)
    rest = x - high.astype(jnp.float32)
    middle = rest.astype(jnp.bfloat16)
    low = (rest - middle.astype(jnp.float32)).astype(jnp.bfloat16)
    return high, middle, low


def attend_kernel(order_ref, rows_ref, out_ref, keys_ref, values_ref):
    which = lax.broadcasted_iota(jnp.int32, (STATS, HEAD_DIM), 0)
    for turn in range(SPANS):
        span = jnp.int32(0)
        for other in range(1, SPANS):
            span = span + jnp.where(order_ref[other] == turn, other, 0)
        first = span * PLACES
        for place in range(PLACES):
            both = rows_ref[first + place, QROWS:, :].astype(jnp.float32)
            target = turn * KBLOCK + place * KROWS
            keys_ref[target : target + KROWS, :] = both[:KROWS]
            values_ref[target : target + KROWS, :] = both[KROWS:]
        seen = (turn + 1) * KBLOCK
        keys = keys_ref[:seen, :].astype(jnp.bfloat16)
        values = values_ref[:seen, :].astype(jnp.bfloat16)
        own = rows_ref[pl.ds(first, PLACES), :QROWS, :].reshape(QBLOCK, HEAD_DIM)
        scores = lax.dot_general(
            own, keys, (((1,), (1,)), ((), ())), preferred_element_type=jnp.float32
        )
        scores = scores * EXP2_SCALE
        highest = jnp.max(scores, axis=1, keepdims=True)
        weights = jnp.exp2(scores - highest)
        total = jnp.sum(weights, axis=1, keepdims=True)
        mixed = jnp.dot(weights.astype(jnp.bfloat16), values, preferred_element_type=jnp.float32)
        mixed = (mixed / total).astype(jnp.bfloat16)
        logsum = highest + jnp.log2(total)
        wide = jnp.transpose(jnp.broadcast_to(logsum, (QBLOCK, HEAD_DIM)))
        high, middle, low = (t.astype(jnp.float32) for t in split_three(wide[:STATS]))
        for group in range(GROUPS):
            half = group * PIECE // HEAD_DIM
            lanes = slice(half * HEAD_DIM, (half + 1) * HEAD_DIM)
            stat = jnp.where(
                which == 0, high[:, lanes], jnp.where(which == 1, middle[:, lanes], low[:, lanes])
            )
            piece = span * GROUPS + group
            out_ref[piece, :PIECE, :] = mixed[group * PIECE : (group + 1) * PIECE]
            out_ref[piece, PIECE:, :] = stat.astype(jnp.bfloat16)


def merge_kernel(group_ref, parts_ref, out_ref, turn_ref):
    stats = parts_ref[:, PIECE:, :].astype(jnp.float32)
    logsum = stats[:, 0, :] + stats[:, 1, :] + stats[:, 2, :]
    pad = jnp.zeros((HEAD_DIM - SPANS * GROUPS, HEAD_DIM), jnp.float32)
    turn_ref[...] = jnp.transpose(jnp.concatenate([logsum, pad], axis=0))
    begin = lax.rem(group_ref[0], HEAD_DIM // PIECE) * PIECE
    mine = turn_ref[pl.ds(pl.multiple_of(begin, PIECE), PIECE), :]
    for group in range(GROUPS):
        cols = [mine[:, s * GROUPS + group : s * GROUPS + group + 1] for s in range(SPANS)]
        highest = functools.reduce(jnp.maximum, cols)
        shares = [jnp.exp2(c - highest) for c in cols]
        total = functools.reduce(jnp.add, shares)
        mixed = jnp.zeros((PIECE, HEAD_DIM), jnp.float32)
        for s in range(SPANS):
            part = parts_ref[s * GROUPS + group, :PIECE, :].astype(jnp.float32)
            mixed = mixed + part * (shares[s] / total)
        mixed = mixed.astype(jnp.bfloat16)
        for place in range(PLACES):
            out_ref[place, :, group * HEAD_DIM : (group + 1) * HEAD_DIM] = mixed


def project_kernel(level_ref, rows_ref, weight_ref, gate_ref, out_ref):
    acc = jnp.zeros((BLOCKS * PIECE, out_ref.shape[1]), jnp.float32)
    for head in range(HEADS_HERE):
        for pair in range(GROUPS // 2):
            lanes = slice(2 * pair * HEAD_DIM, 2 * (pair + 1) * HEAD_DIM)
            left = jnp.concatenate(
                [rows_ref[head * BLOCKS + b, :, lanes] for b in range(BLOCKS)], axis=0
            )
            mine = slice(head * HEAD_DIM, (head + 1) * HEAD_DIM)
            right = jnp.concatenate(
                [weight_ref[2 * pair, :, mine], weight_ref[2 * pair + 1, :, mine]], axis=1
            )
            acc = acc + lax.dot_general(
                left, right, (((1,), (1,)), ((), ())), preferred_element_type=jnp.float32
            )
    gated = (acc * gate_ref[pl.ds(level_ref[0], 1), :]).astype(jnp.bfloat16)
    for block in range(BLOCKS):
        for side in range(2):
            source = block * PIECE + side * QROWS
            target = side * ROWS + block * QROWS
            out_ref[target : target + QROWS, :] = gated[source : source + QROWS]


def shards(queries, keys, values, out_weight, gate_table, noise_level, span_order):
    my_span = lax.axis_index("span")
    my_group = lax.axis_index("head")
    weight = lax.all_gather(out_weight.T, "head", axis=0, tiled=False)
    shard = (ROWS, HEADS_HERE * HEAD_DIM)
    packed = pl.pallas_call(
        pack_kernel,
        out_shape=jax.ShapeDtypeStruct((SPANS * PLACES, QROWS + 2 * KROWS, HEAD_DIM), jnp.bfloat16),
        in_specs=[ANY] * 3,
        out_specs=VMEM,
        scratch_shapes=[pltpu.VMEM(shard, jnp.bfloat16)] * 3
        + [
            pltpu.VMEM((SPANS, 2 * KROWS, shard[1]), jnp.float32),
            pltpu.SemaphoreType.DMA((3,)),
        ],
        compiler_params=params(),
        name="pack",
    )(queries, keys, values)
    rows = lax.all_to_all(packed, ("span", "seq"), 0, 0, tiled=True)
    parts = pl.pallas_call(
        attend_kernel,
        out_shape=jax.ShapeDtypeStruct((SPANS * GROUPS, PIECE + STATS, HEAD_DIM), jnp.bfloat16),
        in_specs=[SMEM, VMEM],
        out_specs=VMEM,
        scratch_shapes=[pltpu.VMEM((SPANS * KBLOCK, HEAD_DIM), jnp.float32)] * 2,
        compiler_params=params(),
        name="attend",
    )(span_order, rows)
    parts = lax.all_to_all(parts, ("span", "head"), 0, 0, tiled=True)
    parts, weight = lax.optimization_barrier((parts, weight))
    merged = pl.pallas_call(
        merge_kernel,
        out_shape=jax.ShapeDtypeStruct((PLACES, PIECE, GROUPS * HEAD_DIM), jnp.bfloat16),
        in_specs=[SMEM, VMEM],
        out_specs=VMEM,
        scratch_shapes=[pltpu.VMEM((HEAD_DIM, HEAD_DIM), jnp.float32)],
        compiler_params=params(),
        name="merge",
    )(my_group.reshape(1), parts)
    merged = lax.all_to_all(merged, "seq", 0, 0, tiled=True)
    level = lax.dynamic_slice(noise_level, (my_span,), (1,))
    return pl.pallas_call(
        project_kernel,
        out_shape=jax.ShapeDtypeStruct((BLOCKS * PIECE, out_weight.shape[1]), jnp.bfloat16),
        in_specs=[SMEM, VMEM, VMEM, VMEM],
        out_specs=VMEM,
        compiler_params=params(),
        name="project",
    )(level, merged, weight, gate_table)


def solution(mesh):
    return jax.shard_map(
        shards,
        mesh=mesh,
        in_specs=(
            P(("span", "seq"), "head"),
            P(("span", "seq"), "head"),
            P(("span", "seq"), "head"),
            P("head", "seq"),
            P(None, "seq"),
            P(),
            P(),
        ),
        out_specs=P(("span", "head"), "seq"),
        check_vma=False,
    )
```

time: 149 us -> 137 us (0.919)
  blocking collectives: 12.5 us -> 36.4 us
  starting transfers between devices: 32.2 us -> 14.3 us
  waiting for transfers between devices: 74.5 us -> 59.3 us
  local copies, waits for them, and re-layouts: 7.89 us -> 5.72 us
    all_to_all x0 -> x1, blocking collectives: none -> 36.4 us  [shards(): rows = lax.all_to_all(packed, ('span', 'seq'), 0, 0, tiled=True)]
    all_to_all x1 -> x0, waiting for transfers between devices: 15.8 us -> none  [shards(): rows = lax.all_to_all(packed, 'seq', 0, 0, tiled=True)]
    all_to_all x1 -> x0, starting transfers between devices: 15.7 us -> none  [shards(): rows = lax.all_to_all(packed, 'seq', 0, 0, tiled=True)]
    all_gather x1 -> x0, blocking collectives: 12.5 us -> none  [shards(): q_all = lax.all_gather(own, 'span', axis=0, tiled=False)]
    unnamed x15 -> x14, local copies, waits for them, and re-layouts: 7.28 us -> 5.07 us
    all_to_all x1, starting transfers between devices: 9.12 us -> 7.62 us  [shards(): merged = lax.all_to_all(merged, 'seq', 0, 0, tiled=True)]
  transfers between devices with their start and end apart: 4 -> 3, of which waited for: 3 -> 2; matrix products, arithmetic and copies ran while one was open for 0% -> 0% of each run, Pallas kernels for 4% -> 3%
where the time goes in v2:
time: 137 us
  waiting for transfers between devices  59.3 us (43%)
  blocking collectives  36.4 us (27%)
  starting transfers between devices  14.3 us (10%)
  between operations  13.4 us (10%)
  Pallas kernels  7.6 us (6%)
  local copies, waits for them, and re-layouts  5.72 us (4%)
    all_to_all x1, waiting for transfers between devices, shards(): merged = lax.all_to_all(merged, 'seq', 0, 0, tiled=True)  48.8 us
    all_to_all x1, blocking collectives, shards(): rows = lax.all_to_all(packed, ('span', 'seq'), 0, 0, tiled=True)  36.4 us
    all_to_all x1, waiting for transfers between devices, shards(): parts = lax.all_to_all(parts, ('span', 'head'), 0, 0, tiled=True)  9.84 us
    all_to_all x1, starting transfers between devices, shards(): merged = lax.all_to_all(merged, 'seq', 0, 0, tiled=True)  7.62 us
    all_to_all x1, starting transfers between devices, shards(): parts = lax.all_to_all(parts, ('span', 'head'), 0, 0, tiled=True)  6.7 us
    unnamed x14, local copies, waits for them, and re-layouts  5.07 us
    pallas_call x1, Pallas kernels, shards(): pl.pallas_call(attend_kernel, out_shape=jax.ShapeDtypeStruct((SPANS * GRO...  3.12 us
  transfers between devices with their start and end apart: 3, of which 2 were waited for; matrix products, arithmetic and copies ran while one was open for 0% of the time, Pallas kernels for 3%

profile of v2, /device:TPU:42, one launch (start us, length us, event | category | flops | bytes accessed | tf_op | source)
XLA Modules:
  0.0 136.8 jit_solution(9407738295904062612)
XLA Ops:
  6.5 0.0 all-gather.3.cloned.1.call-start
  6.5 0.7 all-gather.3.cloned.1.call-update
  7.3 0.0 copy-start.2
  7.3 0.8 copy-done.2
  8.1 0.0 copy-start.3
  8.1 0.8 copy-done.3
  8.9 0.0 copy-start.4
  8.9 0.8 copy-done.4
  9.7 0.3 pack.1
  10.1 0.0 copy-start.6
  10.1 0.0 copy-start.1
  10.1 36.4 %all_to_all.15.rows_ref = bf16[64,40,128]{2,1,0:T(8,128)(2,1)S(1)} all-to-all(bf16[64,40,128]{2,1,0:T(8,128)(2,1)S(1)} %pack.1), channel_id=1, replica_groups=mesh['span'=4,'head'=8,'seq'=16] {'span','seq'}, dimensions={0} | all-to-all | bytes 1310720 | tf_op jit(solution)/shard_map/all_to_all | solution.py:175
  46.5 0.0 copy-start.5
  46.5 0.7 copy-done.5
  47.2 3.1 %attend.1 = bf16[32,40,128]{2,1,0:T(8,128)(2,1)} custom-call(s32[4]{0:T(128)S(1)} %copy-done.5, bf16[64,40,128]{2,1,0:T(8,128)(2,1)S(1)} %all_to_all.15.rows_ref), custom_call_target="tpu_custom_call" | custom-call | tf_op jit(solution)/shard_map/attend/pallas_call | solution.py:176
  50.3 6.7 %all-to-all-start.1 = ((bf16[32,40,128]{2,1,0:T(8,128)(2,1)}), bf16[32,40,128]{2,1,0:T(8,128)(2,1)S(1)}, u32[]{:S(2)}, u32[]{:S(2)}) async-start(bf16[32,40,128]{2,1,0:T(8,128)(2,1)} %attend.1), calls=%async_computation.1 | async-start | bytes 655360 | tf_op jit(solution)/shard_map/all_to_all | solution.py:185
  57.0 9.8 %all-to-all-done.1.parts_ref = bf16[32,40,128]{2,1,0:T(8,128)(2,1)S(1)} async-done(((bf16[32,40,128]{2,1,0:T(8,128)(2,1)}), bf16[32,40,128]{2,1,0:T(8,128)(2,1)S(1)}, u32[]{:S(2)}, u32[]{:S(2)}) %all-to-all-start.1) | async-done | bytes 327712 | tf_op jit(solution)/shard_map/all_to_all | solution.py:185
  66.9 0.0 all-gather.3.cloned.1.call-done
  66.9 1.7 %merge.1 = bf16[16,32,1024]{2,1,0:T(8,128)(2,1)} custom-call(s32[1]{0:T(128)} %bitcast.group_ref, bf16[32,40,128]{2,1,0:T(8,128)(2,1)S(1)} %all-to-all-done.1.parts_ref), custom_call_target="tpu_custom_call" | custom-call | tf_op jit(solution)/shard_map/merge/pallas_call | solution.py:187
  68.6 7.6 %all-to-all-start.2 = ((bf16[16,32,1024]{2,1,0:T(8,128)(2,1)}), bf16[16,32,1024]{2,1,0:T(8,128)(2,1)S(1)}, u32[]{:S(2)}, u32[]{:S(2)}) async-start(bf16[16,32,1024]{2,1,0:T(8,128)(2,1)} %merge.1), calls=%async_computation.2 | async-start | bytes 2097152 | tf_op jit(solution)/shard_map/all_to_all | solution.py:196
  76.2 0.0 copy-done.6
  76.2 0.7 dynamic_slice.3.level_ref
  76.8 48.8 %all-to-all-done.2.rows_ref = bf16[16,32,1024]{2,1,0:T(8,128)(2,1)S(1)} async-done(((bf16[16,32,1024]{2,1,0:T(8,128)(2,1)}), bf16[16,32,1024]{2,1,0:T(8,128)(2,1)S(1)}, u32[]{:S(2)}, u32[]{:S(2)}) %all-to-all-start.2) | async-done | bytes 1048608 | tf_op jit(solution)/shard_map/all_to_all | solution.py:196
  125.6 0.0 copy-done.1
  125.6 0.0 copy-start
  125.6 1.9 %copy-done = bf16[2560,640]{1,0:T(8,128)(2,1)S(1)} copy-done((bf16[2560,640]{1,0:T(8,128)(2,1)S(1)}, bf16[2560,640]{1,0:T(8,128)(2,1)}, u32[]{:S(2)}) %copy-start) | copy-done | bytes 3276824
  127.5 2.5 %project.1 = bf16[96,320]{1,0:T(8,128)(2,1)} custom-call(s32[1]{0:T(128)} %dynamic_slice.3.level_ref, bf16[16,32,1024]{2,1,0:T(8,128)(2,1)S(1)} %all-to-all-done.2.rows_ref, bf16[8,320,640]{2,1,0:T(8,128)(2,1)S(1)} %bitcast.3, f32[50,320]{1,0:T(8,128)S(1)} %copy-done.1), custom_call_target="tpu_custom_call" | custom-call | tf_op jit(solution)/shard_map/project/pallas_call | solution.py:198
Async XLA Ops:
  6.5 60.3 %all-gather.3.cloned.1.call-start = ((), (), s32[]{:S(2)}) async-start(), calls=%async_computation.3 | async-start | bytes 3686400 | tf_op jit(solution)/shard_map/all_gather | solution.py:160
  7.3 0.8 copy-start.2
  8.1 0.8 copy-start.3
  8.9 0.8 copy-start.4
  10.1 66.1 %copy-start.6 = (s32[4]{0:T(128)S(1)}, s32[4]{0:T(128)}, u32[]{:S(2)}) copy-start(s32[4]{0:T(128)} %param.12) | copy-start | bytes 52
  10.1 115.5 %copy-start.1 = (f32[50,320]{1,0:T(8,128)S(1)}, f32[50,320]{1,0:T(8,128)}, u32[]{:S(2)}) copy-start(f32[50,320]{1,0:T(8,128)} %gate_ref.1) | copy-start | bytes 192004
  46.5 0.7 copy-start.5
  50.3 16.6 %all-to-all-start.1 = ((bf16[32,40,128]{2,1,0:T(8,128)(2,1)}), bf16[32,40,128]{2,1,0:T(8,128)(2,1)S(1)}, u32[]{:S(2)}, u32[]{:S(2)}) async-start(bf16[32,40,128]{2,1,0:T(8,128)(2,1)} %attend.1), calls=%async_computation.1 | async-start | bytes 655360 | tf_op jit(solution)/shard_map/all_to_all | solution.py:185
  68.6 57.0 %all-to-all-start.2 = ((bf16[16,32,1024]{2,1,0:T(8,128)(2,1)}), bf16[16,32,1024]{2,1,0:T(8,128)(2,1)S(1)}, u32[]{:S(2)}, u32[]{:S(2)}) async-start(bf16[16,32,1024]{2,1,0:T(8,128)(2,1)} %merge.1), calls=%async_computation.2 | async-start | bytes 2097152 | tf_op jit(solution)/shard_map/all_to_all | solution.py:196
  125.6 1.9 %copy-start = (bf16[2560,640]{1,0:T(8,128)(2,1)S(1)}, bf16[2560,640]{1,0:T(8,128)(2,1)}, u32[]{:S(2)}) copy-start(bf16[2560,640]{1,0:T(8,128)(2,1)} %all-gather.3.cloned.1.call-done) | copy-start | bytes 9830404
Sparse Core Ops, SparseCore 0:
  9.5 36.7 all-gather.2

commit v3 on v2

--- a/solution.py
+++ b/solution.py
@@ -10,6 +10,7 @@
 
 HEAD_DIM = 128
 SPANS = 4
+RING, CORES = 4, 2
 GROUPS = 8
 HEADS_HERE = 5
 BLOCKS = 3
@@ -23,7 +24,7 @@
 STATS = 8
 EXP2_SCALE = math.log2(math.e) / math.sqrt(HEAD_DIM)
 VMEM = pl.BlockSpec(memory_space=pltpu.VMEM)
-ANY = pl.BlockSpec(memory_space=pl.ANY)
+HBM = pl.BlockSpec(memory_space=pltpu.HBM)
 SMEM = pl.BlockSpec(memory_space=pltpu.SMEM)
 
 
@@ -110,15 +111,24 @@
             out_ref[piece, PIECE:, :] = stat.astype(jnp.bfloat16)
 
 
-def merge_kernel(group_ref, parts_ref, out_ref, turn_ref):
-    stats = parts_ref[:, PIECE:, :].astype(jnp.float32)
-    logsum = stats[:, 0, :] + stats[:, 1, :] + stats[:, 2, :]
+def merge_kernel(parts_ref, out_ref, turn_ref):
+    me = lax.axis_index("head")
+    ring, core = me // CORES, lax.rem(me, CORES)
+    slots = []
+    for step in range(RING):
+        there = lax.rem(ring + RING - step, RING) * CORES
+        slots += [there + core, there + (CORES - 1 - core)]
+    rows = []
+    for s in range(SPANS):
+        for group in slots:
+            stats = parts_ref[s * GROUPS + group, PIECE:, :].astype(jnp.float32)
+            rows.append(stats[0:1] + stats[1:2] + stats[2:3])
     pad = jnp.zeros((HEAD_DIM - SPANS * GROUPS, HEAD_DIM), jnp.float32)
-    turn_ref[...] = jnp.transpose(jnp.concatenate([logsum, pad], axis=0))
-    begin = lax.rem(group_ref[0], HEAD_DIM // PIECE) * PIECE
+    turn_ref[...] = jnp.transpose(jnp.concatenate(rows + [pad], axis=0))
+    begin = lax.rem(me, HEAD_DIM // PIECE) * PIECE
     mine = turn_ref[pl.ds(pl.multiple_of(begin, PIECE), PIECE), :]
-    for group in range(GROUPS):
-        cols = [mine[:, s * GROUPS + group : s * GROUPS + group + 1] for s in range(SPANS)]
+    for slot, group in enumerate(slots):
+        cols = [mine[:, s * GROUPS + slot : s * GROUPS + slot + 1] for s in range(SPANS)]
         highest = functools.reduce(jnp.maximum, cols)
         shares = [jnp.exp2(c - highest) for c in cols]
         total = functools.reduce(jnp.add, shares)
@@ -128,25 +138,27 @@
             mixed = mixed + part * (shares[s] / total)
         mixed = mixed.astype(jnp.bfloat16)
         for place in range(PLACES):
-            out_ref[place, :, group * HEAD_DIM : (group + 1) * HEAD_DIM] = mixed
-
-
-def project_kernel(level_ref, rows_ref, weight_ref, gate_ref, out_ref):
+            out_ref[place, :, slot * HEAD_DIM : (slot + 1) * HEAD_DIM] = mixed
+
+
+def project_kernel(level_ref, rows_ref, gate_ref, *refs):
+    blocks, out_ref = refs[:GROUPS], refs[GROUPS]
     acc = jnp.zeros((BLOCKS * PIECE, out_ref.shape[1]), jnp.float32)
-    for head in range(HEADS_HERE):
-        for pair in range(GROUPS // 2):
-            lanes = slice(2 * pair * HEAD_DIM, 2 * (pair + 1) * HEAD_DIM)
+    for pair in range(RING):
+        lanes = slice(2 * pair * HEAD_DIM, 2 * (pair + 1) * HEAD_DIM)
+        for head in range(HEADS_HERE):
             left = jnp.concatenate(
                 [rows_ref[head * BLOCKS + b, :, lanes] for b in range(BLOCKS)], axis=0
             )
             mine = slice(head * HEAD_DIM, (head + 1) * HEAD_DIM)
             right = jnp.concatenate(
-                [weight_ref[2 * pair, :, mine], weight_ref[2 * pair + 1, :, mine]], axis=1
+                [blocks[2 * pair][:, mine], blocks[2 * pair + 1][:, mine]], axis=1
             )
             acc = acc + lax.dot_general(
                 left, right, (((1,), (1,)), ((), ())), preferred_element_type=jnp.float32
             )
-    gated = (acc * gate_ref[pl.ds(level_ref[0], 1), :]).astype(jnp.bfloat16)
+    level = level_ref[lax.axis_index("span")]
+    gated = (acc * gate_ref[pl.ds(level, 1), :]).astype(jnp.bfloat16)
     for block in range(BLOCKS):
         for side in range(2):
             source = block * PIECE + side * QROWS
@@ -154,15 +166,23 @@
             out_ref[target : target + QROWS, :] = gated[source : source + QROWS]
 
 
+def along_ring(x, step):
+    moves = [
+        (r * CORES + c, (r + step) % RING * CORES + c) for r in range(RING) for c in range(CORES)
+    ]
+    return lax.ppermute(x, "head", moves)
+
+
+def across_cores(x):
+    return lax.ppermute(x, "head", [(g, g ^ 1) for g in range(GROUPS)])
+
+
 def shards(queries, keys, values, out_weight, gate_table, noise_level, span_order):
-    my_span = lax.axis_index("span")
-    my_group = lax.axis_index("head")
-    weight = lax.all_gather(out_weight.T, "head", axis=0, tiled=False)
     shard = (ROWS, HEADS_HERE * HEAD_DIM)
     packed = pl.pallas_call(
         pack_kernel,
         out_shape=jax.ShapeDtypeStruct((SPANS * PLACES, QROWS + 2 * KROWS, HEAD_DIM), jnp.bfloat16),
-        in_specs=[ANY] * 3,
+        in_specs=[HBM] * 3,
         out_specs=VMEM,
         scratch_shapes=[pltpu.VMEM(shard, jnp.bfloat16)] * 3
         + [
@@ -172,6 +192,8 @@
         compiler_params=params(),
         name="pack",
     )(queries, keys, values)
+    packed, weight = lax.optimization_barrier((packed, out_weight.T))
+    weights = [weight] + [along_ring(weight, step) for step in range(1, RING)]
     rows = lax.all_to_all(packed, ("span", "seq"), 0, 0, tiled=True)
     parts = pl.pallas_call(
         attend_kernel,
@@ -182,27 +204,29 @@
         compiler_params=params(),
         name="attend",
     )(span_order, rows)
+    parts, weights = lax.optimization_barrier((parts, weights))
+    others = [across_cores(w) for w in weights]
     parts = lax.all_to_all(parts, ("span", "head"), 0, 0, tiled=True)
-    parts, weight = lax.optimization_barrier((parts, weight))
+    parts, others = lax.optimization_barrier((parts, others))
+    blocks = [w for pair in zip(weights, others) for w in pair]
     merged = pl.pallas_call(
         merge_kernel,
         out_shape=jax.ShapeDtypeStruct((PLACES, PIECE, GROUPS * HEAD_DIM), jnp.bfloat16),
-        in_specs=[SMEM, VMEM],
+        in_specs=[VMEM],
         out_specs=VMEM,
         scratch_shapes=[pltpu.VMEM((HEAD_DIM, HEAD_DIM), jnp.float32)],
         compiler_params=params(),
         name="merge",
-    )(my_group.reshape(1), parts)
+    )(parts)
     merged = lax.all_to_all(merged, "seq", 0, 0, tiled=True)
-    level = lax.dynamic_slice(noise_level, (my_span,), (1,))
     return pl.pallas_call(
         project_kernel,
         out_shape=jax.ShapeDtypeStruct((BLOCKS * PIECE, out_weight.shape[1]), jnp.bfloat16),
-        in_specs=[SMEM, VMEM, VMEM, VMEM],
+        in_specs=[SMEM] + [VMEM] * (2 + GROUPS),
         out_specs=VMEM,
         compiler_params=params(),
         name="project",
-    )(level, merged, weight, gate_table)
+    )(noise_level, merged, gate_table, *blocks)
 
 
 def solution(mesh):

time: 137 us -> 115 us (0.84)
  the two profiles are of different devices: /device:TPU:42 before, /device:TPU:20 now
where the time goes in v3:
time: 115 us; the launch traced here: 114 us
  blocking collectives  47.1 us (41%)
  starting transfers between devices  42.2 us (37%)
  waiting for transfers between devices  14.2 us (12%)
  Pallas kernels  7.33 us (6%)
  local copies, waits for them, and re-layouts  3.28 us (3%)
    all_to_all x1, blocking collectives, shards(): merged = lax.all_to_all(merged, 'seq', 0, 0, tiled=True)  47.1 us
    all_to_all x1, starting transfers between devices, shards(): rows = lax.all_to_all(packed, ('span', 'seq'), 0, 0, tiled=True)  16.7 us
    all_to_all x1, waiting for transfers between devices, shards(): rows = lax.all_to_all(packed, ('span', 'seq'), 0, 0, tiled=True)  12 us
    ppermute x3, starting transfers between devices, along_ring(): return lax.ppermute(x, 'head', moves)  9 us
    ppermute x4, starting transfers between devices, across_cores(): return lax.ppermute(x, 'head', [(g, g ^ 1) for g in range(GROUPS)])  8.65 us
    all_to_all x1, starting transfers between devices, shards(): parts = lax.all_to_all(parts, ('span', 'head'), 0, 0, tiled=True)  7.78 us
    unnamed x18, local copies, waits for them, and re-layouts  3.28 us
    pallas_call x1, Pallas kernels, shards(): pl.pallas_call(attend_kernel, out_shape=jax.ShapeDtypeStruct((SPANS * GRO...  3.11 us
  transfers between devices with their start and end apart: 9, of which 3 were waited for; matrix products, arithmetic and copies ran while one was open for 0% of the time, Pallas kernels for 3%

profile of v3, /device:TPU:20, one launch (start us, length us, event | category | flops | bytes accessed | tf_op | source)
XLA Modules:
  0.0 114.3 jit_solution(15201582414725662424)
XLA Ops:
  0.0 0.8 copy-done.4
  0.8 0.8 copy-done.5
  1.7 0.8 copy-done.6
  2.5 1.2 %pack.1 = bf16[64,40,128]{2,1,0:T(8,128)(2,1)} custom-call(bf16[48,640]{1,0:T(8,128)(2,1)S(1)} %copy-done.4, bf16[48,640]{1,0:T(8,128)(2,1)S(1)} %copy-done.5, bf16[48,640]{1,0:T(8,128)(2,1)S(1)} %copy-done.6), custom_call_target="tpu_custom_call" | custom-call | tf_op jit(solution)/shard_map/pack/pallas_call | solution.py:182
  3.7 0.0 copy-start
  3.7 0.0 copy-start.7
  3.7 16.7 %all-to-all-start = ((bf16[64,40,128]{2,1,0:T(8,128)(2,1)}), bf16[64,40,128]{2,1,0:T(8,128)(2,1)S(1)}, u32[]{:S(2)}, u32[]{:S(2)}) async-start(bf16[64,40,128]{2,1,0:T(8,128)(2,1)} %pack.1), calls=%async_computation | async-start | bytes 1310720 | tf_op jit(solution)/shard_map/all_to_all | solution.py:197
  20.4 2.4 %collective-permute-start.2 = (bf16[320,640]{1,0:T(8,128)(2,1)S(1)}, bf16[320,640]{1,0:T(8,128)(2,1)S(1)}, u32[]{:S(2)}, u32[]{:S(2)}) collective-permute-start(bf16[320,640]{1,0:T(8,128)(2,1)S(1)} %bitcast.1), channel_id=1, source_target_pairs={{0,96},{16,112},{32,0},{48,16},{64,32},{80,48},{96,64},{112,80},{1... | collective-permute-start | bytes 1228808 | tf_op jit(solution)/shard_map/ppermute | solution.py:173
  22.9 4.6 %collective-permute-start.1 = (bf16[320,640]{1,0:T(8,128)(2,1)S(1)}, bf16[320,640]{1,0:T(8,128)(2,1)S(1)}, u32[]{:S(2)}, u32[]{:S(2)}) collective-permute-start(bf16[320,640]{1,0:T(8,128)(2,1)S(1)} %bitcast.2), channel_id=1, source_target_pairs={{0,64},{16,80},{32,96},{48,112},{64,0},{80,16},{96,32},{112,48},{1... | collective-permute-start | bytes 1228808 | tf_op jit(solution)/shard_map/ppermute | solution.py:173
  27.5 1.9 %collective-permute-start = (bf16[320,640]{1,0:T(8,128)(2,1)S(1)}, bf16[320,640]{1,0:T(8,128)(2,1)S(1)}, u32[]{:S(2)}, u32[]{:S(2)}) collective-permute-start(bf16[320,640]{1,0:T(8,128)(2,1)S(1)} %bitcast.3), channel_id=1, source_target_pairs={{0,32},{16,48},{32,64},{48,80},{64,96},{80,112},{96,0},{112,16},{1... | collective-permute-start | bytes 1228808 | tf_op jit(solution)/shard_map/ppermute | solution.py:173
  29.4 12.0 %all-to-all-done.rows_ref = bf16[64,40,128]{2,1,0:T(8,128)(2,1)S(1)} async-done(((bf16[64,40,128]{2,1,0:T(8,128)(2,1)}), bf16[64,40,128]{2,1,0:T(8,128)(2,1)S(1)}, u32[]{:S(2)}, u32[]{:S(2)}) %all-to-all-start) | async-done | bytes 655392 | tf_op jit(solution)/shard_map/all_to_all | solution.py:197
  41.5 0.0 copy-done.7
  41.5 3.1 %attend.1 = bf16[32,40,128]{2,1,0:T(8,128)(2,1)} custom-call(s32[4]{0:T(128)S(1)} %copy-done.7, bf16[64,40,128]{2,1,0:T(8,128)(2,1)S(1)} %all-to-all-done.rows_ref), custom_call_target="tpu_custom_call" | custom-call | tf_op jit(solution)/shard_map/attend/pallas_call | solution.py:198
  44.6 0.0 collective-permute-done.2.refs_6_
  44.6 0.0 collective-permute-done.1.refs_4_
  44.6 0.8 collective-permute-done.refs_2_
  45.4 7.8 %all-to-all-start.1 = ((bf16[32,40,128]{2,1,0:T(8,128)(2,1)}), bf16[32,40,128]{2,1,0:T(8,128)(2,1)S(1)}, u32[]{:S(2)}, u32[]{:S(2)}) async-start(bf16[32,40,128]{2,1,0:T(8,128)(2,1)} %attend.1), calls=%async_computation.1 | async-start | bytes 655360 | tf_op jit(solution)/shard_map/all_to_all | solution.py:209
  53.2 2.1 %collective-permute-start.3 = (bf16[320,640]{1,0:T(8,128)(2,1)S(1)}, bf16[320,640]{1,0:T(8,128)(2,1)S(1)}, u32[]{:S(2)}, u32[]{:S(2)}) collective-permute-start(bf16[320,640]{1,0:T(8,128)(2,1)S(1)} %bitcast.4), channel_id=1, source_target_pairs={{0,16},{16,0},{32,48},{48,32},{64,80},{80,64},{96,112},{112,96},{1... | collective-permute-start | bytes 1228808 | tf_op jit(solution)/shard_map/ppermute | solution.py:177
  55.3 2.3 %collective-permute-start.4 = (bf16[320,640]{1,0:T(8,128)(2,1)S(1)}, bf16[320,640]{1,0:T(8,128)(2,1)S(1)}, u32[]{:S(2)}, u32[]{:S(2)}) collective-permute-start(bf16[320,640]{1,0:T(8,128)(2,1)S(1)} %collective-permute-done.refs_2_), channel_id=1, source_target_pairs={{0,16},{16,0},{32,48},{48,32},{64,80},{80,64},{96,112},{112,96},{1... | collective-permute-start | bytes 1228808 | tf_op jit(solution)/shard_map/ppermute | solution.py:177
  57.6 2.1 %collective-permute-start.5 = (bf16[320,640]{1,0:T(8,128)(2,1)S(1)}, bf16[320,640]{1,0:T(8,128)(2,1)S(1)}, u32[]{:S(2)}, u32[]{:S(2)}) collective-permute-start(bf16[320,640]{1,0:T(8,128)(2,1)S(1)} %collective-permute-done.1.refs_4_), channel_id=1, source_target_pairs={{0,16},{16,0},{32,48},{48,32},{64,80},{80,64},{96,112},{112,96},{1... | collective-permute-start | bytes 1228808 | tf_op jit(solution)/shard_map/ppermute | solution.py:177
  59.6 2.3 %collective-permute-start.6 = (bf16[320,640]{1,0:T(8,128)(2,1)S(1)}, bf16[320,640]{1,0:T(8,128)(2,1)S(1)}, u32[]{:S(2)}, u32[]{:S(2)}) collective-permute-start(bf16[320,640]{1,0:T(8,128)(2,1)S(1)} %collective-permute-done.2.refs_6_), channel_id=1, source_target_pairs={{0,16},{16,0},{32,48},{48,32},{64,80},{80,64},{96,112},{112,96},{1... | collective-permute-start | bytes 1228808 | tf_op jit(solution)/shard_map/ppermute | solution.py:177
  61.9 0.0 collective-permute-done.3.refs_1_
  61.9 0.0 collective-permute-done.4.refs_3_
  61.9 0.0 collective-permute-done.5.refs_5_
  61.9 1.3 %collective-permute-done.6.refs_7_ = bf16[320,640]{1,0:T(8,128)(2,1)S(1)} collective-permute-done((bf16[320,640]{1,0:T(8,128)(2,1)S(1)}, bf16[320,640]{1,0:T(8,128)(2,1)S(1)}, u32[]{:S(2)}, u32[]{:S(2)}) %collective-permute-start.6) | collective-permute-done | bytes 409632 | tf_op jit(solution)/shard_map/ppermute | solution.py:177
  63.3 0.8 copy-done.1
  64.0 0.0 all-to-all-done.1.parts_ref
  64.0 0.7 merge.1
  64.8 0.0 copy-start.3
  64.8 0.0 copy-start.8
  64.8 47.1 %all_to_all.15.rows_ref = bf16[16,32,1024]{2,1,0:T(8,128)(2,1)S(1)} all-to-all(bf16[16,32,1024]{2,1,0:T(8,128)(2,1)S(1)} %merge.1), channel_id=1, replica_groups=mesh['span'=4,'head'=8,'seq'=16] {'seq'}, dimensions={0} | all-to-all | bytes 2097152 | tf_op jit(solution)/shard_map/all_to_all | solution.py:221
  111.9 2.3 %project.1 = bf16[96,320]{1,0:T(8,128)(2,1)} custom-call(s32[4]{0:T(128)S(1)} %copy-done.8, bf16[16,32,1024]{2,1,0:T(8,128)(2,1)S(1)} %all_to_all.15.rows_ref, f32[50,320]{1,0:T(8,128)S(1)} %copy-done.3, bf16[320,640]{1,0:T(8,128)(2,1)S(1)} %bitcast.5, bf16[320,640]{1,0:T(8,128)(2,1)S(1)} %collective-permute-done.3.refs_1_, ...), custom_call_target="tpu_custom_call" | custom-call | tf_op jit(solution)/shard_map/project/pallas_call | solution.py:222
  (9 shorter events, 0.0 us)
Async XLA Ops:
  0.0 0.8 copy-start.4
  0.8 0.8 copy-start.5
  1.7 0.8 copy-start.6
  3.7 16.7 %copy-start = (bf16[640,320]{0,1:T(8,128)(2,1)S(1)}, bf16[640,320]{0,1:T(8,128)(2,1)}, u32[]{:S(2)}) copy-start(bf16[640,320]{0,1:T(8,128)(2,1)} %param.10) | copy-start | bytes 1228804
  3.7 37.8 %copy-start.7 = (s32[4]{0:T(128)S(1)}, s32[4]{0:T(128)}, u32[]{:S(2)}) copy-start(s32[4]{0:T(128)} %order_ref.1) | copy-start | bytes 52
  3.7 37.8 %all-to-all-start = ((bf16[64,40,128]{2,1,0:T(8,128)(2,1)}), bf16[64,40,128]{2,1,0:T(8,128)(2,1)S(1)}, u32[]{:S(2)}, u32[]{:S(2)}) async-start(bf16[64,40,128]{2,1,0:T(8,128)(2,1)} %pack.1), calls=%async_computation | async-start | bytes 1310720 | tf_op jit(solution)/shard_map/all_to_all | solution.py:197
  20.4 24.2 %collective-permute-start.2 = (bf16[320,640]{1,0:T(8,128)(2,1)S(1)}, bf16[320,640]{1,0:T(8,128)(2,1)S(1)}, u32[]{:S(2)}, u32[]{:S(2)}) collective-permute-start(bf16[320,640]{1,0:T(8,128)(2,1)S(1)} %bitcast.1), channel_id=1, source_target_pairs={{0,96},{16,112},{32,0},{48,16},{64,32},{80,48},{96,64},{112,80},{1... | collective-permute-start | bytes 1228808 | tf_op jit(solution)/shard_map/ppermute | solution.py:173
  22.9 21.7 %collective-permute-start.1 = (bf16[320,640]{1,0:T(8,128)(2,1)S(1)}, bf16[320,640]{1,0:T(8,128)(2,1)S(1)}, u32[]{:S(2)}, u32[]{:S(2)}) collective-permute-start(bf16[320,640]{1,0:T(8,128)(2,1)S(1)} %bitcast.2), channel_id=1, source_target_pairs={{0,64},{16,80},{32,96},{48,112},{64,0},{80,16},{96,32},{112,48},{1... | collective-permute-start | bytes 1228808 | tf_op jit(solution)/shard_map/ppermute | solution.py:173
  27.5 17.9 %collective-permute-start = (bf16[320,640]{1,0:T(8,128)(2,1)S(1)}, bf16[320,640]{1,0:T(8,128)(2,1)S(1)}, u32[]{:S(2)}, u32[]{:S(2)}) collective-permute-start(bf16[320,640]{1,0:T(8,128)(2,1)S(1)} %bitcast.3), channel_id=1, source_target_pairs={{0,32},{16,48},{32,64},{48,80},{64,96},{80,112},{96,0},{112,16},{1... | collective-permute-start | bytes 1228808 | tf_op jit(solution)/shard_map/ppermute | solution.py:173
  45.4 18.6 %all-to-all-start.1 = ((bf16[32,40,128]{2,1,0:T(8,128)(2,1)}), bf16[32,40,128]{2,1,0:T(8,128)(2,1)S(1)}, u32[]{:S(2)}, u32[]{:S(2)}) async-start(bf16[32,40,128]{2,1,0:T(8,128)(2,1)} %attend.1), calls=%async_computation.1 | async-start | bytes 655360 | tf_op jit(solution)/shard_map/all_to_all | solution.py:209
  53.2 8.7 %collective-permute-start.3 = (bf16[320,640]{1,0:T(8,128)(2,1)S(1)}, bf16[320,640]{1,0:T(8,128)(2,1)S(1)}, u32[]{:S(2)}, u32[]{:S(2)}) collective-permute-start(bf16[320,640]{1,0:T(8,128)(2,1)S(1)} %bitcast.4), channel_id=1, source_target_pairs={{0,16},{16,0},{32,48},{48,32},{64,80},{80,64},{96,112},{112,96},{1... | collective-permute-start | bytes 1228808 | tf_op jit(solution)/shard_map/ppermute | solution.py:177
  55.3 6.6 %collective-permute-start.4 = (bf16[320,640]{1,0:T(8,128)(2,1)S(1)}, bf16[320,640]{1,0:T(8,128)(2,1)S(1)}, u32[]{:S(2)}, u32[]{:S(2)}) collective-permute-start(bf16[320,640]{1,0:T(8,128)(2,1)S(1)} %collective-permute-done.refs_2_), channel_id=1, source_target_pairs={{0,16},{16,0},{32,48},{48,32},{64,80},{80,64},{96,112},{112,96},{1... | collective-permute-start | bytes 1228808 | tf_op jit(solution)/shard_map/ppermute | solution.py:177
  57.6 4.4 %collective-permute-start.5 = (bf16[320,640]{1,0:T(8,128)(2,1)S(1)}, bf16[320,640]{1,0:T(8,128)(2,1)S(1)}, u32[]{:S(2)}, u32[]{:S(2)}) collective-permute-start(bf16[320,640]{1,0:T(8,128)(2,1)S(1)} %collective-permute-done.1.refs_4_), channel_id=1, source_target_pairs={{0,16},{16,0},{32,48},{48,32},{64,80},{80,64},{96,112},{112,96},{1... | collective-permute-start | bytes 1228808 | tf_op jit(solution)/shard_map/ppermute | solution.py:177
  59.6 3.6 %collective-permute-start.6 = (bf16[320,640]{1,0:T(8,128)(2,1)S(1)}, bf16[320,640]{1,0:T(8,128)(2,1)S(1)}, u32[]{:S(2)}, u32[]{:S(2)}) collective-permute-start(bf16[320,640]{1,0:T(8,128)(2,1)S(1)} %collective-permute-done.2.refs_6_), channel_id=1, source_target_pairs={{0,16},{16,0},{32,48},{48,32},{64,80},{80,64},{96,112},{112,96},{1... | collective-permute-start | bytes 1228808 | tf_op jit(solution)/shard_map/ppermute | solution.py:177
  63.3 0.8 copy-start.1
  64.8 47.2 %copy-start.2 = (bf16[320,640]{1,0:T(8,128)(2,1)S(1)}, bf16[320,640]{1,0:T(8,128)(2,1)}, u32[]{:S(2)}) copy-start(bf16[320,640]{1,0:T(8,128)(2,1)} %copy-done.1) | copy-start | bytes 1228804
  64.8 47.2 %copy-start.3 = (f32[50,320]{1,0:T(8,128)S(1)}, f32[50,320]{1,0:T(8,128)}, u32[]{:S(2)}) copy-start(f32[50,320]{1,0:T(8,128)} %gate_ref.1) | copy-start | bytes 192004
  64.8 47.2 %copy-start.8 = (s32[4]{0:T(128)S(1)}, s32[4]{0:T(128)}, u32[]{:S(2)}) copy-start(s32[4]{0:T(128)} %level_ref.1) | copy-start | bytes 52

commit v4 on v3

--- a/solution.py
+++ b/solution.py
@@ -22,6 +22,8 @@
 QBLOCK = PLACES * QROWS
 PIECE = QBLOCK // GROUPS
 STATS = 8
+HEAD = ("ring", "core")
+SEQ = ("far", "side", "part")
 EXP2_SCALE = math.log2(math.e) / math.sqrt(HEAD_DIM)
 VMEM = pl.BlockSpec(memory_space=pltpu.VMEM)
 HBM = pl.BlockSpec(memory_space=pltpu.HBM)
@@ -112,12 +114,11 @@
 
 
 def merge_kernel(parts_ref, out_ref, turn_ref):
-    me = lax.axis_index("head")
-    ring, core = me // CORES, lax.rem(me, CORES)
+    ring, core = lax.axis_index("ring"), lax.axis_index("core")
     slots = []
     for step in range(RING):
-        there = lax.rem(ring + RING - step, RING) * CORES
-        slots += [there + core, there + (CORES - 1 - core)]
+        there = lax.rem(ring + step, RING) * CORES
+        slots += [there + c for c in range(CORES)]
     rows = []
     for s in range(SPANS):
         for group in slots:
@@ -125,7 +126,7 @@
             rows.append(stats[0:1] + stats[1:2] + stats[2:3])
     pad = jnp.zeros((HEAD_DIM - SPANS * GROUPS, HEAD_DIM), jnp.float32)
     turn_ref[...] = jnp.transpose(jnp.concatenate(rows + [pad], axis=0))
-    begin = lax.rem(me, HEAD_DIM // PIECE) * PIECE
+    begin = lax.rem(ring * CORES + core, HEAD_DIM // PIECE) * PIECE
     mine = turn_ref[pl.ds(pl.multiple_of(begin, PIECE), PIECE), :]
     for slot, group in enumerate(slots):
         cols = [mine[:, s * GROUPS + slot : s * GROUPS + slot + 1] for s in range(SPANS)]
@@ -137,44 +138,79 @@
             part = parts_ref[s * GROUPS + group, :PIECE, :].astype(jnp.float32)
             mixed = mixed + part * (shares[s] / total)
         mixed = mixed.astype(jnp.bfloat16)
+        step, half = slot // CORES, slot % CORES
+        side = step % 2
+        lanes = slice(0, HEAD_DIM) if step in (0, 3) else slice(HEAD_DIM, 2 * HEAD_DIM)
         for place in range(PLACES):
-            out_ref[place, :, slot * HEAD_DIM : (slot + 1) * HEAD_DIM] = mixed
-
-
-def project_kernel(level_ref, rows_ref, gate_ref, *refs):
-    blocks, out_ref = refs[:GROUPS], refs[GROUPS]
-    acc = jnp.zeros((BLOCKS * PIECE, out_ref.shape[1]), jnp.float32)
-    for pair in range(RING):
-        lanes = slice(2 * pair * HEAD_DIM, 2 * (pair + 1) * HEAD_DIM)
-        for head in range(HEADS_HERE):
-            left = jnp.concatenate(
-                [rows_ref[head * BLOCKS + b, :, lanes] for b in range(BLOCKS)], axis=0
-            )
-            mine = slice(head * HEAD_DIM, (head + 1) * HEAD_DIM)
-            right = jnp.concatenate(
-                [blocks[2 * pair][:, mine], blocks[2 * pair + 1][:, mine]], axis=1
-            )
-            acc = acc + lax.dot_general(
-                left, right, (((1,), (1,)), ((), ())), preferred_element_type=jnp.float32
-            )
+            if side_of(place) == side:
+                out_ref[half * PLACES + place, :, lanes] = mixed
+
+
+def project_kernel(rows_ref, mine_a, mine_b, theirs_a, theirs_b, out_ref):
+    side = lax.axis_index("side")
+    width = out_ref.shape[2]
+    acc = jnp.zeros((CORES * BLOCKS * PIECE, 2 * width), jnp.float32)
+    for head in range(HEADS_HERE):
+        left = jnp.concatenate(
+            [
+                rows_ref[c * PLACES + head * BLOCKS + b]
+                for c in range(CORES)
+                for b in range(BLOCKS)
+            ],
+            axis=0,
+        )
+        cols = slice(head * HEAD_DIM, (head + 1) * HEAD_DIM)
+        right = jnp.concatenate(
+            [
+                jnp.concatenate([first[:, cols], second[:, cols]], axis=1)
+                for first, second in ((mine_a, mine_b), (theirs_a, theirs_b))
+            ],
+            axis=0,
+        )
+        acc = acc + lax.dot_general(
+            left, right, (((1,), (1,)), ((), ())), preferred_element_type=jnp.float32
+        )
+    acc = acc.astype(jnp.bfloat16)
+    for core in range(CORES):
+        for block in range(BLOCKS):
+            for half in range(2):
+                source = (core * BLOCKS + block) * PIECE + half * QROWS
+                target = half * ROWS + block * QROWS
+                part = acc[source : source + QROWS]
+                out_ref[core * 2 + side, target : target + QROWS, :] = part[:, :width]
+                out_ref[core * 2 + 1 - side, target : target + QROWS, :] = part[:, width:]
+
+
+def finish_kernel(level_ref, parts_ref, gate_ref, out_ref):
     level = level_ref[lax.axis_index("span")]
-    gated = (acc * gate_ref[pl.ds(level, 1), :]).astype(jnp.bfloat16)
-    for block in range(BLOCKS):
-        for side in range(2):
-            source = block * PIECE + side * QROWS
-            target = side * ROWS + block * QROWS
-            out_ref[target : target + QROWS, :] = gated[source : source + QROWS]
-
-
-def along_ring(x, step):
+    total = parts_ref[0].astype(jnp.float32)
+    for i in range(1, parts_ref.shape[0]):
+        total = total + parts_ref[i].astype(jnp.float32)
+    out_ref[...] = (total * gate_ref[pl.ds(level, 1), :]).astype(jnp.bfloat16)
+
+
+def side_of(place):
+    return place // 2 % 2
+
+
+def near_weights(x):
     moves = [
-        (r * CORES + c, (r + step) % RING * CORES + c) for r in range(RING) for c in range(CORES)
+        ((r * 4 + z) * 2 + i, ((r + i) % RING * 4 + z) * 2 + i)
+        for r in range(RING)
+        for z in range(4)
+        for i in range(2)
     ]
-    return lax.ppermute(x, "head", moves)
-
-
-def across_cores(x):
-    return lax.ppermute(x, "head", [(g, g ^ 1) for g in range(GROUPS)])
+    return lax.ppermute(x, ("ring", "far", "side"), moves)
+
+
+def far_weights(x):
+    moves = [
+        ((r * 4 + z) * 2 + i, ((r + RING - 2 + i) % RING * 4 + z) * 2 + i)
+        for r in range(RING)
+        for z in range(4)
+        for i in range(2)
+    ]
+    return lax.ppermute(x, ("ring", "far", "side"), moves)
 
 
 def shards(queries, keys, values, out_weight, gate_table, noise_level, span_order):
@@ -189,12 +225,13 @@
             pltpu.VMEM((SPANS, 2 * KROWS, shard[1]), jnp.float32),
             pltpu.SemaphoreType.DMA((3,)),
         ],
-        compiler_params=params(),
+        compiler_params=params(60),
         name="pack",
     )(queries, keys, values)
     packed, weight = lax.optimization_barrier((packed, out_weight.T))
-    weights = [weight] + [along_ring(weight, step) for step in range(1, RING)]
-    rows = lax.all_to_all(packed, ("span", "seq"), 0, 0, tiled=True)
+    swapped = lax.ppermute(weight, "side", [(0, 1), (1, 0)])
+    mine = near_weights(weight), far_weights(weight)
+    rows = lax.all_to_all(packed, ("span",) + SEQ, 0, 0, tiled=True)
     parts = pl.pallas_call(
         attend_kernel,
         out_shape=jax.ShapeDtypeStruct((SPANS * GROUPS, PIECE + STATS, HEAD_DIM), jnp.bfloat16),
@@ -204,44 +241,58 @@
         compiler_params=params(),
         name="attend",
     )(span_order, rows)
-    parts, weights = lax.optimization_barrier((parts, weights))
-    others = [across_cores(w) for w in weights]
-    parts = lax.all_to_all(parts, ("span", "head"), 0, 0, tiled=True)
-    parts, others = lax.optimization_barrier((parts, others))
-    blocks = [w for pair in zip(weights, others) for w in pair]
+    parts, mine, swapped = lax.optimization_barrier((parts, mine, swapped))
+    near = near_weights(swapped)
+    parts = lax.all_to_all(parts, ("span",) + HEAD, 0, 0, tiled=True)
     merged = pl.pallas_call(
         merge_kernel,
-        out_shape=jax.ShapeDtypeStruct((PLACES, PIECE, GROUPS * HEAD_DIM), jnp.bfloat16),
+        out_shape=jax.ShapeDtypeStruct((CORES * PLACES, PIECE, 2 * HEAD_DIM), jnp.bfloat16),
         in_specs=[VMEM],
         out_specs=VMEM,
         scratch_shapes=[pltpu.VMEM((HEAD_DIM, HEAD_DIM), jnp.float32)],
         compiler_params=params(),
         name="merge",
     )(parts)
-    merged = lax.all_to_all(merged, "seq", 0, 0, tiled=True)
+    merged, near, swapped = lax.optimization_barrier((merged, near, swapped))
+    theirs = near, far_weights(swapped)
+    merged = lax.all_to_all(merged, ("core",) + SEQ, 0, 0, tiled=True)
+    shape = (BLOCKS * PIECE, out_weight.shape[1])
+    sums = pl.pallas_call(
+        project_kernel,
+        out_shape=jax.ShapeDtypeStruct((2 * CORES,) + shape, jnp.bfloat16),
+        in_specs=[VMEM] * 5,
+        out_specs=VMEM,
+        compiler_params=params(),
+        name="project",
+    )(merged, *mine, *theirs)
+    sums = lax.all_to_all(sums, ("core", "side"), 0, 0, tiled=True)
     return pl.pallas_call(
-        project_kernel,
-        out_shape=jax.ShapeDtypeStruct((BLOCKS * PIECE, out_weight.shape[1]), jnp.bfloat16),
-        in_specs=[SMEM] + [VMEM] * (2 + GROUPS),
-        out_specs=VMEM,
-        compiler_params=params(),
-        name="project",
-    )(noise_level, merged, gate_table, *blocks)
+        finish_kernel,
+        out_shape=jax.ShapeDtypeStruct(shape, jnp.bfloat16),
+        in_specs=[SMEM, VMEM, VMEM],
+        out_specs=VMEM,
+        compiler_params=params(),
+        name="finish",
+    )(noise_level, sums, gate_table)
 
 
 def solution(mesh):
+    fine = jax.sharding.Mesh(
+        mesh.devices.reshape(SPANS, RING, CORES, 4, 2, 2),
+        ("span", "ring", "core", "far", "side", "part"),
+    )
     return jax.shard_map(
         shards,
-        mesh=mesh,
+        mesh=fine,
         in_specs=(
-            P(("span", "seq"), "head"),
-            P(("span", "seq"), "head"),
-            P(("span", "seq"), "head"),
-            P("head", "seq"),
-            P(None, "seq"),
+            P(("span",) + SEQ, HEAD),
+            P(("span",) + SEQ, HEAD),
+            P(("span",) + SEQ, HEAD),
+            P(HEAD, SEQ),
+            P(None, SEQ),
             P(),
             P(),
         ),
-        out_specs=P(("span", "head"), "seq"),
+        out_specs=P(("span",) + HEAD, SEQ),
         check_vma=False,
     )

time: 115 us -> 110 us (0.957)
  the two profiles are of different devices: /device:TPU:20 before, /device:TPU:8 now
where the time goes in v4:
time: 110 us; the launch traced here: 109 us
  starting transfers between devices  48.6 us (44%)
  waiting for transfers between devices  43.4 us (39%)
  blocking collectives  8.88 us (8%)
  Pallas kernels  8.35 us (8%)
    all_to_all x1, starting transfers between devices, shards(): rows = lax.all_to_all(packed, ('span',) + SEQ, 0, 0, tiled=True)  16.7 us
    all_to_all x1, waiting for transfers between devices, shards(): rows = lax.all_to_all(packed, ('span',) + SEQ, 0, 0, tiled=True)  13.2 us
    all_to_all x1, starting transfers between devices, shards(): merged = lax.all_to_all(merged, ('core',) + SEQ, 0, 0, tiled=True)  12 us
    ppermute x2, waiting for transfers between devices, far_weights(): return lax.ppermute(x, ('ring', 'far', 'side'), moves)  12 us
    all_to_all x1, waiting for transfers between devices, shards(): parts = lax.all_to_all(parts, ('span',) + HEAD, 0, 0, tiled=True)  10.7 us
    all_to_all x1, blocking collectives, shards(): sums = lax.all_to_all(sums, ('core', 'side'), 0, 0, tiled=True)  8.88 us
    ppermute x2, starting transfers between devices, far_weights(): return lax.ppermute(x, ('ring', 'far', 'side'), moves)  8 us
    all_to_all x1, waiting for transfers between devices, shards(): merged = lax.all_to_all(merged, ('core',) + SEQ, 0, 0, tiled=True)  7.48 us
  transfers between devices with their start and end apart: 8, of which 4 were waited for; matrix products, arithmetic and copies ran while one was open for 0% of the time, Pallas kernels for 4%

profile of v4, /device:TPU:8, one launch (start us, length us, event | category | flops | bytes accessed | tf_op | source)
XLA Modules:
  0.0 109.4 jit_solution(14403795912822035282)
XLA Ops:
  0.0 1.8 %pack.1 = bf16[64,40,128]{2,1,0:T(8,128)(2,1)} custom-call(bf16[48,640]{1,0:T(8,128)(2,1)} %q_hbm.1, bf16[48,640]{1,0:T(8,128)(2,1)} %k_hbm.1, bf16[48,640]{1,0:T(8,128)(2,1)} %v_hbm.1), custom_call_target="tpu_custom_call" | custom-call | tf_op jit(solution)/shard_map/pack/pallas_call | solution.py:218
  1.8 0.0 copy-start.3
  1.8 0.0 copy-start.1
  1.8 16.7 %all-to-all-start = ((bf16[64,40,128]{2,1,0:T(8,128)(2,1)}), bf16[64,40,128]{2,1,0:T(8,128)(2,1)S(1)}, u32[]{:S(2)}, u32[]{:S(2)}) async-start(bf16[64,40,128]{2,1,0:T(8,128)(2,1)} %pack.1), calls=%async_computation | async-start | bytes 1310720 | tf_op jit(solution)/shard_map/all_to_all | solution.py:234
  18.6 0.0 copy-done.3
  18.6 3.4 %collective-permute-start.2 = (bf16[320,640]{1,0:T(8,128)(2,1)S(1)}, bf16[320,640]{1,0:T(8,128)(2,1)S(1)}, u32[]{:S(2)}, u32[]{:S(2)}) collective-permute-start(bf16[320,640]{1,0:T(8,128)(2,1)S(1)} %bitcast.1), channel_id=1, source_target_pairs={{0,2},{2,0},{1,3},{3,1},{4,6},{6,4},{5,7},{7,5},{8,10},{10,8},{9,1... | collective-permute-start | bytes 1228808 | tf_op jit(solution)/shard_map/ppermute | solution.py:232
  22.0 4.9 %collective-permute-start.1 = (bf16[320,640]{1,0:T(8,128)(2,1)S(1)}, bf16[320,640]{1,0:T(8,128)(2,1)S(1)}, u32[]{:S(2)}, u32[]{:S(2)}) collective-permute-start(bf16[320,640]{1,0:T(8,128)(2,1)S(1)} %bitcast.2), channel_id=1, source_target_pairs={{0,64},{2,98},{4,68},{6,102},{8,72},{10,106},{12,76},{14,110},{32,... | collective-permute-start | bytes 1228808 | tf_op jit(solution)/shard_map/ppermute | solution.py:213
  26.9 0.7 collective-permute-start
  27.6 13.2 %all-to-all-done.rows_ref = bf16[64,40,128]{2,1,0:T(8,128)(2,1)S(1)} async-done(((bf16[64,40,128]{2,1,0:T(8,128)(2,1)}), bf16[64,40,128]{2,1,0:T(8,128)(2,1)S(1)}, u32[]{:S(2)}, u32[]{:S(2)}) %all-to-all-start) | async-done | bytes 655392 | tf_op jit(solution)/shard_map/all_to_all | solution.py:234
  40.8 0.0 copy-done.1
  40.8 3.1 %attend.1 = bf16[32,40,128]{2,1,0:T(8,128)(2,1)} custom-call(s32[4]{0:T(128)S(1)} %copy-done.1, bf16[64,40,128]{2,1,0:T(8,128)(2,1)S(1)} %all-to-all-done.rows_ref), custom_call_target="tpu_custom_call" | custom-call | tf_op jit(solution)/shard_map/attend/pallas_call | solution.py:235
  44.0 0.0 collective-permute-done.2
  44.0 0.0 collective-permute-done.1.mine_b
  44.0 0.0 collective-permute-done.mine_a
  44.0 7.1 %all-to-all-start.1 = ((bf16[32,40,128]{2,1,0:T(8,128)(2,1)}), bf16[32,40,128]{2,1,0:T(8,128)(2,1)S(1)}, u32[]{:S(2)}, u32[]{:S(2)}) async-start(bf16[32,40,128]{2,1,0:T(8,128)(2,1)} %attend.1), calls=%async_computation.1 | async-start | bytes 655360 | tf_op jit(solution)/shard_map/all_to_all | solution.py:246
  51.1 0.7 collective-permute-start.3
  51.8 10.7 %all-to-all-done.1.parts_ref = bf16[32,40,128]{2,1,0:T(8,128)(2,1)S(1)} async-done(((bf16[32,40,128]{2,1,0:T(8,128)(2,1)}), bf16[32,40,128]{2,1,0:T(8,128)(2,1)S(1)}, u32[]{:S(2)}, u32[]{:S(2)}) %all-to-all-start.1) | async-done | bytes 327712 | tf_op jit(solution)/shard_map/all_to_all | solution.py:246
  62.5 1.5 %merge.1 = bf16[32,32,256]{2,1,0:T(8,128)(2,1)} custom-call(bf16[32,40,128]{2,1,0:T(8,128)(2,1)S(1)} %all-to-all-done.1.parts_ref), custom_call_target="tpu_custom_call" | custom-call | tf_op jit(solution)/shard_map/merge/pallas_call | solution.py:247
  64.0 0.0 collective-permute-done.3.theirs_a
  64.0 12.0 %all-to-all-start.2 = ((bf16[32,32,256]{2,1,0:T(8,128)(2,1)}), bf16[32,32,256]{2,1,0:T(8,128)(2,1)S(1)}, u32[]{:S(2)}, u32[]{:S(2)}) async-start(bf16[32,32,256]{2,1,0:T(8,128)(2,1)} %merge.1), calls=%async_computation.2 | async-start | bytes 1048576 | tf_op jit(solution)/shard_map/all_to_all | solution.py:258
  76.0 3.1 %collective-permute-start.4 = (bf16[320,640]{1,0:T(8,128)(2,1)S(1)}, bf16[320,640]{1,0:T(8,128)(2,1)S(1)}, u32[]{:S(2)}, u32[]{:S(2)}) collective-permute-start(bf16[320,640]{1,0:T(8,128)(2,1)S(1)} %collective-permute-done.2), channel_id=1, source_target_pairs={{0,64},{2,98},{4,68},{6,102},{8,72},{10,106},{12,76},{14,110},{32,... | collective-permute-start | bytes 1228808 | tf_op jit(solution)/shard_map/ppermute | solution.py:213
  79.0 12.0 %collective-permute-done.4.theirs_b = bf16[320,640]{1,0:T(8,128)(2,1)S(1)} collective-permute-done((bf16[320,640]{1,0:T(8,128)(2,1)S(1)}, bf16[320,640]{1,0:T(8,128)(2,1)S(1)}, u32[]{:S(2)}, u32[]{:S(2)}) %collective-permute-start.4) | collective-permute-done | bytes 409632 | tf_op jit(solution)/shard_map/ppermute | solution.py:213
  91.0 7.5 %all-to-all-done.2.rows_ref = bf16[32,32,256]{2,1,0:T(8,128)(2,1)S(1)} async-done(((bf16[32,32,256]{2,1,0:T(8,128)(2,1)}), bf16[32,32,256]{2,1,0:T(8,128)(2,1)S(1)}, u32[]{:S(2)}, u32[]{:S(2)}) %all-to-all-start.2) | async-done | bytes 524320 | tf_op jit(solution)/shard_map/all_to_all | solution.py:258
  98.5 0.7 project.1
  99.2 0.0 copy-start
  99.3 0.0 copy-start.2
  99.3 8.9 %all_to_all.20.parts_ref = bf16[4,96,320]{2,1,0:T(8,128)(2,1)S(1)} all-to-all(bf16[4,96,320]{2,1,0:T(8,128)(2,1)S(1)} %project.1), channel_id=1, replica_groups=mesh['span'=4,'ring'=4,'core'=2,'far'=4,'side'=2,'part'=2] {'core','side'}, dimensions={0} | all-to-all | bytes 491520 | tf_op jit(solution)/shard_map/all_to_all | solution.py:268
  108.1 0.0 copy-done
  108.1 0.0 copy-done.2
  108.1 1.2 %finish.1 = bf16[96,320]{1,0:T(8,128)(2,1)} custom-call(s32[4]{0:T(128)S(1)} %copy-done.2, bf16[4,96,320]{2,1,0:T(8,128)(2,1)S(1)} %all_to_all.20.parts_ref, f32[50,320]{1,0:T(8,128)S(1)} %copy-done), custom_call_target="tpu_custom_call" | custom-call | tf_op jit(solution)/shard_map/finish/pallas_call | solution.py:269
Async XLA Ops:
  1.8 16.8 %copy-start.3 = (bf16[640,320]{0,1:T(8,128)(2,1)S(1)}, bf16[640,320]{0,1:T(8,128)(2,1)}, u32[]{:S(2)}) copy-start(bf16[640,320]{0,1:T(8,128)(2,1)} %param.10) | copy-start | bytes 1228804
  1.8 39.0 %copy-start.1 = (s32[4]{0:T(128)S(1)}, s32[4]{0:T(128)}, u32[]{:S(2)}) copy-start(s32[4]{0:T(128)} %order_ref.1) | copy-start | bytes 52
  1.8 39.0 %all-to-all-start = ((bf16[64,40,128]{2,1,0:T(8,128)(2,1)}), bf16[64,40,128]{2,1,0:T(8,128)(2,1)S(1)}, u32[]{:S(2)}, u32[]{:S(2)}) async-start(bf16[64,40,128]{2,1,0:T(8,128)(2,1)} %pack.1), calls=%async_computation | async-start | bytes 1310720 | tf_op jit(solution)/shard_map/all_to_all | solution.py:234
  18.6 25.4 %collective-permute-start.2 = (bf16[320,640]{1,0:T(8,128)(2,1)S(1)}, bf16[320,640]{1,0:T(8,128)(2,1)S(1)}, u32[]{:S(2)}, u32[]{:S(2)}) collective-permute-start(bf16[320,640]{1,0:T(8,128)(2,1)S(1)} %bitcast.1), channel_id=1, source_target_pairs={{0,2},{2,0},{1,3},{3,1},{4,6},{6,4},{5,7},{7,5},{8,10},{10,8},{9,1... | collective-permute-start | bytes 1228808 | tf_op jit(solution)/shard_map/ppermute | solution.py:232
  22.0 22.0 %collective-permute-start.1 = (bf16[320,640]{1,0:T(8,128)(2,1)S(1)}, bf16[320,640]{1,0:T(8,128)(2,1)S(1)}, u32[]{:S(2)}, u32[]{:S(2)}) collective-permute-start(bf16[320,640]{1,0:T(8,128)(2,1)S(1)} %bitcast.2), channel_id=1, source_target_pairs={{0,64},{2,98},{4,68},{6,102},{8,72},{10,106},{12,76},{14,110},{32,... | collective-permute-start | bytes 1228808 | tf_op jit(solution)/shard_map/ppermute | solution.py:213
  26.9 17.1 %collective-permute-start = (bf16[320,640]{1,0:T(8,128)(2,1)S(1)}, bf16[320,640]{1,0:T(8,128)(2,1)S(1)}, u32[]{:S(2)}, u32[]{:S(2)}) collective-permute-start(bf16[320,640]{1,0:T(8,128)(2,1)S(1)} %bitcast.3), channel_id=1, source_target_pairs={{0,0},{2,34},{4,4},{6,38},{8,8},{10,42},{12,12},{14,46},{32,32},{3... | collective-permute-start | bytes 1228808 | tf_op jit(solution)/shard_map/ppermute | solution.py:203
  44.0 18.5 %all-to-all-start.1 = ((bf16[32,40,128]{2,1,0:T(8,128)(2,1)}), bf16[32,40,128]{2,1,0:T(8,128)(2,1)S(1)}, u32[]{:S(2)}, u32[]{:S(2)}) async-start(bf16[32,40,128]{2,1,0:T(8,128)(2,1)} %attend.1), calls=%async_computation.1 | async-start | bytes 655360 | tf_op jit(solution)/shard_map/all_to_all | solution.py:246
  51.1 12.9 %collective-permute-start.3 = (bf16[320,640]{1,0:T(8,128)(2,1)S(1)}, bf16[320,640]{1,0:T(8,128)(2,1)S(1)}, u32[]{:S(2)}, u32[]{:S(2)}) collective-permute-start(bf16[320,640]{1,0:T(8,128)(2,1)S(1)} %collective-permute-done.2), channel_id=1, source_target_pairs={{0,0},{2,34},{4,4},{6,38},{8,8},{10,42},{12,12},{14,46},{32,32},{3... | collective-permute-start | bytes 1228808 | tf_op jit(solution)/shard_map/ppermute | solution.py:203
  64.0 34.5 %all-to-all-start.2 = ((bf16[32,32,256]{2,1,0:T(8,128)(2,1)}), bf16[32,32,256]{2,1,0:T(8,128)(2,1)S(1)}, u32[]{:S(2)}, u32[]{:S(2)}) async-start(bf16[32,32,256]{2,1,0:T(8,128)(2,1)} %merge.1), calls=%async_computation.2 | async-start | bytes 1048576 | tf_op jit(solution)/shard_map/all_to_all | solution.py:258
  76.0 15.1 %collective-permute-start.4 = (bf16[320,640]{1,0:T(8,128)(2,1)S(1)}, bf16[320,640]{1,0:T(8,128)(2,1)S(1)}, u32[]{:S(2)}, u32[]{:S(2)}) collective-permute-start(bf16[320,640]{1,0:T(8,128)(2,1)S(1)} %collective-permute-done.2), channel_id=1, source_target_pairs={{0,64},{2,98},{4,68},{6,102},{8,72},{10,106},{12,76},{14,110},{32,... | collective-permute-start | bytes 1228808 | tf_op jit(solution)/shard_map/ppermute | solution.py:213
  99.2 8.9 %copy-start = (f32[50,320]{1,0:T(8,128)S(1)}, f32[50,320]{1,0:T(8,128)}, u32[]{:S(2)}) copy-start(f32[50,320]{1,0:T(8,128)} %gate_ref.1) | copy-start | bytes 192004
  99.3 8.9 %copy-start.2 = (s32[4]{0:T(128)S(1)}, s32[4]{0:T(128)}, u32[]{:S(2)}) copy-start(s32[4]{0:T(128)} %level_ref.1) | copy-start | bytes 52

commit v5 on v4

v5 whole, which is shorter than its diff:
```python
import functools
import math

import jax
import jax.numpy as jnp
from jax import lax
from jax.experimental import pallas as pl
from jax.experimental.pallas import tpu as pltpu
from jax.sharding import PartitionSpec as P

HEAD_DIM = 128
SPANS = 4
RING, CORES = 4, 2
GROUPS = 8
HEADS_HERE = 5
BLOCKS = 3
PLACES = 16
ROWS = 48
QROWS = ROWS // BLOCKS
KROWS = ROWS // SPANS
KBLOCK = PLACES * KROWS
QBLOCK = PLACES * QROWS
CHUNK = 2 * QROWS
CUT = 192
STATS = 8
HEAD = ("ring", "core")
SEQ = ("far", "side", "part")
EXP2_SCALE = math.log2(math.e) / math.sqrt(HEAD_DIM)
VMEM = pl.BlockSpec(memory_space=pltpu.VMEM)
HBM = pl.BlockSpec(memory_space=pltpu.HBM)
SMEM = pl.BlockSpec(memory_space=pltpu.SMEM)


def params(mib=24):
    return pltpu.CompilerParams(vmem_limit_bytes=mib * 2**20)


def pack_kernel(q_hbm, k_hbm, v_hbm, out_ref, q_ref, k_ref, v_ref, kv_ref, sems):
    copies = [
        pltpu.make_async_copy(source, target, sems.at[i])
        for i, (source, target) in enumerate(((q_hbm, q_ref), (k_hbm, k_ref), (v_hbm, v_ref)))
    ]
    for copy in copies:
        copy.start()
    for span in range(SPANS):
        for place in range(HEADS_HERE * BLOCKS, PLACES):
            out_ref[span * PLACES + place] = jnp.zeros(out_ref.shape[1:], out_ref.dtype)
    copies[0].wait()
    for head in range(HEADS_HERE):
        cols = slice(head * HEAD_DIM, (head + 1) * HEAD_DIM)
        for block in range(BLOCKS):
            part = q_ref[block * QROWS : (block + 1) * QROWS, cols]
            for span in range(SPANS):
                out_ref[span * PLACES + head * BLOCKS + block, :QROWS, :] = part
    copies[1].wait()
    copies[2].wait()
    key_rows = k_ref[...].astype(jnp.float32)
    value_rows = v_ref[...].astype(jnp.float32)
    for span in range(SPANS):
        kv_ref[span, :KROWS, :] = key_rows[span * KROWS : (span + 1) * KROWS]
        kv_ref[span, KROWS:, :] = value_rows[span * KROWS : (span + 1) * KROWS]
    for span in range(SPANS):
        both = kv_ref[span].astype(jnp.bfloat16)
        for head in range(HEADS_HERE):
            part = both[:, head * HEAD_DIM : (head + 1) * HEAD_DIM]
            for block in range(BLOCKS):
                out_ref[span * PLACES + head * BLOCKS + block, QROWS:, :] = part


def split_three(x):
    high = x.astype(jnp.bfloat16)
    rest = x - high.astype(jnp.float32)
    middle = rest.astype(jnp.bfloat16)
    low = (rest - middle.astype(jnp.float32)).astype(jnp.bfloat16)
    return high, middle, low


def attend_kernel(order_ref, rows_ref, out_ref, keys_ref, values_ref):
    which = lax.broadcasted_iota(jnp.int32, (STATS, HEAD_DIM), 0)
    for turn in range(SPANS):
        span = jnp.int32(0)
        for other in range(1, SPANS):
            span = span + jnp.where(order_ref[other] == turn, other, 0)
        first = span * PLACES
        for place in range(PLACES):
            both = rows_ref[first + place, QROWS:, :].astype(jnp.float32)
            target = turn * KBLOCK + place * KROWS
            keys_ref[target : target + KROWS, :] = both[:KROWS]
            values_ref[target : target + KROWS, :] = both[KROWS:]
        seen = (turn + 1) * KBLOCK
        keys = keys_ref[:seen, :].astype(jnp.bfloat16)
        values = values_ref[:seen, :].astype(jnp.bfloat16)
        own = rows_ref[pl.ds(first, PLACES), :QROWS, :].reshape(QBLOCK, HEAD_DIM)
        scores = lax.dot_general(
            own, keys, (((1,), (1,)), ((), ())), preferred_element_type=jnp.float32
        )
        scores = scores * EXP2_SCALE
        highest = jnp.max(scores, axis=1, keepdims=True)
        weights = jnp.exp2(scores - highest)
        total = jnp.sum(weights, axis=1, keepdims=True)
        mixed = jnp.dot(weights.astype(jnp.bfloat16), values, preferred_element_type=jnp.float32)
        mixed = (mixed / total).astype(jnp.bfloat16)
        logsum = highest + jnp.log2(total)
        wide = jnp.transpose(jnp.broadcast_to(logsum, (QBLOCK, HEAD_DIM)))
        terms = [t.astype(jnp.float32) for t in split_three(wide[:STATS])]
        stat = jnp.zeros((STATS, HEAD_DIM), jnp.float32)
        for half in range(2):
            lanes = slice(half * HEAD_DIM, (half + 1) * HEAD_DIM)
            for i, term in enumerate(terms):
                stat = jnp.where(which == 3 * half + i, term[:, lanes], stat)
        for core in range(CORES):
            piece = span * CORES + core
            for ring in range(RING):
                source = (ring * CORES + core) * CHUNK
                out_ref[piece, ring * CHUNK : (ring + 1) * CHUNK, :] = mixed[source : source + CHUNK]
            out_ref[piece, RING * CHUNK :, :] = stat.astype(jnp.bfloat16)


def merge_kernel(parts_ref, out_ref, turn_ref):
    core = lax.axis_index("core")
    slots = (core, CORES - 1 - core)
    rows = []
    for half in range(2):
        for slot in slots:
            for s in range(SPANS):
                stats = parts_ref[s * CORES + slot, RING * CHUNK :, :].astype(jnp.float32)
                first = 3 * half
                rows.append(stats[first : first + 1] + stats[first + 1 : first + 2] + stats[first + 2 : first + 3])
    pad = jnp.zeros((HEAD_DIM - len(rows), HEAD_DIM), jnp.float32)
    turn_ref[...] = jnp.transpose(jnp.concatenate(rows + [pad], axis=0))
    for ring in range(RING):
        half, inner = divmod(ring, HEAD_DIM // (CORES * CHUNK))
        begin = pl.multiple_of((inner * CORES + core) * CHUNK, CHUNK)
        mine = turn_ref[pl.ds(begin, CHUNK), :]
        for i, slot in enumerate(slots):
            first = (half * CORES + i) * SPANS
            cols = [mine[:, first + s : first + s + 1] for s in range(SPANS)]
            highest = functools.reduce(jnp.maximum, cols)
            shares = [jnp.exp2(c - highest) for c in cols]
            total = functools.reduce(jnp.add, shares)
            mixed = jnp.zeros((CHUNK, HEAD_DIM), jnp.float32)
            for s in range(SPANS):
                part = parts_ref[s * CORES + slot, ring * CHUNK : (ring + 1) * CHUNK, :]
                mixed = mixed + part.astype(jnp.float32) * (shares[s] / total)
            mixed = mixed.astype(jnp.bfloat16)
            lanes = slice(i * HEAD_DIM, (i + 1) * HEAD_DIM)
            for place in range(PLACES):
                side = side_of(place)
                out_ref[place, ring * QROWS : (ring + 1) * QROWS, lanes] = mixed[
                    side * QROWS : (side + 1) * QROWS
                ]


def project_kernel(rows_ref, own_ref, other_ref, *refs):
    swaps, out_ref = refs[:4], refs[4]
    side = lax.axis_index("side")
    left = [
        jnp.concatenate(
            [
                jnp.concatenate(
                    [rows_ref[head * BLOCKS + b, :, lanes] for b in range(BLOCKS)], axis=0
                )
                for head in range(HEADS_HERE)
            ],
            axis=1,
        )
        for lanes in (slice(0, HEAD_DIM), slice(HEAD_DIM, 2 * HEAD_DIM))
    ]
    own, other = (jnp.concatenate([a[...], b[...]], axis=0) for a, b in (swaps[:2], swaps[2:]))
    for weights, target in (((own_ref[...], other_ref[...]), side), ((own, other), 1 - side)):
        sums = [
            lax.dot_general(x, w, (((1,), (1,)), ((), ())), preferred_element_type=jnp.float32)
            for x, w in zip(left, weights)
        ]
        total = (sums[0] + sums[1]).astype(jnp.bfloat16)
        for ring in range(RING):
            for block in range(BLOCKS):
                source = (block * RING + ring) * QROWS
                out_ref[ring * 2 + target, block * QROWS : (block + 1) * QROWS, :] = total[
                    source : source + QROWS
                ]


def finish_kernel(level_ref, parts_ref, gate_ref, out_ref):
    level = level_ref[lax.axis_index("span")]
    gate = gate_ref[pl.ds(level, 1), :]
    for side in range(2):
        total = parts_ref[side].astype(jnp.float32)
        for ring in range(1, RING):
            total = total + parts_ref[ring * 2 + side].astype(jnp.float32)
        out_ref[side * ROWS : (side + 1) * ROWS, :] = (total * gate).astype(jnp.bfloat16)


def side_of(place):
    return place // 2 % 2


def swap_sides(x):
    return lax.ppermute(x, "side", [(0, 1), (1, 0)])


def swap_cores(x):
    return lax.ppermute(x, "core", [(0, 1), (1, 0)])


def shards(queries, keys, values, out_weight, gate_table, noise_level, span_order):
    shard = (ROWS, HEADS_HERE * HEAD_DIM)
    packed = pl.pallas_call(
        pack_kernel,
        out_shape=jax.ShapeDtypeStruct((SPANS * PLACES, QROWS + 2 * KROWS, HEAD_DIM), jnp.bfloat16),
        in_specs=[HBM] * 3,
        out_specs=VMEM,
        scratch_shapes=[pltpu.VMEM(shard, jnp.bfloat16)] * 3
        + [
            pltpu.VMEM((SPANS, 2 * KROWS, shard[1]), jnp.float32),
            pltpu.SemaphoreType.DMA((3,)),
        ],
        compiler_params=params(60),
        name="pack",
    )(queries, keys, values)
    packed, weight = lax.optimization_barrier((packed, out_weight.T))
    other = swap_cores(weight)
    first = swap_sides(weight[:CUT])
    rows = lax.all_to_all(packed, ("span",) + SEQ, 0, 0, tiled=True)
    parts = pl.pallas_call(
        attend_kernel,
        out_shape=jax.ShapeDtypeStruct((SPANS * CORES, RING * CHUNK + STATS, HEAD_DIM), jnp.bfloat16),
        in_specs=[SMEM, VMEM],
        out_specs=VMEM,
        scratch_shapes=[pltpu.VMEM((SPANS * KBLOCK, HEAD_DIM), jnp.float32)] * 2,
        compiler_params=params(),
        name="attend",
    )(span_order, rows)
    parts, first, other = lax.optimization_barrier((parts, first, other))
    second = swap_sides(weight[CUT:])
    parts = lax.all_to_all(parts, ("span", "core"), 0, 0, tiled=True)
    parts, second = lax.optimization_barrier((parts, second))
    merged = pl.pallas_call(
        merge_kernel,
        out_shape=jax.ShapeDtypeStruct((PLACES, RING * QROWS, CORES * HEAD_DIM), jnp.bfloat16),
        in_specs=[VMEM],
        out_specs=VMEM,
        scratch_shapes=[pltpu.VMEM((HEAD_DIM, HEAD_DIM), jnp.float32)],
        compiler_params=params(),
        name="merge",
    )(parts)
    merged, first, second = lax.optimization_barrier((merged, first, second))
    first_other, second_other = swap_cores(first), swap_cores(second)
    merged = lax.all_to_all(merged, SEQ, 0, 0, tiled=True)
    sums = pl.pallas_call(
        project_kernel,
        out_shape=jax.ShapeDtypeStruct((RING * 2, ROWS, out_weight.shape[1]), jnp.bfloat16),
        in_specs=[VMEM] * 7,
        out_specs=VMEM,
        compiler_params=params(),
        name="project",
    )(merged, weight, other, first, second, first_other, second_other)
    sums = lax.all_to_all(sums, ("ring", "side"), 0, 0, tiled=True)
    return pl.pallas_call(
        finish_kernel,
        out_shape=jax.ShapeDtypeStruct((2 * ROWS, out_weight.shape[1]), jnp.bfloat16),
        in_specs=[SMEM, VMEM, VMEM],
        out_specs=VMEM,
        compiler_params=params(),
        name="finish",
    )(noise_level, sums, gate_table)


def solution(mesh):
    fine = jax.sharding.Mesh(
        mesh.devices.reshape(SPANS, RING, CORES, 4, 2, 2),
        ("span", "ring", "core", "far", "side", "part"),
    )
    return jax.shard_map(
        shards,
        mesh=fine,
        in_specs=(
            P(("span",) + SEQ, HEAD),
            P(("span",) + SEQ, HEAD),
            P(("span",) + SEQ, HEAD),
            P(HEAD, SEQ),
            P(None, SEQ),
            P(),
            P(),
        ),
        out_specs=P(("span",) + HEAD, SEQ),
        check_vma=False,
    )
```

time: 110 us -> 99.4 us (0.904)
  starting transfers between devices: 48.6 us -> 39.9 us
  waiting for transfers between devices: 43.4 us -> 37.6 us
  blocking collectives: 8.88 us -> 12.6 us
    all_to_all x2, starting transfers between devices: 19.1 us -> 9.83 us  [the longest x1 5.44 us: shards(): merged = lax.all_to_all(merged, SEQ, 0, 0, tiled=True)]
    ppermute x5, waiting for transfers between devices: 12 us -> 5.51 us  [the longest x2 4.5 us: swap_sides(): return lax.ppermute(x, 'side', [(0, 1), (1, 0)])]
    all_to_all x1, blocking collectives: 8.88 us -> 12.6 us  [shards(): sums = lax.all_to_all(sums, ('ring', 'side'), 0, 0, tiled=True)]
    all_to_all x1, waiting for transfers between devices: 13.2 us -> 16.9 us  [shards(): rows = lax.all_to_all(packed, ('span',) + SEQ, 0, 0, tiled=True)]
    all_to_all x2, waiting for transfers between devices: 18.2 us -> 15.2 us  [the longest x1 15.2 us: shards(): merged = lax.all_to_all(merged, SEQ, 0, 0, tiled=True)]
  transfers between devices with their start and end apart: 8 -> 8, of which waited for: 4 -> 4; matrix products, arithmetic and copies ran while one was open for 0% -> 0% of each run, Pallas kernels for 4% -> 3%
where the time goes in v5:
time: 99.4 us; the launch traced here: 98.7 us
  starting transfers between devices  39.9 us (40%)
  waiting for transfers between devices  37.6 us (38%)
  blocking collectives  12.6 us (13%)
  Pallas kernels  8.4 us (8%)
    all_to_all x1, waiting for transfers between devices, shards(): rows = lax.all_to_all(packed, ('span',) + SEQ, 0, 0, tiled=True)  16.9 us
    all_to_all x1, starting transfers between devices, shards(): rows = lax.all_to_all(packed, ('span',) + SEQ, 0, 0, tiled=True)  16.7 us
    all_to_all x1, waiting for transfers between devices, shards(): merged = lax.all_to_all(merged, SEQ, 0, 0, tiled=True)  15.2 us
    all_to_all x1, blocking collectives, shards(): sums = lax.all_to_all(sums, ('ring', 'side'), 0, 0, tiled=True)  12.6 us
    ppermute x2, starting transfers between devices, swap_sides(): return lax.ppermute(x, 'side', [(0, 1), (1, 0)])  7.12 us
    ppermute x3, starting transfers between devices, swap_cores(): return lax.ppermute(x, 'core', [(0, 1), (1, 0)])  6.25 us
    all_to_all x1, starting transfers between devices, shards(): merged = lax.all_to_all(merged, SEQ, 0, 0, tiled=True)  5.44 us
    ppermute x2, waiting for transfers between devices, swap_sides(): return lax.ppermute(x, 'side', [(0, 1), (1, 0)])  4.5 us
  transfers between devices with their start and end apart: 8, of which 4 were waited for; matrix products, arithmetic and copies ran while one was open for 0% of the time, Pallas kernels for 3%

profile of v5, /device:TPU:8, one launch (start us, length us, event | category | flops | bytes accessed | tf_op | source)
XLA Modules:
  0.0 98.7 jit_solution(13892331898119801780)
XLA Ops:
  0.0 1.8 %pack.1 = bf16[64,40,128]{2,1,0:T(8,128)(2,1)} custom-call(bf16[48,640]{1,0:T(8,128)(2,1)} %q_hbm.1, bf16[48,640]{1,0:T(8,128)(2,1)} %k_hbm.1, bf16[48,640]{1,0:T(8,128)(2,1)} %v_hbm.1), custom_call_target="tpu_custom_call" | custom-call | tf_op jit(solution)/shard_map/pack/pallas_call | solution.py:208
  1.8 0.0 copy-start
  1.8 16.7 %all-to-all-start = ((bf16[64,40,128]{2,1,0:T(8,128)(2,1)}), bf16[64,40,128]{2,1,0:T(8,128)(2,1)S(1)}, u32[]{:S(2)}, u32[]{:S(2)}) async-start(bf16[64,40,128]{2,1,0:T(8,128)(2,1)} %pack.1), calls=%async_computation | async-start | bytes 1310720 | tf_op jit(solution)/shard_map/all_to_all | solution.py:224
  18.6 0.0 copy-done
  18.6 0.0 copy-start.2
  18.6 1.9 %collective-permute-start.1 = (bf16[320,640]{1,0:T(8,128)(2,1)S(1)}, bf16[320,640]{1,0:T(8,128)(2,1)S(1)}, u32[]{:S(2)}, u32[]{:S(2)}) collective-permute-start(bf16[320,640]{1,0:T(8,128)(2,1)S(1)} %bitcast.1), channel_id=1, source_target_pairs={{0,16},{16,0},{1,17},{17,1},{2,18},{18,2},{3,19},{19,3},{4,20},{20... | collective-permute-start | bytes 1228808 | tf_op jit(solution)/shard_map/ppermute | solution.py:203
  20.6 3.4 %collective-permute-start = (bf16[192,640]{1,0:T(8,128)(2,1)S(1)}, bf16[192,640]{1,0:T(8,128)(2,1)S(1)}, u32[]{:S(2)}, u32[]{:S(2)}) collective-permute-start(bf16[192,640]{1,0:T(8,128)(2,1)S(1)} %slice.6), channel_id=1, source_target_pairs={{0,2},{2,0},{1,3},{3,1},{4,6},{6,4},{5,7},{7,5},{8,10},{10,8},{9,1... | collective-permute-start | bytes 737288 | tf_op jit(solution)/shard_map/ppermute | solution.py:199
  23.9 16.9 %all-to-all-done.rows_ref = bf16[64,40,128]{2,1,0:T(8,128)(2,1)S(1)} async-done(((bf16[64,40,128]{2,1,0:T(8,128)(2,1)}), bf16[64,40,128]{2,1,0:T(8,128)(2,1)S(1)}, u32[]{:S(2)}, u32[]{:S(2)}) %all-to-all-start) | async-done | bytes 655392 | tf_op jit(solution)/shard_map/all_to_all | solution.py:224
  40.8 0.0 copy-done.2
  40.8 3.1 %attend.1 = bf16[8,136,128]{2,1,0:T(8,128)(2,1)} custom-call(s32[4]{0:T(128)S(1)} %copy-done.2, bf16[64,40,128]{2,1,0:T(8,128)(2,1)S(1)} %all-to-all-done.rows_ref), custom_call_target="tpu_custom_call" | custom-call | tf_op jit(solution)/shard_map/attend/pallas_call | solution.py:225
  43.9 0.0 collective-permute-done.refs_0_
  43.9 0.0 collective-permute-done.1.other_ref
  43.9 4.4 %all-to-all-start.1 = ((bf16[8,136,128]{2,1,0:T(8,128)(2,1)}), bf16[8,136,128]{2,1,0:T(8,128)(2,1)S(1)}, u32[]{:S(2)}, u32[]{:S(2)}) async-start(bf16[8,136,128]{2,1,0:T(8,128)(2,1)} %attend.1), calls=%async_computation.1 | async-start | bytes 557056 | tf_op jit(solution)/shard_map/all_to_all | solution.py:236
  48.3 3.7 %collective-permute-start.2 = (bf16[128,640]{1,0:T(8,128)(2,1)S(1)}, bf16[128,640]{1,0:T(8,128)(2,1)S(1)}, u32[]{:S(2)}, u32[]{:S(2)}) collective-permute-start(bf16[128,640]{1,0:T(8,128)(2,1)S(1)} %slice.7), channel_id=1, source_target_pairs={{0,2},{2,0},{1,3},{3,1},{4,6},{6,4},{5,7},{7,5},{8,10},{10,8},{9,1... | collective-permute-start | bytes 491528 | tf_op jit(solution)/shard_map/ppermute | solution.py:199
  52.1 4.5 %collective-permute-done.2.refs_1_ = bf16[128,640]{1,0:T(8,128)(2,1)S(1)} collective-permute-done((bf16[128,640]{1,0:T(8,128)(2,1)S(1)}, bf16[128,640]{1,0:T(8,128)(2,1)S(1)}, u32[]{:S(2)}, u32[]{:S(2)}) %collective-permute-start.2) | collective-permute-done | bytes 163872 | tf_op jit(solution)/shard_map/ppermute | solution.py:199
  56.6 0.0 all-to-all-done.1.parts_ref
  56.6 1.4 %merge.1 = bf16[16,64,256]{2,1,0:T(8,128)(2,1)} custom-call(bf16[8,136,128]{2,1,0:T(8,128)(2,1)S(1)} %all-to-all-done.1.parts_ref), custom_call_target="tpu_custom_call" | custom-call | tf_op jit(solution)/shard_map/merge/pallas_call | solution.py:238
  58.0 5.4 %all-to-all-start.2 = ((bf16[16,64,256]{2,1,0:T(8,128)(2,1)}), bf16[16,64,256]{2,1,0:T(8,128)(2,1)S(1)}, u32[]{:S(2)}, u32[]{:S(2)}) async-start(bf16[16,64,256]{2,1,0:T(8,128)(2,1)} %merge.1), calls=%async_computation.2 | async-start | bytes 1048576 | tf_op jit(solution)/shard_map/all_to_all | solution.py:249
  63.5 1.9 %collective-permute-start.3 = (bf16[192,640]{1,0:T(8,128)(2,1)S(1)}, bf16[192,640]{1,0:T(8,128)(2,1)S(1)}, u32[]{:S(2)}, u32[]{:S(2)}) collective-permute-start(bf16[192,640]{1,0:T(8,128)(2,1)S(1)} %collective-permute-done.refs_0_), channel_id=1, source_target_pairs={{0,16},{16,0},{1,17},{17,1},{2,18},{18,2},{3,19},{19,3},{4,20},{20... | collective-permute-start | bytes 737288 | tf_op jit(solution)/shard_map/ppermute | solution.py:203
  65.4 2.4 %collective-permute-start.4 = (bf16[128,640]{1,0:T(8,128)(2,1)S(1)}, bf16[128,640]{1,0:T(8,128)(2,1)S(1)}, u32[]{:S(2)}, u32[]{:S(2)}) collective-permute-start(bf16[128,640]{1,0:T(8,128)(2,1)S(1)} %collective-permute-done.2.refs_1_), channel_id=1, source_target_pairs={{0,16},{16,0},{1,17},{17,1},{2,18},{18,2},{3,19},{19,3},{4,20},{20... | collective-permute-start | bytes 491528 | tf_op jit(solution)/shard_map/ppermute | solution.py:203
  67.8 1.0 %collective-permute-done.4.refs_3_ = bf16[128,640]{1,0:T(8,128)(2,1)S(1)} collective-permute-done((bf16[128,640]{1,0:T(8,128)(2,1)S(1)}, bf16[128,640]{1,0:T(8,128)(2,1)S(1)}, u32[]{:S(2)}, u32[]{:S(2)}) %collective-permute-start.4) | collective-permute-done | bytes 163872 | tf_op jit(solution)/shard_map/ppermute | solution.py:203
  68.8 0.0 collective-permute-done.3.refs_2_
  68.8 15.2 %all-to-all-done.2.rows_ref = bf16[16,64,256]{2,1,0:T(8,128)(2,1)S(1)} async-done(((bf16[16,64,256]{2,1,0:T(8,128)(2,1)}), bf16[16,64,256]{2,1,0:T(8,128)(2,1)S(1)}, u32[]{:S(2)}, u32[]{:S(2)}) %all-to-all-start.2) | async-done | bytes 524320 | tf_op jit(solution)/shard_map/all_to_all | solution.py:249
  84.0 0.8 project.1
  84.9 0.0 copy-start.1
  84.9 0.0 copy-start.3
  84.9 12.6 %all_to_all.20.parts_ref = bf16[8,48,320]{2,1,0:T(8,128)(2,1)S(1)} all-to-all(bf16[8,48,320]{2,1,0:T(8,128)(2,1)S(1)} %project.1), channel_id=1, replica_groups=mesh['span'=4,'ring'=4,'core'=2,'far'=4,'side'=2,'part'=2] {'ring','side'}, dimensions={0} | all-to-all | bytes 491520 | tf_op jit(solution)/shard_map/all_to_all | solution.py:258
  97.5 0.0 copy-done.1
  97.5 0.0 copy-done.3
  97.5 1.2 %finish.1 = bf16[96,320]{1,0:T(8,128)(2,1)} custom-call(s32[4]{0:T(128)S(1)} %copy-done.3, bf16[8,48,320]{2,1,0:T(8,128)(2,1)S(1)} %all_to_all.20.parts_ref, f32[50,320]{1,0:T(8,128)S(1)} %copy-done.1), custom_call_target="tpu_custom_call" | custom-call | tf_op jit(solution)/shard_map/finish/pallas_call | solution.py:259
  (2 shorter events, 0.0 us)
Async XLA Ops:
  1.8 16.8 %copy-start = (bf16[640,320]{0,1:T(8,128)(2,1)S(1)}, bf16[640,320]{0,1:T(8,128)(2,1)}, u32[]{:S(2)}) copy-start(bf16[640,320]{0,1:T(8,128)(2,1)} %param.10) | copy-start | bytes 1228804
  1.8 39.0 %all-to-all-start = ((bf16[64,40,128]{2,1,0:T(8,128)(2,1)}), bf16[64,40,128]{2,1,0:T(8,128)(2,1)S(1)}, u32[]{:S(2)}, u32[]{:S(2)}) async-start(bf16[64,40,128]{2,1,0:T(8,128)(2,1)} %pack.1), calls=%async_computation | async-start | bytes 1310720 | tf_op jit(solution)/shard_map/all_to_all | solution.py:224
  18.6 22.2 %copy-start.2 = (s32[4]{0:T(128)S(1)}, s32[4]{0:T(128)}, u32[]{:S(2)}) copy-start(s32[4]{0:T(128)} %order_ref.1) | copy-start | bytes 52
  18.6 25.3 %collective-permute-start.1 = (bf16[320,640]{1,0:T(8,128)(2,1)S(1)}, bf16[320,640]{1,0:T(8,128)(2,1)S(1)}, u32[]{:S(2)}, u32[]{:S(2)}) collective-permute-start(bf16[320,640]{1,0:T(8,128)(2,1)S(1)} %bitcast.1), channel_id=1, source_target_pairs={{0,16},{16,0},{1,17},{17,1},{2,18},{18,2},{3,19},{19,3},{4,20},{20... | collective-permute-start | bytes 1228808 | tf_op jit(solution)/shard_map/ppermute | solution.py:203
  20.6 23.4 %collective-permute-start = (bf16[192,640]{1,0:T(8,128)(2,1)S(1)}, bf16[192,640]{1,0:T(8,128)(2,1)S(1)}, u32[]{:S(2)}, u32[]{:S(2)}) collective-permute-start(bf16[192,640]{1,0:T(8,128)(2,1)S(1)} %slice.6), channel_id=1, source_target_pairs={{0,2},{2,0},{1,3},{3,1},{4,6},{6,4},{5,7},{7,5},{8,10},{10,8},{9,1... | collective-permute-start | bytes 737288 | tf_op jit(solution)/shard_map/ppermute | solution.py:199
  43.9 12.7 %all-to-all-start.1 = ((bf16[8,136,128]{2,1,0:T(8,128)(2,1)}), bf16[8,136,128]{2,1,0:T(8,128)(2,1)S(1)}, u32[]{:S(2)}, u32[]{:S(2)}) async-start(bf16[8,136,128]{2,1,0:T(8,128)(2,1)} %attend.1), calls=%async_computation.1 | async-start | bytes 557056 | tf_op jit(solution)/shard_map/all_to_all | solution.py:236
  48.3 8.3 %collective-permute-start.2 = (bf16[128,640]{1,0:T(8,128)(2,1)S(1)}, bf16[128,640]{1,0:T(8,128)(2,1)S(1)}, u32[]{:S(2)}, u32[]{:S(2)}) collective-permute-start(bf16[128,640]{1,0:T(8,128)(2,1)S(1)} %slice.7), channel_id=1, source_target_pairs={{0,2},{2,0},{1,3},{3,1},{4,6},{6,4},{5,7},{7,5},{8,10},{10,8},{9,1... | collective-permute-start | bytes 491528 | tf_op jit(solution)/shard_map/ppermute | solution.py:199
  58.0 26.0 %all-to-all-start.2 = ((bf16[16,64,256]{2,1,0:T(8,128)(2,1)}), bf16[16,64,256]{2,1,0:T(8,128)(2,1)S(1)}, u32[]{:S(2)}, u32[]{:S(2)}) async-start(bf16[16,64,256]{2,1,0:T(8,128)(2,1)} %merge.1), calls=%async_computation.2 | async-start | bytes 1048576 | tf_op jit(solution)/shard_map/all_to_all | solution.py:249
  63.5 5.4 %collective-permute-start.3 = (bf16[192,640]{1,0:T(8,128)(2,1)S(1)}, bf16[192,640]{1,0:T(8,128)(2,1)S(1)}, u32[]{:S(2)}, u32[]{:S(2)}) collective-permute-start(bf16[192,640]{1,0:T(8,128)(2,1)S(1)} %collective-permute-done.refs_0_), channel_id=1, source_target_pairs={{0,16},{16,0},{1,17},{17,1},{2,18},{18,2},{3,19},{19,3},{4,20},{20... | collective-permute-start | bytes 737288 | tf_op jit(solution)/shard_map/ppermute | solution.py:203
  65.4 3.4 %collective-permute-start.4 = (bf16[128,640]{1,0:T(8,128)(2,1)S(1)}, bf16[128,640]{1,0:T(8,128)(2,1)S(1)}, u32[]{:S(2)}, u32[]{:S(2)}) collective-permute-start(bf16[128,640]{1,0:T(8,128)(2,1)S(1)} %collective-permute-done.2.refs_1_), channel_id=1, source_target_pairs={{0,16},{16,0},{1,17},{17,1},{2,18},{18,2},{3,19},{19,3},{4,20},{20... | collective-permute-start | bytes 491528 | tf_op jit(solution)/shard_map/ppermute | solution.py:203
  84.9 12.7 %copy-start.1 = (f32[50,320]{1,0:T(8,128)S(1)}, f32[50,320]{1,0:T(8,128)}, u32[]{:S(2)}) copy-start(f32[50,320]{1,0:T(8,128)} %gate_ref.1) | copy-start | bytes 192004
  84.9 12.7 %copy-start.3 = (s32[4]{0:T(128)S(1)}, s32[4]{0:T(128)}, u32[]{:S(2)}) copy-start(s32[4]{0:T(128)} %level_ref.1) | copy-start | bytes 52

commit v6 on v5

--- a/solution.py
+++ b/solution.py
@@ -21,14 +21,13 @@
 KBLOCK = PLACES * KROWS
 QBLOCK = PLACES * QROWS
 CHUNK = 2 * QROWS
-CUT = 192
+CUT = 176
 STATS = 8
 HEAD = ("ring", "core")
 SEQ = ("far", "side", "part")
 EXP2_SCALE = math.log2(math.e) / math.sqrt(HEAD_DIM)
 VMEM = pl.BlockSpec(memory_space=pltpu.VMEM)
 HBM = pl.BlockSpec(memory_space=pltpu.HBM)
-SMEM = pl.BlockSpec(memory_space=pltpu.SMEM)
 
 
 def params(mib=24):
@@ -76,44 +75,54 @@
 
 
 def attend_kernel(order_ref, rows_ref, out_ref, keys_ref, values_ref):
-    which = lax.broadcasted_iota(jnp.int32, (STATS, HEAD_DIM), 0)
+    line = order_ref[...]
+    order = [line[0, i] for i in range(SPANS)]
+    spans = []
     for turn in range(SPANS):
         span = jnp.int32(0)
         for other in range(1, SPANS):
-            span = span + jnp.where(order_ref[other] == turn, other, 0)
-        first = span * PLACES
+            span = span + jnp.where(order[other] == turn, other, 0)
+        spans.append(span)
         for place in range(PLACES):
-            both = rows_ref[first + place, QROWS:, :].astype(jnp.float32)
+            both = rows_ref[span * PLACES + place, QROWS:, :].astype(jnp.float32)
             target = turn * KBLOCK + place * KROWS
             keys_ref[target : target + KROWS, :] = both[:KROWS]
             values_ref[target : target + KROWS, :] = both[KROWS:]
+    keys = keys_ref[...].astype(jnp.bfloat16)
+    values = values_ref[...].astype(jnp.bfloat16)
+    state = []
+    for turn, span in enumerate(spans):
         seen = (turn + 1) * KBLOCK
-        keys = keys_ref[:seen, :].astype(jnp.bfloat16)
-        values = values_ref[:seen, :].astype(jnp.bfloat16)
-        own = rows_ref[pl.ds(first, PLACES), :QROWS, :].reshape(QBLOCK, HEAD_DIM)
+        own = rows_ref[pl.ds(span * PLACES, PLACES), :QROWS, :].reshape(QBLOCK, HEAD_DIM)
         scores = lax.dot_general(
-            own, keys, (((1,), (1,)), ((), ())), preferred_element_type=jnp.float32
-        )
-        scores = scores * EXP2_SCALE
-        highest = jnp.max(scores, axis=1, keepdims=True)
-        weights = jnp.exp2(scores - highest)
-        total = jnp.sum(weights, axis=1, keepdims=True)
-        mixed = jnp.dot(weights.astype(jnp.bfloat16), values, preferred_element_type=jnp.float32)
-        mixed = (mixed / total).astype(jnp.bfloat16)
-        logsum = highest + jnp.log2(total)
-        wide = jnp.transpose(jnp.broadcast_to(logsum, (QBLOCK, HEAD_DIM)))
-        terms = [t.astype(jnp.float32) for t in split_three(wide[:STATS])]
-        stat = jnp.zeros((STATS, HEAD_DIM), jnp.float32)
-        for half in range(2):
-            lanes = slice(half * HEAD_DIM, (half + 1) * HEAD_DIM)
-            for i, term in enumerate(terms):
-                stat = jnp.where(which == 3 * half + i, term[:, lanes], stat)
+            keys[:seen], own, (((1,), (1,)), ((), ())), preferred_element_type=jnp.float32
+        )
+        state.append(scores)
+    soft = []
+    for scores in state:
+        highest = jnp.max(scores, axis=0, keepdims=True) * EXP2_SCALE
+        weights = jnp.exp2(scores * EXP2_SCALE - highest)
+        total = jnp.sum(weights, axis=0, keepdims=True)
+        soft.append((highest, weights.astype(jnp.bfloat16), total))
+    for turn, span in enumerate(spans):
+        seen = (turn + 1) * KBLOCK
+        highest, weights, total = soft[turn]
+        mixed = lax.dot_general(
+            weights, values[:seen], (((0,), (0,)), ((), ())), preferred_element_type=jnp.float32
+        )
+        mixed = (mixed * jnp.transpose(jnp.broadcast_to(1.0 / total, (HEAD_DIM, QBLOCK)))).astype(jnp.bfloat16)
+        terms = [t.astype(jnp.float32) for t in split_three(highest + jnp.log2(total))]
+        stat = [t[:, half * HEAD_DIM : (half + 1) * HEAD_DIM] for half in range(2) for t in terms]
+        stat = jnp.concatenate(
+            stat + [jnp.zeros((STATS - len(stat), HEAD_DIM), jnp.float32)], axis=0
+        )
         for core in range(CORES):
-            piece = span * CORES + core
             for ring in range(RING):
                 source = (ring * CORES + core) * CHUNK
-                out_ref[piece, ring * CHUNK : (ring + 1) * CHUNK, :] = mixed[source : source + CHUNK]
-            out_ref[piece, RING * CHUNK :, :] = stat.astype(jnp.bfloat16)
+                out_ref[span * CORES + core, ring * CHUNK : (ring + 1) * CHUNK, :] = mixed[
+                    source : source + CHUNK
+                ]
+            out_ref[span * CORES + core, RING * CHUNK :, :] = stat.astype(jnp.bfloat16)
 
 
 def merge_kernel(parts_ref, out_ref, turn_ref):
@@ -181,14 +190,12 @@
                 ]
 
 
-def finish_kernel(level_ref, parts_ref, gate_ref, out_ref):
-    level = level_ref[lax.axis_index("span")]
-    gate = gate_ref[pl.ds(level, 1), :]
+def finish_kernel(parts_ref, gate_ref, out_ref):
     for side in range(2):
         total = parts_ref[side].astype(jnp.float32)
         for ring in range(1, RING):
             total = total + parts_ref[ring * 2 + side].astype(jnp.float32)
-        out_ref[side * ROWS : (side + 1) * ROWS, :] = (total * gate).astype(jnp.bfloat16)
+        out_ref[side * ROWS : (side + 1) * ROWS, :] = (total * gate_ref[...]).astype(jnp.bfloat16)
 
 
 def side_of(place):
@@ -218,20 +225,21 @@
         compiler_params=params(60),
         name="pack",
     )(queries, keys, values)
+    level = lax.dynamic_index_in_dim(noise_level, lax.axis_index("span"), 0, keepdims=False)
+    gate_row = lax.dynamic_slice_in_dim(gate_table, level, 1, 0)
     packed, weight = lax.optimization_barrier((packed, out_weight.T))
-    other = swap_cores(weight)
     first = swap_sides(weight[:CUT])
     rows = lax.all_to_all(packed, ("span",) + SEQ, 0, 0, tiled=True)
     parts = pl.pallas_call(
         attend_kernel,
         out_shape=jax.ShapeDtypeStruct((SPANS * CORES, RING * CHUNK + STATS, HEAD_DIM), jnp.bfloat16),
-        in_specs=[SMEM, VMEM],
+        in_specs=[VMEM, VMEM],
         out_specs=VMEM,
         scratch_shapes=[pltpu.VMEM((SPANS * KBLOCK, HEAD_DIM), jnp.float32)] * 2,
         compiler_params=params(),
         name="attend",
-    )(span_order, rows)
-    parts, first, other = lax.optimization_barrier((parts, first, other))
+    )(span_order.reshape(1, SPANS), rows)
+    parts, first, gate_row = lax.optimization_barrier((parts, first, gate_row))
     second = swap_sides(weight[CUT:])
     parts = lax.all_to_all(parts, ("span", "core"), 0, 0, tiled=True)
     parts, second = lax.optimization_barrier((parts, second))
@@ -244,8 +252,8 @@
         compiler_params=params(),
         name="merge",
     )(parts)
-    merged, first, second = lax.optimization_barrier((merged, first, second))
-    first_other, second_other = swap_cores(first), swap_cores(second)
+    merged, weight, first, second = lax.optimization_barrier((merged, weight, first, second))
+    other, first_other, second_other = swap_cores(weight), swap_cores(first), swap_cores(second)
     merged = lax.all_to_all(merged, SEQ, 0, 0, tiled=True)
     sums = pl.pallas_call(
         project_kernel,
@@ -259,11 +267,11 @@
     return pl.pallas_call(
         finish_kernel,
         out_shape=jax.ShapeDtypeStruct((2 * ROWS, out_weight.shape[1]), jnp.bfloat16),
-        in_specs=[SMEM, VMEM, VMEM],
+        in_specs=[VMEM, VMEM],
         out_specs=VMEM,
         compiler_params=params(),
         name="finish",
-    )(noise_level, sums, gate_table)
+    )(sums, gate_row)
 
 
 def solution(mesh):

time: 99.4 us -> 98.5 us (level)
  waiting for transfers between devices: 37.6 us -> 34.6 us
  between operations: 0.13 us -> 2.08 us
  Pallas kernels: 8.4 us -> 6.59 us
  local copies, waits for them, and re-layouts: 0.06 us -> 1.3 us
    all_to_all x1, waiting for transfers between devices: 15.2 us -> 12.7 us  [shards(): merged = lax.all_to_all(merged, SEQ, 0, 0, tiled=True)]
    pallas_call x1, Pallas kernels: 3.09 us -> 1.78 us  [shards(): pl.pallas_call(attend_kernel, out_shape=jax.ShapeDtypeStruct((SPANS * COR...]
    all_to_all x1, waiting for transfers between devices: 16.9 us -> 15.6 us  [shards(): rows = lax.all_to_all(packed, ('span',) + SEQ, 0, 0, tiled=True)]
  transfers between devices with their start and end apart: 8 -> 8, of which waited for: 4 -> 4; matrix products, arithmetic and copies ran while one was open for 0% -> 1% of each run, Pallas kernels for 3% -> 2%
where the time goes in v6:
time: 98.5 us; the launch traced here: 97.9 us
  starting transfers between devices  40.8 us (41%)
  waiting for transfers between devices  34.6 us (35%)
  blocking collectives  12.5 us (13%)
  Pallas kernels  6.59 us (7%)
  between operations  2.08 us (2%)
  local copies, waits for them, and re-layouts  1.3 us (1%)
    all_to_all x1, starting transfers between devices, shards(): rows = lax.all_to_all(packed, ('span',) + SEQ, 0, 0, tiled=True)  16.7 us
    all_to_all x1, waiting for transfers between devices, shards(): rows = lax.all_to_all(packed, ('span',) + SEQ, 0, 0, tiled=True)  15.6 us
    all_to_all x1, waiting for transfers between devices, shards(): merged = lax.all_to_all(merged, SEQ, 0, 0, tiled=True)  12.7 us
    all_to_all x1, blocking collectives, shards(): sums = lax.all_to_all(sums, ('ring', 'side'), 0, 0, tiled=True)  12.5 us
    ppermute x2, starting transfers between devices, swap_sides(): return lax.ppermute(x, 'side', [(0, 1), (1, 0)])  7.1 us
    all_to_all x1, starting transfers between devices, shards(): merged = lax.all_to_all(merged, SEQ, 0, 0, tiled=True)  6.33 us
    ppermute x3, starting transfers between devices, swap_cores(): return lax.ppermute(x, 'core', [(0, 1), (1, 0)])  6.25 us
    ppermute x2, waiting for transfers between devices, swap_sides(): return lax.ppermute(x, 'side', [(0, 1), (1, 0)])  4.94 us
  transfers between devices with their start and end apart: 8, of which 4 were waited for; matrix products, arithmetic and copies ran while one was open for 1% of the time, Pallas kernels for 2%

profile of v6, /device:TPU:8, one launch (start us, length us, event | category | flops | bytes accessed | tf_op | source)
XLA Modules:
  0.0 97.9 jit_solution(11730834307214345317)
XLA Ops:
  0.0 0.0 copy-start
  0.0 1.8 %pack.1 = bf16[64,40,128]{2,1,0:T(8,128)(2,1)} custom-call(bf16[48,640]{1,0:T(8,128)(2,1)} %q_hbm.1, bf16[48,640]{1,0:T(8,128)(2,1)} %k_hbm.1, bf16[48,640]{1,0:T(8,128)(2,1)} %v_hbm.1), custom_call_target="tpu_custom_call" | custom-call | tf_op jit(solution)/shard_map/pack/pallas_call | solution.py:215
  1.9 0.0 copy-start.1
  1.9 16.7 %all-to-all-start = ((bf16[64,40,128]{2,1,0:T(8,128)(2,1)}), bf16[64,40,128]{2,1,0:T(8,128)(2,1)S(1)}, u32[]{:S(2)}, u32[]{:S(2)}) async-start(bf16[64,40,128]{2,1,0:T(8,128)(2,1)} %pack.1), calls=%async_computation | async-start | bytes 1310720 | tf_op jit(solution)/shard_map/all_to_all | solution.py:232
  18.6 0.0 copy-done.1
  18.6 3.4 %collective-permute-start = (bf16[176,640]{1,0:T(8,128)(2,1)S(1)}, bf16[176,640]{1,0:T(8,128)(2,1)S(1)}, u32[]{:S(2)}, u32[]{:S(2)}) collective-permute-start(bf16[176,640]{1,0:T(8,128)(2,1)S(1)} %slice.6), channel_id=1, source_target_pairs={{0,2},{2,0},{1,3},{3,1},{4,6},{6,4},{5,7},{7,5},{8,10},{10,8},{9,1... | collective-permute-start | bytes 675848 | tf_op jit(solution)/shard_map/ppermute | solution.py:206
  22.0 0.0 copy-start.3
  22.0 0.6 copy-done.3
  22.7 0.6 dynamic_slice.7
  25.2 0.0 copy-done
  25.2 0.0 copy-start.2
  25.3 15.6 %all-to-all-done.rows_ref = bf16[64,40,128]{2,1,0:T(8,128)(2,1)S(1)} async-done(((bf16[64,40,128]{2,1,0:T(8,128)(2,1)}), bf16[64,40,128]{2,1,0:T(8,128)(2,1)S(1)}, u32[]{:S(2)}, u32[]{:S(2)}) %all-to-all-start) | async-done | bytes 655392 | tf_op jit(solution)/shard_map/all_to_all | solution.py:232
  40.9 0.0 copy-done.2
  40.9 1.8 %attend.1 = bf16[8,136,128]{2,1,0:T(8,128)(2,1)} custom-call(s32[1,4]{1,0:T(1,128)S(1)} %bitcast.7, bf16[64,40,128]{2,1,0:T(8,128)(2,1)S(1)} %all-to-all-done.rows_ref), custom_call_target="tpu_custom_call" | custom-call | tf_op jit(solution)/shard_map/attend/pallas_call | solution.py:233
  42.6 0.0 collective-permute-done.refs_0_
  42.6 4.4 %all-to-all-start.1 = ((bf16[8,136,128]{2,1,0:T(8,128)(2,1)}), bf16[8,136,128]{2,1,0:T(8,128)(2,1)S(1)}, u32[]{:S(2)}, u32[]{:S(2)}) async-start(bf16[8,136,128]{2,1,0:T(8,128)(2,1)} %attend.1), calls=%async_computation.1 | async-start | bytes 557056 | tf_op jit(solution)/shard_map/all_to_all | solution.py:244
  47.1 3.7 %collective-permute-start.1 = (bf16[144,640]{1,0:T(8,128)(2,1)S(1)}, bf16[144,640]{1,0:T(8,128)(2,1)S(1)}, u32[]{:S(2)}, u32[]{:S(2)}) collective-permute-start(bf16[144,640]{1,0:T(8,128)(2,1)S(1)} %slice.7), channel_id=1, source_target_pairs={{0,2},{2,0},{1,3},{3,1},{4,6},{6,4},{5,7},{7,5},{8,10},{10,8},{9,1... | collective-permute-start | bytes 552968 | tf_op jit(solution)/shard_map/ppermute | solution.py:206
  50.8 4.9 %collective-permute-done.1.refs_1_ = bf16[144,640]{1,0:T(8,128)(2,1)S(1)} collective-permute-done((bf16[144,640]{1,0:T(8,128)(2,1)S(1)}, bf16[144,640]{1,0:T(8,128)(2,1)S(1)}, u32[]{:S(2)}, u32[]{:S(2)}) %collective-permute-start.1) | collective-permute-done | bytes 184352 | tf_op jit(solution)/shard_map/ppermute | solution.py:206
  55.7 0.0 all-to-all-done.1.parts_ref
  55.7 1.4 %merge.1 = bf16[16,64,256]{2,1,0:T(8,128)(2,1)} custom-call(bf16[8,136,128]{2,1,0:T(8,128)(2,1)S(1)} %all-to-all-done.1.parts_ref), custom_call_target="tpu_custom_call" | custom-call | tf_op jit(solution)/shard_map/merge/pallas_call | solution.py:246
  57.2 6.3 %all-to-all-start.2 = ((bf16[16,64,256]{2,1,0:T(8,128)(2,1)}), bf16[16,64,256]{2,1,0:T(8,128)(2,1)S(1)}, u32[]{:S(2)}, u32[]{:S(2)}) async-start(bf16[16,64,256]{2,1,0:T(8,128)(2,1)} %merge.1), calls=%async_computation.2 | async-start | bytes 1048576 | tf_op jit(solution)/shard_map/all_to_all | solution.py:257
  63.5 1.9 %collective-permute-start.2 = (bf16[320,640]{1,0:T(8,128)(2,1)S(1)}, bf16[320,640]{1,0:T(8,128)(2,1)S(1)}, u32[]{:S(2)}, u32[]{:S(2)}) collective-permute-start(bf16[320,640]{1,0:T(8,128)(2,1)S(1)} %bitcast.5), channel_id=1, source_target_pairs={{0,16},{16,0},{1,17},{17,1},{2,18},{18,2},{3,19},{19,3},{4,20},{20... | collective-permute-start | bytes 1228808 | tf_op jit(solution)/shard_map/ppermute | solution.py:210
  65.4 2.4 %collective-permute-start.3 = (bf16[176,640]{1,0:T(8,128)(2,1)S(1)}, bf16[176,640]{1,0:T(8,128)(2,1)S(1)}, u32[]{:S(2)}, u32[]{:S(2)}) collective-permute-start(bf16[176,640]{1,0:T(8,128)(2,1)S(1)} %collective-permute-done.refs_0_), channel_id=1, source_target_pairs={{0,16},{16,0},{1,17},{17,1},{2,18},{18,2},{3,19},{19,3},{4,20},{20... | collective-permute-start | bytes 675848 | tf_op jit(solution)/shard_map/ppermute | solution.py:210
  67.9 1.9 %collective-permute-start.4 = (bf16[144,640]{1,0:T(8,128)(2,1)S(1)}, bf16[144,640]{1,0:T(8,128)(2,1)S(1)}, u32[]{:S(2)}, u32[]{:S(2)}) collective-permute-start(bf16[144,640]{1,0:T(8,128)(2,1)S(1)} %collective-permute-done.1.refs_1_), channel_id=1, source_target_pairs={{0,16},{16,0},{1,17},{17,1},{2,18},{18,2},{3,19},{19,3},{4,20},{20... | collective-permute-start | bytes 552968 | tf_op jit(solution)/shard_map/ppermute | solution.py:210
  69.8 1.4 %collective-permute-done.4.refs_3_ = bf16[144,640]{1,0:T(8,128)(2,1)S(1)} collective-permute-done((bf16[144,640]{1,0:T(8,128)(2,1)S(1)}, bf16[144,640]{1,0:T(8,128)(2,1)S(1)}, u32[]{:S(2)}, u32[]{:S(2)}) %collective-permute-start.4) | collective-permute-done | bytes 184352 | tf_op jit(solution)/shard_map/ppermute | solution.py:210
  71.2 0.0 collective-permute-done.3.refs_2_
  71.2 0.0 collective-permute-done.2.other_ref
  71.2 12.7 %all-to-all-done.2.rows_ref = bf16[16,64,256]{2,1,0:T(8,128)(2,1)S(1)} async-done(((bf16[16,64,256]{2,1,0:T(8,128)(2,1)}), bf16[16,64,256]{2,1,0:T(8,128)(2,1)S(1)}, u32[]{:S(2)}, u32[]{:S(2)}) %all-to-all-start.2) | async-done | bytes 524320 | tf_op jit(solution)/shard_map/all_to_all | solution.py:257
  83.9 0.8 project.1
  84.7 12.5 %all_to_all.20.parts_ref = bf16[8,48,320]{2,1,0:T(8,128)(2,1)S(1)} all-to-all(bf16[8,48,320]{2,1,0:T(8,128)(2,1)S(1)} %project.1), channel_id=1, replica_groups=mesh['span'=4,'ring'=4,'core'=2,'far'=4,'side'=2,'part'=2] {'ring','side'}, dimensions={0} | all-to-all | bytes 491520 | tf_op jit(solution)/shard_map/all_to_all | solution.py:266
  97.2 0.7 finish.1
  (3 shorter events, 0.0 us)
Async XLA Ops:
  0.0 25.2 %copy-start = (f32[50,320]{1,0:T(8,128)S(1)}, f32[50,320]{1,0:T(8,128)}, u32[]{:S(2)}) copy-start(f32[50,320]{1,0:T(8,128)} %param.11) | copy-start | bytes 192004
  1.9 16.8 %copy-start.1 = (bf16[640,320]{0,1:T(8,128)(2,1)S(1)}, bf16[640,320]{0,1:T(8,128)(2,1)}, u32[]{:S(2)}) copy-start(bf16[640,320]{0,1:T(8,128)(2,1)} %param.10) | copy-start | bytes 1228804
  1.9 39.0 %all-to-all-start = ((bf16[64,40,128]{2,1,0:T(8,128)(2,1)}), bf16[64,40,128]{2,1,0:T(8,128)(2,1)S(1)}, u32[]{:S(2)}, u32[]{:S(2)}) async-start(bf16[64,40,128]{2,1,0:T(8,128)(2,1)} %pack.1), calls=%async_computation | async-start | bytes 1310720 | tf_op jit(solution)/shard_map/all_to_all | solution.py:232
  18.6 24.0 %collective-permute-start = (bf16[176,640]{1,0:T(8,128)(2,1)S(1)}, bf16[176,640]{1,0:T(8,128)(2,1)S(1)}, u32[]{:S(2)}, u32[]{:S(2)}) collective-permute-start(bf16[176,640]{1,0:T(8,128)(2,1)S(1)} %slice.6), channel_id=1, source_target_pairs={{0,2},{2,0},{1,3},{3,1},{4,6},{6,4},{5,7},{7,5},{8,10},{10,8},{9,1... | collective-permute-start | bytes 675848 | tf_op jit(solution)/shard_map/ppermute | solution.py:206
  22.0 0.7 copy-start.3
  25.2 15.6 %copy-start.2 = (s32[4]{0:T(128)S(1)}, s32[4]{0:T(128)}, u32[]{:S(2)}) copy-start(s32[4]{0:T(128)} %param.13) | copy-start | bytes 52
  42.6 13.1 %all-to-all-start.1 = ((bf16[8,136,128]{2,1,0:T(8,128)(2,1)}), bf16[8,136,128]{2,1,0:T(8,128)(2,1)S(1)}, u32[]{:S(2)}, u32[]{:S(2)}) async-start(bf16[8,136,128]{2,1,0:T(8,128)(2,1)} %attend.1), calls=%async_computation.1 | async-start | bytes 557056 | tf_op jit(solution)/shard_map/all_to_all | solution.py:244
  47.1 8.7 %collective-permute-start.1 = (bf16[144,640]{1,0:T(8,128)(2,1)S(1)}, bf16[144,640]{1,0:T(8,128)(2,1)S(1)}, u32[]{:S(2)}, u32[]{:S(2)}) collective-permute-start(bf16[144,640]{1,0:T(8,128)(2,1)S(1)} %slice.7), channel_id=1, source_target_pairs={{0,2},{2,0},{1,3},{3,1},{4,6},{6,4},{5,7},{7,5},{8,10},{10,8},{9,1... | collective-permute-start | bytes 552968 | tf_op jit(solution)/shard_map/ppermute | solution.py:206
  57.2 26.7 %all-to-all-start.2 = ((bf16[16,64,256]{2,1,0:T(8,128)(2,1)}), bf16[16,64,256]{2,1,0:T(8,128)(2,1)S(1)}, u32[]{:S(2)}, u32[]{:S(2)}) async-start(bf16[16,64,256]{2,1,0:T(8,128)(2,1)} %merge.1), calls=%async_computation.2 | async-start | bytes 1048576 | tf_op jit(solution)/shard_map/all_to_all | solution.py:257
  63.5 7.7 %collective-permute-start.2 = (bf16[320,640]{1,0:T(8,128)(2,1)S(1)}, bf16[320,640]{1,0:T(8,128)(2,1)S(1)}, u32[]{:S(2)}, u32[]{:S(2)}) collective-permute-start(bf16[320,640]{1,0:T(8,128)(2,1)S(1)} %bitcast.5), channel_id=1, source_target_pairs={{0,16},{16,0},{1,17},{17,1},{2,18},{18,2},{3,19},{19,3},{4,20},{20... | collective-permute-start | bytes 1228808 | tf_op jit(solution)/shard_map/ppermute | solution.py:210
  65.4 5.7 %collective-permute-start.3 = (bf16[176,640]{1,0:T(8,128)(2,1)S(1)}, bf16[176,640]{1,0:T(8,128)(2,1)S(1)}, u32[]{:S(2)}, u32[]{:S(2)}) collective-permute-start(bf16[176,640]{1,0:T(8,128)(2,1)S(1)} %collective-permute-done.refs_0_), channel_id=1, source_target_pairs={{0,16},{16,0},{1,17},{17,1},{2,18},{18,2},{3,19},{19,3},{4,20},{20... | collective-permute-start | bytes 675848 | tf_op jit(solution)/shard_map/ppermute | solution.py:210
  67.9 3.3 %collective-permute-start.4 = (bf16[144,640]{1,0:T(8,128)(2,1)S(1)}, bf16[144,640]{1,0:T(8,128)(2,1)S(1)}, u32[]{:S(2)}, u32[]{:S(2)}) collective-permute-start(bf16[144,640]{1,0:T(8,128)(2,1)S(1)} %collective-permute-done.1.refs_1_), channel_id=1, source_target_pairs={{0,16},{16,0},{1,17},{17,1},{2,18},{18,2},{3,19},{19,3},{4,20},{20... | collective-permute-start | bytes 552968 | tf_op jit(solution)/shard_map/ppermute | solution.py:210

commit v7 on v6

--- a/solution.py
+++ b/solution.py
@@ -21,7 +21,6 @@
 KBLOCK = PLACES * KROWS
 QBLOCK = PLACES * QROWS
 CHUNK = 2 * QROWS
-CUT = 176
 STATS = 8
 HEAD = ("ring", "core")
 SEQ = ("far", "side", "part")
@@ -32,6 +31,10 @@
 
 def params(mib=24):
     return pltpu.CompilerParams(vmem_limit_bytes=mib * 2**20)
+
+
+def spot(place):
+    return place % 2 * (PLACES // 2) + place // 2
 
 
 def pack_kernel(q_hbm, k_hbm, v_hbm, out_ref, q_ref, k_ref, v_ref, kv_ref, sems):
@@ -43,14 +46,14 @@
         copy.start()
     for span in range(SPANS):
         for place in range(HEADS_HERE * BLOCKS, PLACES):
-            out_ref[span * PLACES + place] = jnp.zeros(out_ref.shape[1:], out_ref.dtype)
+            out_ref[span * PLACES + spot(place)] = jnp.zeros(out_ref.shape[1:], out_ref.dtype)
     copies[0].wait()
     for head in range(HEADS_HERE):
         cols = slice(head * HEAD_DIM, (head + 1) * HEAD_DIM)
         for block in range(BLOCKS):
             part = q_ref[block * QROWS : (block + 1) * QROWS, cols]
             for span in range(SPANS):
-                out_ref[span * PLACES + head * BLOCKS + block, :QROWS, :] = part
+                out_ref[span * PLACES + spot(head * BLOCKS + block), :QROWS, :] = part
     copies[1].wait()
     copies[2].wait()
     key_rows = k_ref[...].astype(jnp.float32)
@@ -63,7 +66,7 @@
         for head in range(HEADS_HERE):
             part = both[:, head * HEAD_DIM : (head + 1) * HEAD_DIM]
             for block in range(BLOCKS):
-                out_ref[span * PLACES + head * BLOCKS + block, QROWS:, :] = part
+                out_ref[span * PLACES + spot(head * BLOCKS + block), QROWS:, :] = part
 
 
 def split_three(x):
@@ -93,7 +96,9 @@
     state = []
     for turn, span in enumerate(spans):
         seen = (turn + 1) * KBLOCK
-        own = rows_ref[pl.ds(span * PLACES, PLACES), :QROWS, :].reshape(QBLOCK, HEAD_DIM)
+        own = jnp.concatenate(
+            [rows_ref[span * PLACES + spot(place), :QROWS, :] for place in range(PLACES)], axis=0
+        )
         scores = lax.dot_general(
             keys[:seen], own, (((1,), (1,)), ((), ())), preferred_element_type=jnp.float32
         )
@@ -160,8 +165,7 @@
                 ]
 
 
-def project_kernel(rows_ref, own_ref, other_ref, *refs):
-    swaps, out_ref = refs[:4], refs[4]
+def project_kernel(rows_ref, own_ref, other_ref, theirs_ref, theirs_other_ref, out_ref):
     side = lax.axis_index("side")
     left = [
         jnp.concatenate(
@@ -175,10 +179,12 @@
         )
         for lanes in (slice(0, HEAD_DIM), slice(HEAD_DIM, 2 * HEAD_DIM))
     ]
-    own, other = (jnp.concatenate([a[...], b[...]], axis=0) for a, b in (swaps[:2], swaps[2:]))
-    for weights, target in (((own_ref[...], other_ref[...]), side), ((own, other), 1 - side)):
+    for weights, target in (
+        ((own_ref, other_ref), side),
+        ((theirs_ref, theirs_other_ref), 1 - side),
+    ):
         sums = [
-            lax.dot_general(x, w, (((1,), (1,)), ((), ())), preferred_element_type=jnp.float32)
+            lax.dot_general(x, w[...], (((1,), (1,)), ((), ())), preferred_element_type=jnp.float32)
             for x, w in zip(left, weights)
         ]
         total = (sums[0] + sums[1]).astype(jnp.bfloat16)
@@ -228,8 +234,9 @@
     level = lax.dynamic_index_in_dim(noise_level, lax.axis_index("span"), 0, keepdims=False)
     gate_row = lax.dynamic_slice_in_dim(gate_table, level, 1, 0)
     packed, weight = lax.optimization_barrier((packed, out_weight.T))
-    first = swap_sides(weight[:CUT])
-    rows = lax.all_to_all(packed, ("span",) + SEQ, 0, 0, tiled=True)
+    theirs, other = swap_sides(weight), swap_cores(weight)
+    theirs_other = swap_cores(theirs)
+    rows = lax.all_to_all(packed, ("span", "part", "far", "side"), 0, 0, tiled=True)
     parts = pl.pallas_call(
         attend_kernel,
         out_shape=jax.ShapeDtypeStruct((SPANS * CORES, RING * CHUNK + STATS, HEAD_DIM), jnp.bfloat16),
@@ -239,10 +246,9 @@
         compiler_params=params(),
         name="attend",
     )(span_order.reshape(1, SPANS), rows)
-    parts, first, gate_row = lax.optimization_barrier((parts, first, gate_row))
-    second = swap_sides(weight[CUT:])
+    parts, other, gate_row = lax.optimization_barrier((parts, other, gate_row))
     parts = lax.all_to_all(parts, ("span", "core"), 0, 0, tiled=True)
-    parts, second = lax.optimization_barrier((parts, second))
+    parts, theirs, theirs_other = lax.optimization_barrier((parts, theirs, theirs_other))
     merged = pl.pallas_call(
         merge_kernel,
         out_shape=jax.ShapeDtypeStruct((PLACES, RING * QROWS, CORES * HEAD_DIM), jnp.bfloat16),
@@ -252,17 +258,15 @@
         compiler_params=params(),
         name="merge",
     )(parts)
-    merged, weight, first, second = lax.optimization_barrier((merged, weight, first, second))
-    other, first_other, second_other = swap_cores(weight), swap_cores(first), swap_cores(second)
     merged = lax.all_to_all(merged, SEQ, 0, 0, tiled=True)
     sums = pl.pallas_call(
         project_kernel,
         out_shape=jax.ShapeDtypeStruct((RING * 2, ROWS, out_weight.shape[1]), jnp.bfloat16),
-        in_specs=[VMEM] * 7,
+        in_specs=[VMEM] * 5,
         out_specs=VMEM,
         compiler_params=params(),
         name="project",
-    )(merged, weight, other, first, second, first_other, second_other)
+    )(merged, weight, other, theirs, theirs_other)
     sums = lax.all_to_all(sums, ("ring", "side"), 0, 0, tiled=True)
     return pl.pallas_call(
         finish_kernel,

time: 98.5 us -> 94.9 us (0.963)
  blocking collectives: 12.5 us -> 37.8 us
  waiting for transfers between devices: 34.6 us -> 19.3 us
  starting transfers between devices: 40.8 us -> 28.2 us
    all_to_all x0 -> x1, blocking collectives: none -> 25.3 us  [shards(): merged = lax.all_to_all(merged, SEQ, 0, 0, tiled=True)]
    all_to_all x2 -> x1, waiting for transfers between devices: 28.3 us -> 13.2 us  [shards(): lax.all_to_all(packed, ('span', 'part', 'far', 'side'), 0, 0, tiled=True)]
    all_to_all x2 -> x1, starting transfers between devices: 23.1 us -> 16.7 us  [shards(): lax.all_to_all(packed, ('span', 'part', 'far', 'side'), 0, 0, tiled=True)]
    ppermute x2 -> x1, waiting for transfers between devices: 4.94 us -> 0.01 us  [swap_sides(): return lax.ppermute(x, 'side', [(0, 1), (1, 0)])]
    all_to_all x1, waiting for transfers between devices: 0.01 us -> 4.52 us  [shards(): parts = lax.all_to_all(parts, ('span', 'core'), 0, 0, tiled=True)]
    ppermute x2 -> x1, starting transfers between devices: 7.1 us -> 3.37 us  [swap_sides(): return lax.ppermute(x, 'side', [(0, 1), (1, 0)])]
    ppermute x3 -> x2, starting transfers between devices: 6.25 us -> 3.97 us  [swap_cores(): return lax.ppermute(x, 'core', [(0, 1), (1, 0)])]
  transfers between devices with their start and end apart: 8 -> 5, of which waited for: 4 -> 3; matrix products, arithmetic and copies ran while one was open for 1% -> 1% of each run, Pallas kernels for 2% -> 2%
where the time goes in v7:
time: 94.9 us; the launch traced here: 94.4 us
  blocking collectives  37.8 us (40%)
  starting transfers between devices  28.2 us (30%)
  waiting for transfers between devices  19.3 us (20%)
  Pallas kernels  5.79 us (6%)
  between operations  2.06 us (2%)
  local copies, waits for them, and re-layouts  1.26 us (1%)
    all_to_all x1, blocking collectives, shards(): merged = lax.all_to_all(merged, SEQ, 0, 0, tiled=True)  25.3 us
    all_to_all x1, starting transfers between devices, shards(): lax.all_to_all(packed, ('span', 'part', 'far', 'side'), 0, 0, tiled=True)  16.7 us
    all_to_all x1, waiting for transfers between devices, shards(): lax.all_to_all(packed, ('span', 'part', 'far', 'side'), 0, 0, tiled=True)  13.2 us
    all_to_all x1, blocking collectives, shards(): sums = lax.all_to_all(sums, ('ring', 'side'), 0, 0, tiled=True)  12.5 us
    all_to_all x1, waiting for transfers between devices, shards(): parts = lax.all_to_all(parts, ('span', 'core'), 0, 0, tiled=True)  4.52 us
    all_to_all x1, starting transfers between devices, shards(): parts = lax.all_to_all(parts, ('span', 'core'), 0, 0, tiled=True)  4.08 us
    ppermute x2, starting transfers between devices, swap_cores(): return lax.ppermute(x, 'core', [(0, 1), (1, 0)])  3.97 us
    ppermute x1, starting transfers between devices, swap_sides(): return lax.ppermute(x, 'side', [(0, 1), (1, 0)])  3.37 us
  transfers between devices with their start and end apart: 5, of which 3 were waited for; matrix products, arithmetic and copies ran while one was open for 1% of the time, Pallas kernels for 2%

profile of v7, /device:TPU:8, one launch (start us, length us, event | category | flops | bytes accessed | tf_op | source)
XLA Modules:
  0.0 94.4 jit_solution(5075126391547409303)
XLA Ops:
  0.0 0.0 copy-start
  0.0 1.8 %pack.1 = bf16[64,40,128]{2,1,0:T(8,128)(2,1)} custom-call(bf16[48,640]{1,0:T(8,128)(2,1)} %q_hbm.1, bf16[48,640]{1,0:T(8,128)(2,1)} %k_hbm.1, bf16[48,640]{1,0:T(8,128)(2,1)} %v_hbm.1), custom_call_target="tpu_custom_call" | custom-call | tf_op jit(solution)/shard_map/pack/pallas_call | solution.py:221
  1.9 0.0 copy-start.1
  1.9 16.7 %all-to-all-start = ((bf16[64,40,128]{2,1,0:T(8,128)(2,1)}), bf16[64,40,128]{2,1,0:T(8,128)(2,1)S(1)}, u32[]{:S(2)}, u32[]{:S(2)}) async-start(bf16[64,40,128]{2,1,0:T(8,128)(2,1)} %pack.1), calls=%async_computation | async-start | bytes 1310720 | tf_op jit(solution)/shard_map/all_to_all | solution.py:239
  18.6 0.0 copy-done.1
  18.6 1.9 %collective-permute-start = (bf16[320,640]{1,0:T(8,128)(2,1)S(1)}, bf16[320,640]{1,0:T(8,128)(2,1)S(1)}, u32[]{:S(2)}, u32[]{:S(2)}) collective-permute-start(bf16[320,640]{1,0:T(8,128)(2,1)S(1)} %bitcast.3), channel_id=1, source_target_pairs={{0,16},{16,0},{1,17},{17,1},{2,18},{18,2},{3,19},{19,3},{4,20},{20... | collective-permute-start | bytes 1228808 | tf_op jit(solution)/shard_map/ppermute | solution.py:216
  20.5 3.4 %collective-permute-start.1 = (bf16[320,640]{1,0:T(8,128)(2,1)S(1)}, bf16[320,640]{1,0:T(8,128)(2,1)S(1)}, u32[]{:S(2)}, u32[]{:S(2)}) collective-permute-start(bf16[320,640]{1,0:T(8,128)(2,1)S(1)} %bitcast.4), channel_id=1, source_target_pairs={{0,2},{2,0},{1,3},{3,1},{4,6},{6,4},{5,7},{7,5},{8,10},{10,8},{9,1... | collective-permute-start | bytes 1228808 | tf_op jit(solution)/shard_map/ppermute | solution.py:212
  23.9 0.0 copy-start.3
  23.9 0.6 copy-done.3
  24.6 0.6 dynamic_slice.7
  27.1 0.0 copy-done
  27.1 0.0 copy-start.2
  27.2 13.2 %all-to-all-done.rows_ref = bf16[64,40,128]{2,1,0:T(8,128)(2,1)S(1)} async-done(((bf16[64,40,128]{2,1,0:T(8,128)(2,1)}), bf16[64,40,128]{2,1,0:T(8,128)(2,1)S(1)}, u32[]{:S(2)}, u32[]{:S(2)}) %all-to-all-start) | async-done | bytes 655392 | tf_op jit(solution)/shard_map/all_to_all | solution.py:239
  40.4 0.0 copy-done.2
  40.4 1.8 %attend.1 = bf16[8,136,128]{2,1,0:T(8,128)(2,1)} custom-call(s32[1,4]{1,0:T(1,128)S(1)} %bitcast.6, bf16[64,40,128]{2,1,0:T(8,128)(2,1)S(1)} %all-to-all-done.rows_ref), custom_call_target="tpu_custom_call" | custom-call | tf_op jit(solution)/shard_map/attend/pallas_call | solution.py:240
  42.2 0.0 collective-permute-done.other_ref
  42.2 4.1 %all-to-all-start.1 = ((bf16[8,136,128]{2,1,0:T(8,128)(2,1)}), bf16[8,136,128]{2,1,0:T(8,128)(2,1)S(1)}, u32[]{:S(2)}, u32[]{:S(2)}) async-start(bf16[8,136,128]{2,1,0:T(8,128)(2,1)} %attend.1), calls=%async_computation.1 | async-start | bytes 557056 | tf_op jit(solution)/shard_map/all_to_all | solution.py:250
  46.2 0.0 collective-permute-done.1.theirs_ref
  46.2 2.0 %collective-permute-start.2 = (bf16[320,640]{1,0:T(8,128)(2,1)S(1)}, bf16[320,640]{1,0:T(8,128)(2,1)S(1)}, u32[]{:S(2)}, u32[]{:S(2)}) collective-permute-start(bf16[320,640]{1,0:T(8,128)(2,1)S(1)} %collective-permute-done.1.theirs_ref), channel_id=1, source_target_pairs={{0,16},{16,0},{1,17},{17,1},{2,18},{18,2},{3,19},{19,3},{4,20},{20... | collective-permute-start | bytes 1228808 | tf_op jit(solution)/shard_map/ppermute | solution.py:216
  48.3 1.6 %collective-permute-done.2.theirs_other_ref = bf16[320,640]{1,0:T(8,128)(2,1)S(1)} collective-permute-done((bf16[320,640]{1,0:T(8,128)(2,1)S(1)}, bf16[320,640]{1,0:T(8,128)(2,1)S(1)}, u32[]{:S(2)}, u32[]{:S(2)}) %collective-permute-start.2) | collective-permute-done | bytes 409632 | tf_op jit(solution)/shard_map/ppermute | solution.py:216
  49.9 4.5 %all-to-all-done.1.parts_ref = bf16[8,136,128]{2,1,0:T(8,128)(2,1)S(1)} async-done(((bf16[8,136,128]{2,1,0:T(8,128)(2,1)}), bf16[8,136,128]{2,1,0:T(8,128)(2,1)S(1)}, u32[]{:S(2)}, u32[]{:S(2)}) %all-to-all-start.1) | async-done | bytes 278560 | tf_op jit(solution)/shard_map/all_to_all | solution.py:250
  54.4 0.6 merge.1
  55.0 25.3 %all_to_all.20.rows_ref = bf16[16,64,256]{2,1,0:T(8,128)(2,1)S(1)} all-to-all(bf16[16,64,256]{2,1,0:T(8,128)(2,1)S(1)} %merge.1), channel_id=1, replica_groups=mesh['span'=4,'ring'=4,'core'=2,'far'=4,'side'=2,'part'=2] {'far','side'..., dimensions={0} | all-to-all | bytes 1048576 | tf_op jit(solution)/shard_map/all_to_all | solution.py:261
  80.4 0.8 project.1
  81.2 12.5 %all_to_all.21.parts_ref = bf16[8,48,320]{2,1,0:T(8,128)(2,1)S(1)} all-to-all(bf16[8,48,320]{2,1,0:T(8,128)(2,1)S(1)} %project.1), channel_id=1, replica_groups=mesh['span'=4,'ring'=4,'core'=2,'far'=4,'side'=2,'part'=2] {'ring','side'}, dimensions={0} | all-to-all | bytes 491520 | tf_op jit(solution)/shard_map/all_to_all | solution.py:270
  93.7 0.7 finish.1
  (1 shorter events, 0.0 us)
Async XLA Ops:
  0.0 27.1 %copy-start = (f32[50,320]{1,0:T(8,128)S(1)}, f32[50,320]{1,0:T(8,128)}, u32[]{:S(2)}) copy-start(f32[50,320]{1,0:T(8,128)} %param.11) | copy-start | bytes 192004
  1.9 16.8 %copy-start.1 = (bf16[640,320]{0,1:T(8,128)(2,1)S(1)}, bf16[640,320]{0,1:T(8,128)(2,1)}, u32[]{:S(2)}) copy-start(bf16[640,320]{0,1:T(8,128)(2,1)} %param.10) | copy-start | bytes 1228804
  1.9 38.5 %all-to-all-start = ((bf16[64,40,128]{2,1,0:T(8,128)(2,1)}), bf16[64,40,128]{2,1,0:T(8,128)(2,1)S(1)}, u32[]{:S(2)}, u32[]{:S(2)}) async-start(bf16[64,40,128]{2,1,0:T(8,128)(2,1)} %pack.1), calls=%async_computation | async-start | bytes 1310720 | tf_op jit(solution)/shard_map/all_to_all | solution.py:239
  18.6 23.5 %collective-permute-start = (bf16[320,640]{1,0:T(8,128)(2,1)S(1)}, bf16[320,640]{1,0:T(8,128)(2,1)S(1)}, u32[]{:S(2)}, u32[]{:S(2)}) collective-permute-start(bf16[320,640]{1,0:T(8,128)(2,1)S(1)} %bitcast.3), channel_id=1, source_target_pairs={{0,16},{16,0},{1,17},{17,1},{2,18},{18,2},{3,19},{19,3},{4,20},{20... | collective-permute-start | bytes 1228808 | tf_op jit(solution)/shard_map/ppermute | solution.py:216
  20.5 25.7 %collective-permute-start.1 = (bf16[320,640]{1,0:T(8,128)(2,1)S(1)}, bf16[320,640]{1,0:T(8,128)(2,1)S(1)}, u32[]{:S(2)}, u32[]{:S(2)}) collective-permute-start(bf16[320,640]{1,0:T(8,128)(2,1)S(1)} %bitcast.4), channel_id=1, source_target_pairs={{0,2},{2,0},{1,3},{3,1},{4,6},{6,4},{5,7},{7,5},{8,10},{10,8},{9,1... | collective-permute-start | bytes 1228808 | tf_op jit(solution)/shard_map/ppermute | solution.py:212
  23.9 0.7 copy-start.3
  27.1 13.2 %copy-start.2 = (s32[4]{0:T(128)S(1)}, s32[4]{0:T(128)}, u32[]{:S(2)}) copy-start(s32[4]{0:T(128)} %param.13) | copy-start | bytes 52
  42.2 12.2 %all-to-all-start.1 = ((bf16[8,136,128]{2,1,0:T(8,128)(2,1)}), bf16[8,136,128]{2,1,0:T(8,128)(2,1)S(1)}, u32[]{:S(2)}, u32[]{:S(2)}) async-start(bf16[8,136,128]{2,1,0:T(8,128)(2,1)} %attend.1), calls=%async_computation.1 | async-start | bytes 557056 | tf_op jit(solution)/shard_map/all_to_all | solution.py:250
  46.2 3.6 %collective-permute-start.2 = (bf16[320,640]{1,0:T(8,128)(2,1)S(1)}, bf16[320,640]{1,0:T(8,128)(2,1)S(1)}, u32[]{:S(2)}, u32[]{:S(2)}) collective-permute-start(bf16[320,640]{1,0:T(8,128)(2,1)S(1)} %collective-permute-done.1.theirs_ref), channel_id=1, source_target_pairs={{0,16},{16,0},{1,17},{17,1},{2,18},{18,2},{3,19},{19,3},{4,20},{20... | collective-permute-start | bytes 1228808 | tf_op jit(solution)/shard_map/ppermute | solution.py:216

commit v8 on v7

--- a/solution.py
+++ b/solution.py
@@ -85,6 +85,7 @@
         span = jnp.int32(0)
         for other in range(1, SPANS):
             span = span + jnp.where(order[other] == turn, other, 0)
+        span = jnp.minimum(span, SPANS - 1)
         spans.append(span)
         for place in range(PLACES):
             both = rows_ref[span * PLACES + place, QROWS:, :].astype(jnp.float32)
@@ -187,21 +188,36 @@
             lax.dot_general(x, w[...], (((1,), (1,)), ((), ())), preferred_element_type=jnp.float32)
             for x, w in zip(left, weights)
         ]
-        total = (sums[0] + sums[1]).astype(jnp.bfloat16)
+        total = sums[0] + sums[1]
         for ring in range(RING):
-            for block in range(BLOCKS):
-                source = (block * RING + ring) * QROWS
-                out_ref[ring * 2 + target, block * QROWS : (block + 1) * QROWS, :] = total[
-                    source : source + QROWS
-                ]
+            piece = jnp.concatenate(
+                [
+                    total[(block * RING + ring) * QROWS : (block * RING + ring + 1) * QROWS]
+                    for block in range(BLOCKS)
+                ],
+                axis=0,
+            )
+            edge = piece[:, 2 * HEAD_DIM :]
+            edge = jnp.concatenate([edge[: ROWS // 2], edge[ROWS // 2 :]], axis=1)
+            dense = [piece[:, :HEAD_DIM], piece[:, HEAD_DIM : 2 * HEAD_DIM], edge]
+            out_ref[ring * 2 + target] = jnp.concatenate(dense, axis=0).astype(jnp.bfloat16)
 
 
 def finish_kernel(parts_ref, gate_ref, out_ref):
+    gate = gate_ref[...]
+    half, width = ROWS // 2, out_ref.shape[1] - 2 * HEAD_DIM
     for side in range(2):
         total = parts_ref[side].astype(jnp.float32)
         for ring in range(1, RING):
             total = total + parts_ref[ring * 2 + side].astype(jnp.float32)
-        out_ref[side * ROWS : (side + 1) * ROWS, :] = (total * gate_ref[...]).astype(jnp.bfloat16)
+        begin = side * ROWS
+        for i in range(2):
+            cols = slice(i * HEAD_DIM, (i + 1) * HEAD_DIM)
+            part = total[i * ROWS : (i + 1) * ROWS] * gate[:, cols]
+            out_ref[begin : begin + ROWS, cols] = part.astype(jnp.bfloat16)
+        edge = total[2 * ROWS :]
+        edge = jnp.concatenate([edge[:, :width], edge[:, width:]], axis=0) * gate[:, 2 * HEAD_DIM :]
+        out_ref[begin : begin + ROWS, 2 * HEAD_DIM :] = edge.astype(jnp.bfloat16)
 
 
 def side_of(place):
@@ -261,7 +277,7 @@
     merged = lax.all_to_all(merged, SEQ, 0, 0, tiled=True)
     sums = pl.pallas_call(
         project_kernel,
-        out_shape=jax.ShapeDtypeStruct((RING * 2, ROWS, out_weight.shape[1]), jnp.bfloat16),
+        out_shape=jax.ShapeDtypeStruct((RING * 2, 2 * ROWS + ROWS // 2, HEAD_DIM), jnp.bfloat16),
         in_specs=[VMEM] * 5,
         out_specs=VMEM,
         compiler_params=params(),

time: 94.9 us -> 94.6 us (level)
  no operation moved by 1% of the time
where the time goes in v8:
time: 94.6 us; the launch traced here: 94.1 us
  blocking collectives  37.4 us (40%)
  starting transfers between devices  28.1 us (30%)
  waiting for transfers between devices  19.3 us (20%)
  Pallas kernels  5.93 us (6%)
  between operations  2.05 us (2%)
  local copies, waits for them, and re-layouts  1.26 us (1%)
    all_to_all x1, blocking collectives, shards(): merged = lax.all_to_all(merged, SEQ, 0, 0, tiled=True)  25.3 us
    all_to_all x1, starting transfers between devices, shards(): lax.all_to_all(packed, ('span', 'part', 'far', 'side'), 0, 0, tiled=True)  16.7 us
    all_to_all x1, waiting for transfers between devices, shards(): lax.all_to_all(packed, ('span', 'part', 'far', 'side'), 0, 0, tiled=True)  13.2 us
    all_to_all x1, blocking collectives, shards(): sums = lax.all_to_all(sums, ('ring', 'side'), 0, 0, tiled=True)  12 us
    all_to_all x1, waiting for transfers between devices, shards(): parts = lax.all_to_all(parts, ('span', 'core'), 0, 0, tiled=True)  4.52 us
    all_to_all x1, starting transfers between devices, shards(): parts = lax.all_to_all(parts, ('span', 'core'), 0, 0, tiled=True)  4.07 us
    ppermute x2, starting transfers between devices, swap_cores(): return lax.ppermute(x, 'core', [(0, 1), (1, 0)])  3.97 us
    ppermute x1, starting transfers between devices, swap_sides(): return lax.ppermute(x, 'side', [(0, 1), (1, 0)])  3.37 us
  transfers between devices with their start and end apart: 5, of which 3 were waited for; matrix products, arithmetic and copies ran while one was open for 1% of the time, Pallas kernels for 2%

profile of v8, /device:TPU:8, one launch (start us, length us, event | category | flops | bytes accessed | tf_op | source)
XLA Modules:
  0.0 94.1 jit_solution(2334088135168045572)
XLA Ops:
  0.0 0.0 copy-start
  0.0 1.8 %pack.1 = bf16[64,40,128]{2,1,0:T(8,128)(2,1)} custom-call(bf16[48,640]{1,0:T(8,128)(2,1)} %q_hbm.1, bf16[48,640]{1,0:T(8,128)(2,1)} %k_hbm.1, bf16[48,640]{1,0:T(8,128)(2,1)} %v_hbm.1), custom_call_target="tpu_custom_call" | custom-call | tf_op jit(solution)/shard_map/pack/pallas_call | solution.py:237
  1.9 0.0 copy-start.1
  1.9 16.7 %all-to-all-start = ((bf16[64,40,128]{2,1,0:T(8,128)(2,1)}), bf16[64,40,128]{2,1,0:T(8,128)(2,1)S(1)}, u32[]{:S(2)}, u32[]{:S(2)}) async-start(bf16[64,40,128]{2,1,0:T(8,128)(2,1)} %pack.1), calls=%async_computation | async-start | bytes 1310720 | tf_op jit(solution)/shard_map/all_to_all | solution.py:255
  18.6 0.0 copy-done.1
  18.6 1.9 %collective-permute-start = (bf16[320,640]{1,0:T(8,128)(2,1)S(1)}, bf16[320,640]{1,0:T(8,128)(2,1)S(1)}, u32[]{:S(2)}, u32[]{:S(2)}) collective-permute-start(bf16[320,640]{1,0:T(8,128)(2,1)S(1)} %bitcast.3), channel_id=1, source_target_pairs={{0,16},{16,0},{1,17},{17,1},{2,18},{18,2},{3,19},{19,3},{4,20},{20... | collective-permute-start | bytes 1228808 | tf_op jit(solution)/shard_map/ppermute | solution.py:232
  20.5 3.4 %collective-permute-start.1 = (bf16[320,640]{1,0:T(8,128)(2,1)S(1)}, bf16[320,640]{1,0:T(8,128)(2,1)S(1)}, u32[]{:S(2)}, u32[]{:S(2)}) collective-permute-start(bf16[320,640]{1,0:T(8,128)(2,1)S(1)} %bitcast.4), channel_id=1, source_target_pairs={{0,2},{2,0},{1,3},{3,1},{4,6},{6,4},{5,7},{7,5},{8,10},{10,8},{9,1... | collective-permute-start | bytes 1228808 | tf_op jit(solution)/shard_map/ppermute | solution.py:228
  23.9 0.0 copy-start.3
  23.9 0.6 copy-done.3
  24.6 0.6 dynamic_slice.7
  27.1 0.0 copy-done
  27.1 0.0 copy-start.2
  27.2 13.2 %all-to-all-done.rows_ref = bf16[64,40,128]{2,1,0:T(8,128)(2,1)S(1)} async-done(((bf16[64,40,128]{2,1,0:T(8,128)(2,1)}), bf16[64,40,128]{2,1,0:T(8,128)(2,1)S(1)}, u32[]{:S(2)}, u32[]{:S(2)}) %all-to-all-start) | async-done | bytes 655392 | tf_op jit(solution)/shard_map/all_to_all | solution.py:255
  40.4 0.0 copy-done.2
  40.4 1.8 %attend.1 = bf16[8,136,128]{2,1,0:T(8,128)(2,1)} custom-call(s32[1,4]{1,0:T(1,128)S(1)} %bitcast.6, bf16[64,40,128]{2,1,0:T(8,128)(2,1)S(1)} %all-to-all-done.rows_ref), custom_call_target="tpu_custom_call" | custom-call | tf_op jit(solution)/shard_map/attend/pallas_call | solution.py:256
  42.2 0.0 collective-permute-done.other_ref
  42.2 4.1 %all-to-all-start.1 = ((bf16[8,136,128]{2,1,0:T(8,128)(2,1)}), bf16[8,136,128]{2,1,0:T(8,128)(2,1)S(1)}, u32[]{:S(2)}, u32[]{:S(2)}) async-start(bf16[8,136,128]{2,1,0:T(8,128)(2,1)} %attend.1), calls=%async_computation.1 | async-start | bytes 557056 | tf_op jit(solution)/shard_map/all_to_all | solution.py:266
  46.2 0.0 collective-permute-done.1.theirs_ref
  46.2 2.0 %collective-permute-start.2 = (bf16[320,640]{1,0:T(8,128)(2,1)S(1)}, bf16[320,640]{1,0:T(8,128)(2,1)S(1)}, u32[]{:S(2)}, u32[]{:S(2)}) collective-permute-start(bf16[320,640]{1,0:T(8,128)(2,1)S(1)} %collective-permute-done.1.theirs_ref), channel_id=1, source_target_pairs={{0,16},{16,0},{1,17},{17,1},{2,18},{18,2},{3,19},{19,3},{4,20},{20... | collective-permute-start | bytes 1228808 | tf_op jit(solution)/shard_map/ppermute | solution.py:232
  48.3 1.6 %collective-permute-done.2.theirs_other_ref = bf16[320,640]{1,0:T(8,128)(2,1)S(1)} collective-permute-done((bf16[320,640]{1,0:T(8,128)(2,1)S(1)}, bf16[320,640]{1,0:T(8,128)(2,1)S(1)}, u32[]{:S(2)}, u32[]{:S(2)}) %collective-permute-start.2) | collective-permute-done | bytes 409632 | tf_op jit(solution)/shard_map/ppermute | solution.py:232
  49.9 4.5 %all-to-all-done.1.parts_ref = bf16[8,136,128]{2,1,0:T(8,128)(2,1)S(1)} async-done(((bf16[8,136,128]{2,1,0:T(8,128)(2,1)}), bf16[8,136,128]{2,1,0:T(8,128)(2,1)S(1)}, u32[]{:S(2)}, u32[]{:S(2)}) %all-to-all-start.1) | async-done | bytes 278560 | tf_op jit(solution)/shard_map/all_to_all | solution.py:266
  54.4 0.6 merge.1
  55.0 25.3 %all_to_all.20.rows_ref = bf16[16,64,256]{2,1,0:T(8,128)(2,1)S(1)} all-to-all(bf16[16,64,256]{2,1,0:T(8,128)(2,1)S(1)} %merge.1), channel_id=1, replica_groups=mesh['span'=4,'ring'=4,'core'=2,'far'=4,'side'=2,'part'=2] {'far','side'..., dimensions={0} | all-to-all | bytes 1048576 | tf_op jit(solution)/shard_map/all_to_all | solution.py:277
  80.4 0.9 project.1
  81.3 12.0 %all_to_all.21.parts_ref = bf16[8,120,128]{2,1,0:T(8,128)(2,1)S(1)} all-to-all(bf16[8,120,128]{2,1,0:T(8,128)(2,1)S(1)} %project.1), channel_id=1, replica_groups=mesh['span'=4,'ring'=4,'core'=2,'far'=4,'side'=2,'part'=2] {'ring','side'}, dimensions={0} | all-to-all | bytes 491520 | tf_op jit(solution)/shard_map/all_to_all | solution.py:286
  93.3 0.7 finish.1
  (1 shorter events, 0.0 us)
Async XLA Ops:
  0.0 27.1 %copy-start = (f32[50,320]{1,0:T(8,128)S(1)}, f32[50,320]{1,0:T(8,128)}, u32[]{:S(2)}) copy-start(f32[50,320]{1,0:T(8,128)} %param.11) | copy-start | bytes 192004
  1.9 16.8 %copy-start.1 = (bf16[640,320]{0,1:T(8,128)(2,1)S(1)}, bf16[640,320]{0,1:T(8,128)(2,1)}, u32[]{:S(2)}) copy-start(bf16[640,320]{0,1:T(8,128)(2,1)} %param.10) | copy-start | bytes 1228804
  1.9 38.5 %all-to-all-start = ((bf16[64,40,128]{2,1,0:T(8,128)(2,1)}), bf16[64,40,128]{2,1,0:T(8,128)(2,1)S(1)}, u32[]{:S(2)}, u32[]{:S(2)}) async-start(bf16[64,40,128]{2,1,0:T(8,128)(2,1)} %pack.1), calls=%async_computation | async-start | bytes 1310720 | tf_op jit(solution)/shard_map/all_to_all | solution.py:255
  18.6 23.5 %collective-permute-start = (bf16[320,640]{1,0:T(8,128)(2,1)S(1)}, bf16[320,640]{1,0:T(8,128)(2,1)S(1)}, u32[]{:S(2)}, u32[]{:S(2)}) collective-permute-start(bf16[320,640]{1,0:T(8,128)(2,1)S(1)} %bitcast.3), channel_id=1, source_target_pairs={{0,16},{16,0},{1,17},{17,1},{2,18},{18,2},{3,19},{19,3},{4,20},{20... | collective-permute-start | bytes 1228808 | tf_op jit(solution)/shard_map/ppermute | solution.py:232
  20.5 25.7 %collective-permute-start.1 = (bf16[320,640]{1,0:T(8,128)(2,1)S(1)}, bf16[320,640]{1,0:T(8,128)(2,1)S(1)}, u32[]{:S(2)}, u32[]{:S(2)}) collective-permute-start(bf16[320,640]{1,0:T(8,128)(2,1)S(1)} %bitcast.4), channel_id=1, source_target_pairs={{0,2},{2,0},{1,3},{3,1},{4,6},{6,4},{5,7},{7,5},{8,10},{10,8},{9,1... | collective-permute-start | bytes 1228808 | tf_op jit(solution)/shard_map/ppermute | solution.py:228
  23.9 0.7 copy-start.3
  27.1 13.2 %copy-start.2 = (s32[4]{0:T(128)S(1)}, s32[4]{0:T(128)}, u32[]{:S(2)}) copy-start(s32[4]{0:T(128)} %param.13) | copy-start | bytes 52
  42.2 12.2 %all-to-all-start.1 = ((bf16[8,136,128]{2,1,0:T(8,128)(2,1)}), bf16[8,136,128]{2,1,0:T(8,128)(2,1)S(1)}, u32[]{:S(2)}, u32[]{:S(2)}) async-start(bf16[8,136,128]{2,1,0:T(8,128)(2,1)} %attend.1), calls=%async_computation.1 | async-start | bytes 557056 | tf_op jit(solution)/shard_map/all_to_all | solution.py:266
  46.2 3.6 %collective-permute-start.2 = (bf16[320,640]{1,0:T(8,128)(2,1)S(1)}, bf16[320,640]{1,0:T(8,128)(2,1)S(1)}, u32[]{:S(2)}, u32[]{:S(2)}) collective-permute-start(bf16[320,640]{1,0:T(8,128)(2,1)S(1)} %collective-permute-done.1.theirs_ref), channel_id=1, source_target_pairs={{0,16},{16,0},{1,17},{17,1},{2,18},{18,2},{3,19},{19,3},{4,20},{20... | collective-permute-start | bytes 1228808 | tf_op jit(solution)/shard_map/ppermute | solution.py:232

commit v9 on v8

--- a/solution.py
+++ b/solution.py
@@ -131,6 +131,10 @@
             out_ref[span * CORES + core, RING * CHUNK :, :] = stat.astype(jnp.bfloat16)
 
 
+def berth(place):
+    return place // 4 * 4 + place % 2 * 2 + place // 2 % 2
+
+
 def merge_kernel(parts_ref, out_ref, turn_ref):
     core = lax.axis_index("core")
     slots = (core, CORES - 1 - core)
@@ -161,7 +165,7 @@
             lanes = slice(i * HEAD_DIM, (i + 1) * HEAD_DIM)
             for place in range(PLACES):
                 side = side_of(place)
-                out_ref[place, ring * QROWS : (ring + 1) * QROWS, lanes] = mixed[
+                out_ref[berth(place), ring * QROWS : (ring + 1) * QROWS, lanes] = mixed[
                     side * QROWS : (side + 1) * QROWS
                 ]
 
@@ -172,7 +176,7 @@
         jnp.concatenate(
             [
                 jnp.concatenate(
-                    [rows_ref[head * BLOCKS + b, :, lanes] for b in range(BLOCKS)], axis=0
+                    [rows_ref[berth(head * BLOCKS + b), :, lanes] for b in range(BLOCKS)], axis=0
                 )
                 for head in range(HEADS_HERE)
             ],
@@ -274,7 +278,7 @@
         compiler_params=params(),
         name="merge",
     )(parts)
-    merged = lax.all_to_all(merged, SEQ, 0, 0, tiled=True)
+    merged = lax.all_to_all(merged, ("far", "part", "side"), 0, 0, tiled=True)
     sums = pl.pallas_call(
         project_kernel,
         out_shape=jax.ShapeDtypeStruct((RING * 2, 2 * ROWS + ROWS // 2, HEAD_DIM), jnp.bfloat16),

time: 94.6 us -> 94.3 us (level)
  no operation moved by 1% of the time
where the time goes in v9:
time: 94.3 us; the launch traced here: 93.8 us
  blocking collectives  37.1 us (39%)
  starting transfers between devices  28.1 us (30%)
  waiting for transfers between devices  19.3 us (20%)
  Pallas kernels  5.93 us (6%)
  between operations  2.05 us (2%)
  local copies, waits for them, and re-layouts  1.26 us (1%)
    all_to_all x1, blocking collectives, shards(): merged = lax.all_to_all(merged, ('far', 'part', 'side'), 0, 0, tiled=True)  25.2 us
    all_to_all x1, starting transfers between devices, shards(): lax.all_to_all(packed, ('span', 'part', 'far', 'side'), 0, 0, tiled=True)  16.7 us
    all_to_all x1, waiting for transfers between devices, shards(): lax.all_to_all(packed, ('span', 'part', 'far', 'side'), 0, 0, tiled=True)  13.2 us
    all_to_all x1, blocking collectives, shards(): sums = lax.all_to_all(sums, ('ring', 'side'), 0, 0, tiled=True)  11.9 us
    all_to_all x1, waiting for transfers between devices, shards(): parts = lax.all_to_all(parts, ('span', 'core'), 0, 0, tiled=True)  4.52 us
    all_to_all x1, starting transfers between devices, shards(): parts = lax.all_to_all(parts, ('span', 'core'), 0, 0, tiled=True)  4.07 us
    ppermute x2, starting transfers between devices, swap_cores(): return lax.ppermute(x, 'core', [(0, 1), (1, 0)])  3.97 us
    ppermute x1, starting transfers between devices, swap_sides(): return lax.ppermute(x, 'side', [(0, 1), (1, 0)])  3.37 us
  transfers between devices with their start and end apart: 5, of which 3 were waited for; matrix products, arithmetic and copies ran while one was open for 1% of the time, Pallas kernels for 2%

profile of v9, /device:TPU:8, one launch (start us, length us, event | category | flops | bytes accessed | tf_op | source)
XLA Modules:
  0.0 93.8 jit_solution(2956751158697899085)
XLA Ops:
  0.0 0.0 copy-start
  0.0 1.8 %pack.1 = bf16[64,40,128]{2,1,0:T(8,128)(2,1)} custom-call(bf16[48,640]{1,0:T(8,128)(2,1)} %q_hbm.1, bf16[48,640]{1,0:T(8,128)(2,1)} %k_hbm.1, bf16[48,640]{1,0:T(8,128)(2,1)} %v_hbm.1), custom_call_target="tpu_custom_call" | custom-call | tf_op jit(solution)/shard_map/pack/pallas_call | solution.py:241
  1.9 0.0 copy-start.1
  1.9 16.7 %all-to-all-start = ((bf16[64,40,128]{2,1,0:T(8,128)(2,1)}), bf16[64,40,128]{2,1,0:T(8,128)(2,1)S(1)}, u32[]{:S(2)}, u32[]{:S(2)}) async-start(bf16[64,40,128]{2,1,0:T(8,128)(2,1)} %pack.1), calls=%async_computation | async-start | bytes 1310720 | tf_op jit(solution)/shard_map/all_to_all | solution.py:259
  18.6 0.0 copy-done.1
  18.6 1.9 %collective-permute-start = (bf16[320,640]{1,0:T(8,128)(2,1)S(1)}, bf16[320,640]{1,0:T(8,128)(2,1)S(1)}, u32[]{:S(2)}, u32[]{:S(2)}) collective-permute-start(bf16[320,640]{1,0:T(8,128)(2,1)S(1)} %bitcast.3), channel_id=1, source_target_pairs={{0,16},{16,0},{1,17},{17,1},{2,18},{18,2},{3,19},{19,3},{4,20},{20... | collective-permute-start | bytes 1228808 | tf_op jit(solution)/shard_map/ppermute | solution.py:236
  20.5 3.4 %collective-permute-start.1 = (bf16[320,640]{1,0:T(8,128)(2,1)S(1)}, bf16[320,640]{1,0:T(8,128)(2,1)S(1)}, u32[]{:S(2)}, u32[]{:S(2)}) collective-permute-start(bf16[320,640]{1,0:T(8,128)(2,1)S(1)} %bitcast.4), channel_id=1, source_target_pairs={{0,2},{2,0},{1,3},{3,1},{4,6},{6,4},{5,7},{7,5},{8,10},{10,8},{9,1... | collective-permute-start | bytes 1228808 | tf_op jit(solution)/shard_map/ppermute | solution.py:232
  23.9 0.0 copy-start.3
  23.9 0.6 copy-done.3
  24.6 0.6 dynamic_slice.7
  27.1 0.0 copy-done
  27.1 0.0 copy-start.2
  27.2 13.2 %all-to-all-done.rows_ref = bf16[64,40,128]{2,1,0:T(8,128)(2,1)S(1)} async-done(((bf16[64,40,128]{2,1,0:T(8,128)(2,1)}), bf16[64,40,128]{2,1,0:T(8,128)(2,1)S(1)}, u32[]{:S(2)}, u32[]{:S(2)}) %all-to-all-start) | async-done | bytes 655392 | tf_op jit(solution)/shard_map/all_to_all | solution.py:259
  40.4 0.0 copy-done.2
  40.4 1.8 %attend.1 = bf16[8,136,128]{2,1,0:T(8,128)(2,1)} custom-call(s32[1,4]{1,0:T(1,128)S(1)} %bitcast.6, bf16[64,40,128]{2,1,0:T(8,128)(2,1)S(1)} %all-to-all-done.rows_ref), custom_call_target="tpu_custom_call" | custom-call | tf_op jit(solution)/shard_map/attend/pallas_call | solution.py:260
  42.2 0.0 collective-permute-done.other_ref
  42.2 4.1 %all-to-all-start.1 = ((bf16[8,136,128]{2,1,0:T(8,128)(2,1)}), bf16[8,136,128]{2,1,0:T(8,128)(2,1)S(1)}, u32[]{:S(2)}, u32[]{:S(2)}) async-start(bf16[8,136,128]{2,1,0:T(8,128)(2,1)} %attend.1), calls=%async_computation.1 | async-start | bytes 557056 | tf_op jit(solution)/shard_map/all_to_all | solution.py:270
  46.2 0.0 collective-permute-done.1.theirs_ref
  46.2 2.0 %collective-permute-start.2 = (bf16[320,640]{1,0:T(8,128)(2,1)S(1)}, bf16[320,640]{1,0:T(8,128)(2,1)S(1)}, u32[]{:S(2)}, u32[]{:S(2)}) collective-permute-start(bf16[320,640]{1,0:T(8,128)(2,1)S(1)} %collective-permute-done.1.theirs_ref), channel_id=1, source_target_pairs={{0,16},{16,0},{1,17},{17,1},{2,18},{18,2},{3,19},{19,3},{4,20},{20... | collective-permute-start | bytes 1228808 | tf_op jit(solution)/shard_map/ppermute | solution.py:236
  48.3 1.6 %collective-permute-done.2.theirs_other_ref = bf16[320,640]{1,0:T(8,128)(2,1)S(1)} collective-permute-done((bf16[320,640]{1,0:T(8,128)(2,1)S(1)}, bf16[320,640]{1,0:T(8,128)(2,1)S(1)}, u32[]{:S(2)}, u32[]{:S(2)}) %collective-permute-start.2) | collective-permute-done | bytes 409632 | tf_op jit(solution)/shard_map/ppermute | solution.py:236
  49.9 4.5 %all-to-all-done.1.parts_ref = bf16[8,136,128]{2,1,0:T(8,128)(2,1)S(1)} async-done(((bf16[8,136,128]{2,1,0:T(8,128)(2,1)}), bf16[8,136,128]{2,1,0:T(8,128)(2,1)S(1)}, u32[]{:S(2)}, u32[]{:S(2)}) %all-to-all-start.1) | async-done | bytes 278560 | tf_op jit(solution)/shard_map/all_to_all | solution.py:270
  54.4 0.6 merge.1
  55.0 25.2 %all_to_all.20.rows_ref = bf16[16,64,256]{2,1,0:T(8,128)(2,1)S(1)} all-to-all(bf16[16,64,256]{2,1,0:T(8,128)(2,1)S(1)} %merge.1), channel_id=1, replica_groups=mesh['span'=4,'ring'=4,'core'=2,'far'=4,'side'=2,'part'=2] {'far','part'..., dimensions={0} | all-to-all | bytes 1048576 | tf_op jit(solution)/shard_map/all_to_all | solution.py:281
  80.2 0.9 project.1
  81.1 11.9 %all_to_all.21.parts_ref = bf16[8,120,128]{2,1,0:T(8,128)(2,1)S(1)} all-to-all(bf16[8,120,128]{2,1,0:T(8,128)(2,1)S(1)} %project.1), channel_id=1, replica_groups=mesh['span'=4,'ring'=4,'core'=2,'far'=4,'side'=2,'part'=2] {'ring','side'}, dimensions={0} | all-to-all | bytes 491520 | tf_op jit(solution)/shard_map/all_to_all | solution.py:290
  93.0 0.7 finish.1
  (1 shorter events, 0.0 us)
Async XLA Ops:
  0.0 27.1 %copy-start = (f32[50,320]{1,0:T(8,128)S(1)}, f32[50,320]{1,0:T(8,128)}, u32[]{:S(2)}) copy-start(f32[50,320]{1,0:T(8,128)} %param.11) | copy-start | bytes 192004
  1.9 16.8 %copy-start.1 = (bf16[640,320]{0,1:T(8,128)(2,1)S(1)}, bf16[640,320]{0,1:T(8,128)(2,1)}, u32[]{:S(2)}) copy-start(bf16[640,320]{0,1:T(8,128)(2,1)} %param.10) | copy-start | bytes 1228804
  1.9 38.5 %all-to-all-start = ((bf16[64,40,128]{2,1,0:T(8,128)(2,1)}), bf16[64,40,128]{2,1,0:T(8,128)(2,1)S(1)}, u32[]{:S(2)}, u32[]{:S(2)}) async-start(bf16[64,40,128]{2,1,0:T(8,128)(2,1)} %pack.1), calls=%async_computation | async-start | bytes 1310720 | tf_op jit(solution)/shard_map/all_to_all | solution.py:259
  18.6 23.5 %collective-permute-start = (bf16[320,640]{1,0:T(8,128)(2,1)S(1)}, bf16[320,640]{1,0:T(8,128)(2,1)S(1)}, u32[]{:S(2)}, u32[]{:S(2)}) collective-permute-start(bf16[320,640]{1,0:T(8,128)(2,1)S(1)} %bitcast.3), channel_id=1, source_target_pairs={{0,16},{16,0},{1,17},{17,1},{2,18},{18,2},{3,19},{19,3},{4,20},{20... | collective-permute-start | bytes 1228808 | tf_op jit(solution)/shard_map/ppermute | solution.py:236
  20.5 25.7 %collective-permute-start.1 = (bf16[320,640]{1,0:T(8,128)(2,1)S(1)}, bf16[320,640]{1,0:T(8,128)(2,1)S(1)}, u32[]{:S(2)}, u32[]{:S(2)}) collective-permute-start(bf16[320,640]{1,0:T(8,128)(2,1)S(1)} %bitcast.4), channel_id=1, source_target_pairs={{0,2},{2,0},{1,3},{3,1},{4,6},{6,4},{5,7},{7,5},{8,10},{10,8},{9,1... | collective-permute-start | bytes 1228808 | tf_op jit(solution)/shard_map/ppermute | solution.py:232
  23.9 0.7 copy-start.3
  27.1 13.2 %copy-start.2 = (s32[4]{0:T(128)S(1)}, s32[4]{0:T(128)}, u32[]{:S(2)}) copy-start(s32[4]{0:T(128)} %param.13) | copy-start | bytes 52
  42.2 12.2 %all-to-all-start.1 = ((bf16[8,136,128]{2,1,0:T(8,128)(2,1)}), bf16[8,136,128]{2,1,0:T(8,128)(2,1)S(1)}, u32[]{:S(2)}, u32[]{:S(2)}) async-start(bf16[8,136,128]{2,1,0:T(8,128)(2,1)} %attend.1), calls=%async_computation.1 | async-start | bytes 557056 | tf_op jit(solution)/shard_map/all_to_all | solution.py:270
  46.2 3.6 %collective-permute-start.2 = (bf16[320,640]{1,0:T(8,128)(2,1)S(1)}, bf16[320,640]{1,0:T(8,128)(2,1)S(1)}, u32[]{:S(2)}, u32[]{:S(2)}) collective-permute-start(bf16[320,640]{1,0:T(8,128)(2,1)S(1)} %collective-permute-done.1.theirs_ref), channel_id=1, source_target_pairs={{0,16},{16,0},{1,17},{17,1},{2,18},{18,2},{3,19},{19,3},{4,20},{20... | collective-permute-start | bytes 1228808 | tf_op jit(solution)/shard_map/ppermute | solution.py:236

commit v10 on v9

--- a/solution.py
+++ b/solution.py
@@ -125,10 +125,10 @@
         for core in range(CORES):
             for ring in range(RING):
                 source = (ring * CORES + core) * CHUNK
-                out_ref[span * CORES + core, ring * CHUNK : (ring + 1) * CHUNK, :] = mixed[
+                out_ref[core * SPANS + span, ring * CHUNK : (ring + 1) * CHUNK, :] = mixed[
                     source : source + CHUNK
                 ]
-            out_ref[span * CORES + core, RING * CHUNK :, :] = stat.astype(jnp.bfloat16)
+            out_ref[core * SPANS + span, RING * CHUNK :, :] = stat.astype(jnp.bfloat16)
 
 
 def berth(place):
@@ -142,7 +142,7 @@
     for half in range(2):
         for slot in slots:
             for s in range(SPANS):
-                stats = parts_ref[s * CORES + slot, RING * CHUNK :, :].astype(jnp.float32)
+                stats = parts_ref[slot * SPANS + s, RING * CHUNK :, :].astype(jnp.float32)
                 first = 3 * half
                 rows.append(stats[first : first + 1] + stats[first + 1 : first + 2] + stats[first + 2 : first + 3])
     pad = jnp.zeros((HEAD_DIM - len(rows), HEAD_DIM), jnp.float32)
@@ -159,7 +159,7 @@
             total = functools.reduce(jnp.add, shares)
             mixed = jnp.zeros((CHUNK, HEAD_DIM), jnp.float32)
             for s in range(SPANS):
-                part = parts_ref[s * CORES + slot, ring * CHUNK : (ring + 1) * CHUNK, :]
+                part = parts_ref[slot * SPANS + s, ring * CHUNK : (ring + 1) * CHUNK, :]
                 mixed = mixed + part.astype(jnp.float32) * (shares[s] / total)
             mixed = mixed.astype(jnp.bfloat16)
             lanes = slice(i * HEAD_DIM, (i + 1) * HEAD_DIM)
@@ -188,11 +188,12 @@
         ((own_ref, other_ref), side),
         ((theirs_ref, theirs_other_ref), 1 - side),
     ):
-        sums = [
-            lax.dot_general(x, w[...], (((1,), (1,)), ((), ())), preferred_element_type=jnp.float32)
-            for x, w in zip(left, weights)
-        ]
-        total = sums[0] + sums[1]
+        total = lax.dot_general(
+            jnp.concatenate(left, axis=1),
+            jnp.concatenate([w[...] for w in weights], axis=1),
+            (((1,), (1,)), ((), ())),
+            preferred_element_type=jnp.float32,
+        )
         for ring in range(RING):
             piece = jnp.concatenate(
                 [
@@ -204,16 +205,16 @@
             edge = piece[:, 2 * HEAD_DIM :]
             edge = jnp.concatenate([edge[: ROWS // 2], edge[ROWS // 2 :]], axis=1)
             dense = [piece[:, :HEAD_DIM], piece[:, HEAD_DIM : 2 * HEAD_DIM], edge]
-            out_ref[ring * 2 + target] = jnp.concatenate(dense, axis=0).astype(jnp.bfloat16)
+            out_ref[target * RING + ring] = jnp.concatenate(dense, axis=0).astype(jnp.bfloat16)
 
 
 def finish_kernel(parts_ref, gate_ref, out_ref):
     gate = gate_ref[...]
     half, width = ROWS // 2, out_ref.shape[1] - 2 * HEAD_DIM
     for side in range(2):
-        total = parts_ref[side].astype(jnp.float32)
+        total = parts_ref[side * RING].astype(jnp.float32)
         for ring in range(1, RING):
-            total = total + parts_ref[ring * 2 + side].astype(jnp.float32)
+            total = total + parts_ref[side * RING + ring].astype(jnp.float32)
         begin = side * ROWS
         for i in range(2):
             cols = slice(i * HEAD_DIM, (i + 1) * HEAD_DIM)
@@ -267,7 +268,7 @@
         name="attend",
     )(span_order.reshape(1, SPANS), rows)
     parts, other, gate_row = lax.optimization_barrier((parts, other, gate_row))
-    parts = lax.all_to_all(parts, ("span", "core"), 0, 0, tiled=True)
+    parts = lax.all_to_all(parts, ("core", "span"), 0, 0, tiled=True)
     parts, theirs, theirs_other = lax.optimization_barrier((parts, theirs, theirs_other))
     merged = pl.pallas_call(
         merge_kernel,
@@ -287,7 +288,7 @@
         compiler_params=params(),
         name="project",
     )(merged, weight, other, theirs, theirs_other)
-    sums = lax.all_to_all(sums, ("ring", "side"), 0, 0, tiled=True)
+    sums = lax.all_to_all(sums, ("side", "ring"), 0, 0, tiled=True)
     return pl.pallas_call(
         finish_kernel,
         out_shape=jax.ShapeDtypeStruct((2 * ROWS, out_weight.shape[1]), jnp.bfloat16),

time: 94.3 us -> 94 us (level)
  the two profiles are of different devices: /device:TPU:8 before, /device:TPU:16 now
where the time goes in v10:
time: 94 us; the launch traced here: 93.5 us
  blocking collectives  37.5 us (40%)
  starting transfers between devices  28.6 us (30%)
  waiting for transfers between devices  18.1 us (19%)
  Pallas kernels  5.87 us (6%)
  between operations  2.05 us (2%)
  local copies, waits for them, and re-layouts  1.26 us (1%)
    all_to_all x1, blocking collectives, shards(): merged = lax.all_to_all(merged, ('far', 'part', 'side'), 0, 0, tiled=True)  26 us
    all_to_all x1, starting transfers between devices, shards(): lax.all_to_all(packed, ('span', 'part', 'far', 'side'), 0, 0, tiled=True)  16.7 us
    all_to_all x1, waiting for transfers between devices, shards(): lax.all_to_all(packed, ('span', 'part', 'far', 'side'), 0, 0, tiled=True)  12.6 us
    all_to_all x1, blocking collectives, shards(): sums = lax.all_to_all(sums, ('side', 'ring'), 0, 0, tiled=True)  11.6 us
    all_to_all x1, starting transfers between devices, shards(): parts = lax.all_to_all(parts, ('core', 'span'), 0, 0, tiled=True)  4.56 us
    ppermute x2, starting transfers between devices, swap_cores(): return lax.ppermute(x, 'core', [(0, 1), (1, 0)])  3.97 us
    all_to_all x1, waiting for transfers between devices, shards(): parts = lax.all_to_all(parts, ('core', 'span'), 0, 0, tiled=True)  3.9 us
    ppermute x1, starting transfers between devices, swap_sides(): return lax.ppermute(x, 'side', [(0, 1), (1, 0)])  3.38 us
  transfers between devices with their start and end apart: 5, of which 3 were waited for; matrix products, arithmetic and copies ran while one was open for 1% of the time, Pallas kernels for 2%

profile of v10, /device:TPU:16, one launch (start us, length us, event | category | flops | bytes accessed | tf_op | source)
XLA Modules:
  0.0 93.5 jit_solution(7810727341131150432)
XLA Ops:
  0.0 0.0 copy-start
  0.0 1.8 %pack.1 = bf16[64,40,128]{2,1,0:T(8,128)(2,1)} custom-call(bf16[48,640]{1,0:T(8,128)(2,1)} %q_hbm.1, bf16[48,640]{1,0:T(8,128)(2,1)} %k_hbm.1, bf16[48,640]{1,0:T(8,128)(2,1)} %v_hbm.1), custom_call_target="tpu_custom_call" | custom-call | tf_op jit(solution)/shard_map/pack/pallas_call | solution.py:242
  1.9 0.0 copy-start.1
  1.9 16.7 %all-to-all-start = ((bf16[64,40,128]{2,1,0:T(8,128)(2,1)}), bf16[64,40,128]{2,1,0:T(8,128)(2,1)S(1)}, u32[]{:S(2)}, u32[]{:S(2)}) async-start(bf16[64,40,128]{2,1,0:T(8,128)(2,1)} %pack.1), calls=%async_computation | async-start | bytes 1310720 | tf_op jit(solution)/shard_map/all_to_all | solution.py:260
  18.6 0.0 copy-done.1
  18.6 1.9 %collective-permute-start = (bf16[320,640]{1,0:T(8,128)(2,1)S(1)}, bf16[320,640]{1,0:T(8,128)(2,1)S(1)}, u32[]{:S(2)}, u32[]{:S(2)}) collective-permute-start(bf16[320,640]{1,0:T(8,128)(2,1)S(1)} %bitcast.3), channel_id=1, source_target_pairs={{0,16},{16,0},{1,17},{17,1},{2,18},{18,2},{3,19},{19,3},{4,20},{20... | collective-permute-start | bytes 1228808 | tf_op jit(solution)/shard_map/ppermute | solution.py:237
  20.5 3.4 %collective-permute-start.1 = (bf16[320,640]{1,0:T(8,128)(2,1)S(1)}, bf16[320,640]{1,0:T(8,128)(2,1)S(1)}, u32[]{:S(2)}, u32[]{:S(2)}) collective-permute-start(bf16[320,640]{1,0:T(8,128)(2,1)S(1)} %bitcast.4), channel_id=1, source_target_pairs={{0,2},{2,0},{1,3},{3,1},{4,6},{6,4},{5,7},{7,5},{8,10},{10,8},{9,1... | collective-permute-start | bytes 1228808 | tf_op jit(solution)/shard_map/ppermute | solution.py:233
  23.9 0.0 copy-start.3
  23.9 0.6 copy-done.3
  24.6 0.6 dynamic_slice.7
  27.1 0.0 copy-done
  27.1 0.0 copy-start.2
  27.1 12.6 %all-to-all-done.rows_ref = bf16[64,40,128]{2,1,0:T(8,128)(2,1)S(1)} async-done(((bf16[64,40,128]{2,1,0:T(8,128)(2,1)}), bf16[64,40,128]{2,1,0:T(8,128)(2,1)S(1)}, u32[]{:S(2)}, u32[]{:S(2)}) %all-to-all-start) | async-done | bytes 655392 | tf_op jit(solution)/shard_map/all_to_all | solution.py:260
  39.8 0.0 copy-done.2
  39.8 1.8 %attend.1 = bf16[8,136,128]{2,1,0:T(8,128)(2,1)} custom-call(s32[1,4]{1,0:T(1,128)S(1)} %bitcast.6, bf16[64,40,128]{2,1,0:T(8,128)(2,1)S(1)} %all-to-all-done.rows_ref), custom_call_target="tpu_custom_call" | custom-call | tf_op jit(solution)/shard_map/attend/pallas_call | solution.py:261
  41.6 0.0 collective-permute-done.other_ref
  41.6 4.6 %all-to-all-start.1 = ((bf16[8,136,128]{2,1,0:T(8,128)(2,1)}), bf16[8,136,128]{2,1,0:T(8,128)(2,1)S(1)}, u32[]{:S(2)}, u32[]{:S(2)}) async-start(bf16[8,136,128]{2,1,0:T(8,128)(2,1)} %attend.1), calls=%async_computation.1 | async-start | bytes 557056 | tf_op jit(solution)/shard_map/all_to_all | solution.py:271
  46.1 0.0 collective-permute-done.1.theirs_ref
  46.1 2.0 %collective-permute-start.2 = (bf16[320,640]{1,0:T(8,128)(2,1)S(1)}, bf16[320,640]{1,0:T(8,128)(2,1)S(1)}, u32[]{:S(2)}, u32[]{:S(2)}) collective-permute-start(bf16[320,640]{1,0:T(8,128)(2,1)S(1)} %collective-permute-done.1.theirs_ref), channel_id=1, source_target_pairs={{0,16},{16,0},{1,17},{17,1},{2,18},{18,2},{3,19},{19,3},{4,20},{20... | collective-permute-start | bytes 1228808 | tf_op jit(solution)/shard_map/ppermute | solution.py:237
  48.2 1.6 %collective-permute-done.2.theirs_other_ref = bf16[320,640]{1,0:T(8,128)(2,1)S(1)} collective-permute-done((bf16[320,640]{1,0:T(8,128)(2,1)S(1)}, bf16[320,640]{1,0:T(8,128)(2,1)S(1)}, u32[]{:S(2)}, u32[]{:S(2)}) %collective-permute-start.2) | collective-permute-done | bytes 409632 | tf_op jit(solution)/shard_map/ppermute | solution.py:237
  49.8 3.9 %all-to-all-done.1.parts_ref = bf16[8,136,128]{2,1,0:T(8,128)(2,1)S(1)} async-done(((bf16[8,136,128]{2,1,0:T(8,128)(2,1)}), bf16[8,136,128]{2,1,0:T(8,128)(2,1)S(1)}, u32[]{:S(2)}, u32[]{:S(2)}) %all-to-all-start.1) | async-done | bytes 278560 | tf_op jit(solution)/shard_map/all_to_all | solution.py:271
  53.7 0.6 merge.1
  54.3 26.0 %all_to_all.20.rows_ref = bf16[16,64,256]{2,1,0:T(8,128)(2,1)S(1)} all-to-all(bf16[16,64,256]{2,1,0:T(8,128)(2,1)S(1)} %merge.1), channel_id=1, replica_groups=mesh['span'=4,'ring'=4,'core'=2,'far'=4,'side'=2,'part'=2] {'far','part'..., dimensions={0} | all-to-all | bytes 1048576 | tf_op jit(solution)/shard_map/all_to_all | solution.py:282
  80.3 0.8 project.1
  81.1 11.6 %all_to_all.21.parts_ref = bf16[8,120,128]{2,1,0:T(8,128)(2,1)S(1)} all-to-all(bf16[8,120,128]{2,1,0:T(8,128)(2,1)S(1)} %project.1), channel_id=1, replica_groups=mesh['span'=4,'ring'=4,'core'=2,'far'=4,'side'=2,'part'=2] {'side','ring'}, dimensions={0} | all-to-all | bytes 491520 | tf_op jit(solution)/shard_map/all_to_all | solution.py:291
  92.7 0.7 finish.1
  (1 shorter events, 0.0 us)
Async XLA Ops:
  0.0 27.1 %copy-start = (f32[50,320]{1,0:T(8,128)S(1)}, f32[50,320]{1,0:T(8,128)}, u32[]{:S(2)}) copy-start(f32[50,320]{1,0:T(8,128)} %param.11) | copy-start | bytes 192004
  1.9 16.7 %copy-start.1 = (bf16[640,320]{0,1:T(8,128)(2,1)S(1)}, bf16[640,320]{0,1:T(8,128)(2,1)}, u32[]{:S(2)}) copy-start(bf16[640,320]{0,1:T(8,128)(2,1)} %param.10) | copy-start | bytes 1228804
  1.9 37.9 %all-to-all-start = ((bf16[64,40,128]{2,1,0:T(8,128)(2,1)}), bf16[64,40,128]{2,1,0:T(8,128)(2,1)S(1)}, u32[]{:S(2)}, u32[]{:S(2)}) async-start(bf16[64,40,128]{2,1,0:T(8,128)(2,1)} %pack.1), calls=%async_computation | async-start | bytes 1310720 | tf_op jit(solution)/shard_map/all_to_all | solution.py:260
  18.6 23.0 %collective-permute-start = (bf16[320,640]{1,0:T(8,128)(2,1)S(1)}, bf16[320,640]{1,0:T(8,128)(2,1)S(1)}, u32[]{:S(2)}, u32[]{:S(2)}) collective-permute-start(bf16[320,640]{1,0:T(8,128)(2,1)S(1)} %bitcast.3), channel_id=1, source_target_pairs={{0,16},{16,0},{1,17},{17,1},{2,18},{18,2},{3,19},{19,3},{4,20},{20... | collective-permute-start | bytes 1228808 | tf_op jit(solution)/shard_map/ppermute | solution.py:237
  20.5 25.6 %collective-permute-start.1 = (bf16[320,640]{1,0:T(8,128)(2,1)S(1)}, bf16[320,640]{1,0:T(8,128)(2,1)S(1)}, u32[]{:S(2)}, u32[]{:S(2)}) collective-permute-start(bf16[320,640]{1,0:T(8,128)(2,1)S(1)} %bitcast.4), channel_id=1, source_target_pairs={{0,2},{2,0},{1,3},{3,1},{4,6},{6,4},{5,7},{7,5},{8,10},{10,8},{9,1... | collective-permute-start | bytes 1228808 | tf_op jit(solution)/shard_map/ppermute | solution.py:233
  23.9 0.7 copy-start.3
  27.1 12.6 %copy-start.2 = (s32[4]{0:T(128)S(1)}, s32[4]{0:T(128)}, u32[]{:S(2)}) copy-start(s32[4]{0:T(128)} %param.13) | copy-start | bytes 52
  41.6 12.1 %all-to-all-start.1 = ((bf16[8,136,128]{2,1,0:T(8,128)(2,1)}), bf16[8,136,128]{2,1,0:T(8,128)(2,1)S(1)}, u32[]{:S(2)}, u32[]{:S(2)}) async-start(bf16[8,136,128]{2,1,0:T(8,128)(2,1)} %attend.1), calls=%async_computation.1 | async-start | bytes 557056 | tf_op jit(solution)/shard_map/all_to_all | solution.py:271
  46.1 3.6 %collective-permute-start.2 = (bf16[320,640]{1,0:T(8,128)(2,1)S(1)}, bf16[320,640]{1,0:T(8,128)(2,1)S(1)}, u32[]{:S(2)}, u32[]{:S(2)}) collective-permute-start(bf16[320,640]{1,0:T(8,128)(2,1)S(1)} %collective-permute-done.1.theirs_ref), channel_id=1, source_target_pairs={{0,16},{16,0},{1,17},{17,1},{2,18},{18,2},{3,19},{19,3},{4,20},{20... | collective-permute-start | bytes 1228808 | tf_op jit(solution)/shard_map/ppermute | solution.py:237

commit v11 on v10

--- a/solution.py
+++ b/solution.py
@@ -33,10 +33,6 @@
     return pltpu.CompilerParams(vmem_limit_bytes=mib * 2**20)
 
 
-def spot(place):
-    return place % 2 * (PLACES // 2) + place // 2
-
-
 def pack_kernel(q_hbm, k_hbm, v_hbm, out_ref, q_ref, k_ref, v_ref, kv_ref, sems):
     copies = [
         pltpu.make_async_copy(source, target, sems.at[i])
@@ -46,14 +42,14 @@
         copy.start()
     for span in range(SPANS):
         for place in range(HEADS_HERE * BLOCKS, PLACES):
-            out_ref[span * PLACES + spot(place)] = jnp.zeros(out_ref.shape[1:], out_ref.dtype)
+            out_ref[place * SPANS + span] = jnp.zeros(out_ref.shape[1:], out_ref.dtype)
     copies[0].wait()
     for head in range(HEADS_HERE):
         cols = slice(head * HEAD_DIM, (head + 1) * HEAD_DIM)
         for block in range(BLOCKS):
             part = q_ref[block * QROWS : (block + 1) * QROWS, cols]
             for span in range(SPANS):
-                out_ref[span * PLACES + spot(head * BLOCKS + block), :QROWS, :] = part
+                out_ref[(head * BLOCKS + block) * SPANS + span, :QROWS, :] = part
     copies[1].wait()
     copies[2].wait()
     key_rows = k_ref[...].astype(jnp.float32)
@@ -66,7 +62,7 @@
         for head in range(HEADS_HERE):
             part = both[:, head * HEAD_DIM : (head + 1) * HEAD_DIM]
             for block in range(BLOCKS):
-                out_ref[span * PLACES + spot(head * BLOCKS + block), QROWS:, :] = part
+                out_ref[(head * BLOCKS + block) * SPANS + span, QROWS:, :] = part
 
 
 def split_three(x):
@@ -88,7 +84,7 @@
         span = jnp.minimum(span, SPANS - 1)
         spans.append(span)
         for place in range(PLACES):
-            both = rows_ref[span * PLACES + place, QROWS:, :].astype(jnp.float32)
+            both = rows_ref[place * SPANS + span, QROWS:, :].astype(jnp.float32)
             target = turn * KBLOCK + place * KROWS
             keys_ref[target : target + KROWS, :] = both[:KROWS]
             values_ref[target : target + KROWS, :] = both[KROWS:]
@@ -98,7 +94,7 @@
     for turn, span in enumerate(spans):
         seen = (turn + 1) * KBLOCK
         own = jnp.concatenate(
-            [rows_ref[span * PLACES + spot(place), :QROWS, :] for place in range(PLACES)], axis=0
+            [rows_ref[place * SPANS + span, :QROWS, :] for place in range(PLACES)], axis=0
         )
         scores = lax.dot_general(
             keys[:seen], own, (((1,), (1,)), ((), ())), preferred_element_type=jnp.float32
@@ -257,7 +253,7 @@
     packed, weight = lax.optimization_barrier((packed, out_weight.T))
     theirs, other = swap_sides(weight), swap_cores(weight)
     theirs_other = swap_cores(theirs)
-    rows = lax.all_to_all(packed, ("span", "part", "far", "side"), 0, 0, tiled=True)
+    rows = lax.all_to_all(packed, SEQ + ("span",), 0, 0, tiled=True)
     parts = pl.pallas_call(
         attend_kernel,
         out_shape=jax.ShapeDtypeStruct((SPANS * CORES, RING * CHUNK + STATS, HEAD_DIM), jnp.bfloat16),

time: 94 us -> 94.4 us (level)
  no operation moved by 1% of the time
where the time goes in v11:
time: 94.4 us; the launch traced here: 93.9 us
  blocking collectives  37.5 us (40%)
  starting transfers between devices  28.8 us (31%)
  waiting for transfers between devices  18.4 us (19%)
  Pallas kernels  5.88 us (6%)
  between operations  2.05 us (2%)
  local copies, waits for them, and re-layouts  1.26 us (1%)
    all_to_all x1, blocking collectives, shards(): merged = lax.all_to_all(merged, ('far', 'part', 'side'), 0, 0, tiled=True)  25.9 us
    all_to_all x1, starting transfers between devices, shards(): rows = lax.all_to_all(packed, SEQ + ('span',), 0, 0, tiled=True)  16.6 us
    all_to_all x1, waiting for transfers between devices, shards(): rows = lax.all_to_all(packed, SEQ + ('span',), 0, 0, tiled=True)  12.9 us
    all_to_all x1, blocking collectives, shards(): sums = lax.all_to_all(sums, ('side', 'ring'), 0, 0, tiled=True)  11.6 us
    all_to_all x1, starting transfers between devices, shards(): parts = lax.all_to_all(parts, ('core', 'span'), 0, 0, tiled=True)  4.84 us
    ppermute x2, starting transfers between devices, swap_cores(): return lax.ppermute(x, 'core', [(0, 1), (1, 0)])  3.97 us
    all_to_all x1, waiting for transfers between devices, shards(): parts = lax.all_to_all(parts, ('core', 'span'), 0, 0, tiled=True)  3.9 us
    ppermute x1, starting transfers between devices, swap_sides(): return lax.ppermute(x, 'side', [(0, 1), (1, 0)])  3.38 us
  transfers between devices with their start and end apart: 5, of which 3 were waited for; matrix products, arithmetic and copies ran while one was open for 1% of the time, Pallas kernels for 2%

profile of v11, /device:TPU:16, one launch (start us, length us, event | category | flops | bytes accessed | tf_op | source)
XLA Modules:
  0.0 93.9 jit_solution(4915847663162034761)
XLA Ops:
  0.0 0.0 copy-start
  0.0 1.8 %pack.1 = bf16[64,40,128]{2,1,0:T(8,128)(2,1)} custom-call(bf16[48,640]{1,0:T(8,128)(2,1)} %q_hbm.1, bf16[48,640]{1,0:T(8,128)(2,1)} %k_hbm.1, bf16[48,640]{1,0:T(8,128)(2,1)} %v_hbm.1), custom_call_target="tpu_custom_call" | custom-call | tf_op jit(solution)/shard_map/pack/pallas_call | solution.py:238
  1.9 0.0 copy-start.1
  1.9 16.6 %all-to-all-start = ((bf16[64,40,128]{2,1,0:T(8,128)(2,1)}), bf16[64,40,128]{2,1,0:T(8,128)(2,1)S(1)}, u32[]{:S(2)}, u32[]{:S(2)}) async-start(bf16[64,40,128]{2,1,0:T(8,128)(2,1)} %pack.1), calls=%async_computation | async-start | bytes 1310720 | tf_op jit(solution)/shard_map/all_to_all | solution.py:256
  18.5 0.0 copy-done.1
  18.5 1.9 %collective-permute-start = (bf16[320,640]{1,0:T(8,128)(2,1)S(1)}, bf16[320,640]{1,0:T(8,128)(2,1)S(1)}, u32[]{:S(2)}, u32[]{:S(2)}) collective-permute-start(bf16[320,640]{1,0:T(8,128)(2,1)S(1)} %bitcast.3), channel_id=1, source_target_pairs={{0,16},{16,0},{1,17},{17,1},{2,18},{18,2},{3,19},{19,3},{4,20},{20... | collective-permute-start | bytes 1228808 | tf_op jit(solution)/shard_map/ppermute | solution.py:233
  20.4 3.4 %collective-permute-start.1 = (bf16[320,640]{1,0:T(8,128)(2,1)S(1)}, bf16[320,640]{1,0:T(8,128)(2,1)S(1)}, u32[]{:S(2)}, u32[]{:S(2)}) collective-permute-start(bf16[320,640]{1,0:T(8,128)(2,1)S(1)} %bitcast.4), channel_id=1, source_target_pairs={{0,2},{2,0},{1,3},{3,1},{4,6},{6,4},{5,7},{7,5},{8,10},{10,8},{9,1... | collective-permute-start | bytes 1228808 | tf_op jit(solution)/shard_map/ppermute | solution.py:229
  23.8 0.0 copy-start.3
  23.8 0.6 copy-done.3
  24.5 0.6 dynamic_slice.7
  27.0 0.0 copy-done
  27.0 0.0 copy-start.2
  27.0 12.9 %all-to-all-done.rows_ref = bf16[64,40,128]{2,1,0:T(8,128)(2,1)S(1)} async-done(((bf16[64,40,128]{2,1,0:T(8,128)(2,1)}), bf16[64,40,128]{2,1,0:T(8,128)(2,1)S(1)}, u32[]{:S(2)}, u32[]{:S(2)}) %all-to-all-start) | async-done | bytes 655392 | tf_op jit(solution)/shard_map/all_to_all | solution.py:256
  40.0 0.0 copy-done.2
  40.0 1.8 %attend.1 = bf16[8,136,128]{2,1,0:T(8,128)(2,1)} custom-call(s32[1,4]{1,0:T(1,128)S(1)} %bitcast.6, bf16[64,40,128]{2,1,0:T(8,128)(2,1)S(1)} %all-to-all-done.rows_ref), custom_call_target="tpu_custom_call" | custom-call | tf_op jit(solution)/shard_map/attend/pallas_call | solution.py:257
  41.8 0.0 collective-permute-done.other_ref
  41.8 4.8 %all-to-all-start.1 = ((bf16[8,136,128]{2,1,0:T(8,128)(2,1)}), bf16[8,136,128]{2,1,0:T(8,128)(2,1)S(1)}, u32[]{:S(2)}, u32[]{:S(2)}) async-start(bf16[8,136,128]{2,1,0:T(8,128)(2,1)} %attend.1), calls=%async_computation.1 | async-start | bytes 557056 | tf_op jit(solution)/shard_map/all_to_all | solution.py:267
  46.6 0.0 collective-permute-done.1.theirs_ref
  46.6 2.0 %collective-permute-start.2 = (bf16[320,640]{1,0:T(8,128)(2,1)S(1)}, bf16[320,640]{1,0:T(8,128)(2,1)S(1)}, u32[]{:S(2)}, u32[]{:S(2)}) collective-permute-start(bf16[320,640]{1,0:T(8,128)(2,1)S(1)} %collective-permute-done.1.theirs_ref), channel_id=1, source_target_pairs={{0,16},{16,0},{1,17},{17,1},{2,18},{18,2},{3,19},{19,3},{4,20},{20... | collective-permute-start | bytes 1228808 | tf_op jit(solution)/shard_map/ppermute | solution.py:233
  48.7 1.6 %collective-permute-done.2.theirs_other_ref = bf16[320,640]{1,0:T(8,128)(2,1)S(1)} collective-permute-done((bf16[320,640]{1,0:T(8,128)(2,1)S(1)}, bf16[320,640]{1,0:T(8,128)(2,1)S(1)}, u32[]{:S(2)}, u32[]{:S(2)}) %collective-permute-start.2) | collective-permute-done | bytes 409632 | tf_op jit(solution)/shard_map/ppermute | solution.py:233
  50.3 3.9 %all-to-all-done.1.parts_ref = bf16[8,136,128]{2,1,0:T(8,128)(2,1)S(1)} async-done(((bf16[8,136,128]{2,1,0:T(8,128)(2,1)}), bf16[8,136,128]{2,1,0:T(8,128)(2,1)S(1)}, u32[]{:S(2)}, u32[]{:S(2)}) %all-to-all-start.1) | async-done | bytes 278560 | tf_op jit(solution)/shard_map/all_to_all | solution.py:267
  54.2 0.6 merge.1
  54.8 25.9 %all_to_all.20.rows_ref = bf16[16,64,256]{2,1,0:T(8,128)(2,1)S(1)} all-to-all(bf16[16,64,256]{2,1,0:T(8,128)(2,1)S(1)} %merge.1), channel_id=1, replica_groups=mesh['span'=4,'ring'=4,'core'=2,'far'=4,'side'=2,'part'=2] {'far','part'..., dimensions={0} | all-to-all | bytes 1048576 | tf_op jit(solution)/shard_map/all_to_all | solution.py:278
  80.7 0.8 project.1
  81.6 11.6 %all_to_all.21.parts_ref = bf16[8,120,128]{2,1,0:T(8,128)(2,1)S(1)} all-to-all(bf16[8,120,128]{2,1,0:T(8,128)(2,1)S(1)} %project.1), channel_id=1, replica_groups=mesh['span'=4,'ring'=4,'core'=2,'far'=4,'side'=2,'part'=2] {'side','ring'}, dimensions={0} | all-to-all | bytes 491520 | tf_op jit(solution)/shard_map/all_to_all | solution.py:287
  93.1 0.7 finish.1
  (1 shorter events, 0.0 us)
Async XLA Ops:
  0.0 27.0 %copy-start = (f32[50,320]{1,0:T(8,128)S(1)}, f32[50,320]{1,0:T(8,128)}, u32[]{:S(2)}) copy-start(f32[50,320]{1,0:T(8,128)} %param.11) | copy-start | bytes 192004
  1.9 16.6 %copy-start.1 = (bf16[640,320]{0,1:T(8,128)(2,1)S(1)}, bf16[640,320]{0,1:T(8,128)(2,1)}, u32[]{:S(2)}) copy-start(bf16[640,320]{0,1:T(8,128)(2,1)} %param.10) | copy-start | bytes 1228804
  1.9 38.1 %all-to-all-start = ((bf16[64,40,128]{2,1,0:T(8,128)(2,1)}), bf16[64,40,128]{2,1,0:T(8,128)(2,1)S(1)}, u32[]{:S(2)}, u32[]{:S(2)}) async-start(bf16[64,40,128]{2,1,0:T(8,128)(2,1)} %pack.1), calls=%async_computation | async-start | bytes 1310720 | tf_op jit(solution)/shard_map/all_to_all | solution.py:256
  18.5 23.3 %collective-permute-start = (bf16[320,640]{1,0:T(8,128)(2,1)S(1)}, bf16[320,640]{1,0:T(8,128)(2,1)S(1)}, u32[]{:S(2)}, u32[]{:S(2)}) collective-permute-start(bf16[320,640]{1,0:T(8,128)(2,1)S(1)} %bitcast.3), channel_id=1, source_target_pairs={{0,16},{16,0},{1,17},{17,1},{2,18},{18,2},{3,19},{19,3},{4,20},{20... | collective-permute-start | bytes 1228808 | tf_op jit(solution)/shard_map/ppermute | solution.py:233
  20.4 26.2 %collective-permute-start.1 = (bf16[320,640]{1,0:T(8,128)(2,1)S(1)}, bf16[320,640]{1,0:T(8,128)(2,1)S(1)}, u32[]{:S(2)}, u32[]{:S(2)}) collective-permute-start(bf16[320,640]{1,0:T(8,128)(2,1)S(1)} %bitcast.4), channel_id=1, source_target_pairs={{0,2},{2,0},{1,3},{3,1},{4,6},{6,4},{5,7},{7,5},{8,10},{10,8},{9,1... | collective-permute-start | bytes 1228808 | tf_op jit(solution)/shard_map/ppermute | solution.py:229
  23.8 0.7 copy-start.3
  27.0 12.9 %copy-start.2 = (s32[4]{0:T(128)S(1)}, s32[4]{0:T(128)}, u32[]{:S(2)}) copy-start(s32[4]{0:T(128)} %param.13) | copy-start | bytes 52
  41.8 12.4 %all-to-all-start.1 = ((bf16[8,136,128]{2,1,0:T(8,128)(2,1)}), bf16[8,136,128]{2,1,0:T(8,128)(2,1)S(1)}, u32[]{:S(2)}, u32[]{:S(2)}) async-start(bf16[8,136,128]{2,1,0:T(8,128)(2,1)} %attend.1), calls=%async_computation.1 | async-start | bytes 557056 | tf_op jit(solution)/shard_map/all_to_all | solution.py:267
  46.6 3.6 %collective-permute-start.2 = (bf16[320,640]{1,0:T(8,128)(2,1)S(1)}, bf16[320,640]{1,0:T(8,128)(2,1)S(1)}, u32[]{:S(2)}, u32[]{:S(2)}) collective-permute-start(bf16[320,640]{1,0:T(8,128)(2,1)S(1)} %collective-permute-done.1.theirs_ref), channel_id=1, source_target_pairs={{0,16},{16,0},{1,17},{17,1},{2,18},{18,2},{3,19},{19,3},{4,20},{20... | collective-permute-start | bytes 1228808 | tf_op jit(solution)/shard_map/ppermute | solution.py:233

commit v12 on v10

--- a/solution.py
+++ b/solution.py
@@ -125,10 +125,10 @@
         for core in range(CORES):
             for ring in range(RING):
                 source = (ring * CORES + core) * CHUNK
-                out_ref[core * SPANS + span, ring * CHUNK : (ring + 1) * CHUNK, :] = mixed[
+                out_ref[span * CORES + core, ring * CHUNK : (ring + 1) * CHUNK, :] = mixed[
                     source : source + CHUNK
                 ]
-            out_ref[core * SPANS + span, RING * CHUNK :, :] = stat.astype(jnp.bfloat16)
+            out_ref[span * CORES + core, RING * CHUNK :, :] = stat.astype(jnp.bfloat16)
 
 
 def berth(place):
@@ -142,7 +142,7 @@
     for half in range(2):
         for slot in slots:
             for s in range(SPANS):
-                stats = parts_ref[slot * SPANS + s, RING * CHUNK :, :].astype(jnp.float32)
+                stats = parts_ref[s * CORES + slot, RING * CHUNK :, :].astype(jnp.float32)
                 first = 3 * half
                 rows.append(stats[first : first + 1] + stats[first + 1 : first + 2] + stats[first + 2 : first + 3])
     pad = jnp.zeros((HEAD_DIM - len(rows), HEAD_DIM), jnp.float32)
@@ -159,7 +159,7 @@
             total = functools.reduce(jnp.add, shares)
             mixed = jnp.zeros((CHUNK, HEAD_DIM), jnp.float32)
             for s in range(SPANS):
-                part = parts_ref[slot * SPANS + s, ring * CHUNK : (ring + 1) * CHUNK, :]
+                part = parts_ref[s * CORES + slot, ring * CHUNK : (ring + 1) * CHUNK, :]
                 mixed = mixed + part.astype(jnp.float32) * (shares[s] / total)
             mixed = mixed.astype(jnp.bfloat16)
             lanes = slice(i * HEAD_DIM, (i + 1) * HEAD_DIM)
@@ -268,7 +268,7 @@
         name="attend",
     )(span_order.reshape(1, SPANS), rows)
     parts, other, gate_row = lax.optimization_barrier((parts, other, gate_row))
-    parts = lax.all_to_all(parts, ("core", "span"), 0, 0, tiled=True)
+    parts = lax.all_to_all(parts, ("span", "core"), 0, 0, tiled=True)
     parts, theirs, theirs_other = lax.optimization_barrier((parts, theirs, theirs_other))
     merged = pl.pallas_call(
         merge_kernel,

time: 94 us -> 94.2 us (level)
  the two profiles are of different devices: /device:TPU:16 before, /device:TPU:8 now
where the time goes in v12:
time: 94.2 us; the launch traced here: 93.7 us
  blocking collectives  37.1 us (39%)
  starting transfers between devices  28.1 us (30%)
  waiting for transfers between devices  19.3 us (20%)
  Pallas kernels  5.86 us (6%)
  between operations  2.05 us (2%)
  local copies, waits for them, and re-layouts  1.26 us (1%)
    all_to_all x1, blocking collectives, shards(): merged = lax.all_to_all(merged, ('far', 'part', 'side'), 0, 0, tiled=True)  25.2 us
    all_to_all x1, starting transfers between devices, shards(): lax.all_to_all(packed, ('span', 'part', 'far', 'side'), 0, 0, tiled=True)  16.7 us
    all_to_all x1, waiting for transfers between devices, shards(): lax.all_to_all(packed, ('span', 'part', 'far', 'side'), 0, 0, tiled=True)  13.2 us
    all_to_all x1, blocking collectives, shards(): sums = lax.all_to_all(sums, ('side', 'ring'), 0, 0, tiled=True)  11.9 us
    all_to_all x1, waiting for transfers between devices, shards(): parts = lax.all_to_all(parts, ('span', 'core'), 0, 0, tiled=True)  4.52 us
    all_to_all x1, starting transfers between devices, shards(): parts = lax.all_to_all(parts, ('span', 'core'), 0, 0, tiled=True)  4.07 us
    ppermute x2, starting transfers between devices, swap_cores(): return lax.ppermute(x, 'core', [(0, 1), (1, 0)])  3.97 us
    ppermute x1, starting transfers between devices, swap_sides(): return lax.ppermute(x, 'side', [(0, 1), (1, 0)])  3.37 us
  transfers between devices with their start and end apart: 5, of which 3 were waited for; matrix products, arithmetic and copies ran while one was open for 1% of the time, Pallas kernels for 2%

profile of v12, /device:TPU:8, one launch (start us, length us, event | category | flops | bytes accessed | tf_op | source)
XLA Modules:
  0.0 93.7 jit_solution(17791365850426271422)
XLA Ops:
  0.0 0.0 copy-start
  0.0 1.8 %pack.1 = bf16[64,40,128]{2,1,0:T(8,128)(2,1)} custom-call(bf16[48,640]{1,0:T(8,128)(2,1)} %q_hbm.1, bf16[48,640]{1,0:T(8,128)(2,1)} %k_hbm.1, bf16[48,640]{1,0:T(8,128)(2,1)} %v_hbm.1), custom_call_target="tpu_custom_call" | custom-call | tf_op jit(solution)/shard_map/pack/pallas_call | solution.py:242
  1.9 0.0 copy-start.1
  1.9 16.7 %all-to-all-start = ((bf16[64,40,128]{2,1,0:T(8,128)(2,1)}), bf16[64,40,128]{2,1,0:T(8,128)(2,1)S(1)}, u32[]{:S(2)}, u32[]{:S(2)}) async-start(bf16[64,40,128]{2,1,0:T(8,128)(2,1)} %pack.1), calls=%async_computation | async-start | bytes 1310720 | tf_op jit(solution)/shard_map/all_to_all | solution.py:260
  18.6 0.0 copy-done.1
  18.6 1.9 %collective-permute-start = (bf16[320,640]{1,0:T(8,128)(2,1)S(1)}, bf16[320,640]{1,0:T(8,128)(2,1)S(1)}, u32[]{:S(2)}, u32[]{:S(2)}) collective-permute-start(bf16[320,640]{1,0:T(8,128)(2,1)S(1)} %bitcast.3), channel_id=1, source_target_pairs={{0,16},{16,0},{1,17},{17,1},{2,18},{18,2},{3,19},{19,3},{4,20},{20... | collective-permute-start | bytes 1228808 | tf_op jit(solution)/shard_map/ppermute | solution.py:237
  20.5 3.4 %collective-permute-start.1 = (bf16[320,640]{1,0:T(8,128)(2,1)S(1)}, bf16[320,640]{1,0:T(8,128)(2,1)S(1)}, u32[]{:S(2)}, u32[]{:S(2)}) collective-permute-start(bf16[320,640]{1,0:T(8,128)(2,1)S(1)} %bitcast.4), channel_id=1, source_target_pairs={{0,2},{2,0},{1,3},{3,1},{4,6},{6,4},{5,7},{7,5},{8,10},{10,8},{9,1... | collective-permute-start | bytes 1228808 | tf_op jit(solution)/shard_map/ppermute | solution.py:233
  23.9 0.0 copy-start.3
  23.9 0.6 copy-done.3
  24.6 0.6 dynamic_slice.7
  27.1 0.0 copy-done
  27.1 0.0 copy-start.2
  27.2 13.2 %all-to-all-done.rows_ref = bf16[64,40,128]{2,1,0:T(8,128)(2,1)S(1)} async-done(((bf16[64,40,128]{2,1,0:T(8,128)(2,1)}), bf16[64,40,128]{2,1,0:T(8,128)(2,1)S(1)}, u32[]{:S(2)}, u32[]{:S(2)}) %all-to-all-start) | async-done | bytes 655392 | tf_op jit(solution)/shard_map/all_to_all | solution.py:260
  40.4 0.0 copy-done.2
  40.4 1.8 %attend.1 = bf16[8,136,128]{2,1,0:T(8,128)(2,1)} custom-call(s32[1,4]{1,0:T(1,128)S(1)} %bitcast.6, bf16[64,40,128]{2,1,0:T(8,128)(2,1)S(1)} %all-to-all-done.rows_ref), custom_call_target="tpu_custom_call" | custom-call | tf_op jit(solution)/shard_map/attend/pallas_call | solution.py:261
  42.2 0.0 collective-permute-done.other_ref
  42.2 4.1 %all-to-all-start.1 = ((bf16[8,136,128]{2,1,0:T(8,128)(2,1)}), bf16[8,136,128]{2,1,0:T(8,128)(2,1)S(1)}, u32[]{:S(2)}, u32[]{:S(2)}) async-start(bf16[8,136,128]{2,1,0:T(8,128)(2,1)} %attend.1), calls=%async_computation.1 | async-start | bytes 557056 | tf_op jit(solution)/shard_map/all_to_all | solution.py:271
  46.2 0.0 collective-permute-done.1.theirs_ref
  46.2 2.0 %collective-permute-start.2 = (bf16[320,640]{1,0:T(8,128)(2,1)S(1)}, bf16[320,640]{1,0:T(8,128)(2,1)S(1)}, u32[]{:S(2)}, u32[]{:S(2)}) collective-permute-start(bf16[320,640]{1,0:T(8,128)(2,1)S(1)} %collective-permute-done.1.theirs_ref), channel_id=1, source_target_pairs={{0,16},{16,0},{1,17},{17,1},{2,18},{18,2},{3,19},{19,3},{4,20},{20... | collective-permute-start | bytes 1228808 | tf_op jit(solution)/shard_map/ppermute | solution.py:237
  48.3 1.6 %collective-permute-done.2.theirs_other_ref = bf16[320,640]{1,0:T(8,128)(2,1)S(1)} collective-permute-done((bf16[320,640]{1,0:T(8,128)(2,1)S(1)}, bf16[320,640]{1,0:T(8,128)(2,1)S(1)}, u32[]{:S(2)}, u32[]{:S(2)}) %collective-permute-start.2) | collective-permute-done | bytes 409632 | tf_op jit(solution)/shard_map/ppermute | solution.py:237
  49.9 4.5 %all-to-all-done.1.parts_ref = bf16[8,136,128]{2,1,0:T(8,128)(2,1)S(1)} async-done(((bf16[8,136,128]{2,1,0:T(8,128)(2,1)}), bf16[8,136,128]{2,1,0:T(8,128)(2,1)S(1)}, u32[]{:S(2)}, u32[]{:S(2)}) %all-to-all-start.1) | async-done | bytes 278560 | tf_op jit(solution)/shard_map/all_to_all | solution.py:271
  54.4 0.6 merge.1
  55.0 25.2 %all_to_all.20.rows_ref = bf16[16,64,256]{2,1,0:T(8,128)(2,1)S(1)} all-to-all(bf16[16,64,256]{2,1,0:T(8,128)(2,1)S(1)} %merge.1), channel_id=1, replica_groups=mesh['span'=4,'ring'=4,'core'=2,'far'=4,'side'=2,'part'=2] {'far','part'..., dimensions={0} | all-to-all | bytes 1048576 | tf_op jit(solution)/shard_map/all_to_all | solution.py:282
  80.2 0.8 project.1
  81.0 11.9 %all_to_all.21.parts_ref = bf16[8,120,128]{2,1,0:T(8,128)(2,1)S(1)} all-to-all(bf16[8,120,128]{2,1,0:T(8,128)(2,1)S(1)} %project.1), channel_id=1, replica_groups=mesh['span'=4,'ring'=4,'core'=2,'far'=4,'side'=2,'part'=2] {'side','ring'}, dimensions={0} | all-to-all | bytes 491520 | tf_op jit(solution)/shard_map/all_to_all | solution.py:291
  92.9 0.7 finish.1
  (1 shorter events, 0.0 us)
Async XLA Ops:
  0.0 27.1 %copy-start = (f32[50,320]{1,0:T(8,128)S(1)}, f32[50,320]{1,0:T(8,128)}, u32[]{:S(2)}) copy-start(f32[50,320]{1,0:T(8,128)} %param.11) | copy-start | bytes 192004
  1.9 16.8 %copy-start.1 = (bf16[640,320]{0,1:T(8,128)(2,1)S(1)}, bf16[640,320]{0,1:T(8,128)(2,1)}, u32[]{:S(2)}) copy-start(bf16[640,320]{0,1:T(8,128)(2,1)} %param.10) | copy-start | bytes 1228804
  1.9 38.5 %all-to-all-start = ((bf16[64,40,128]{2,1,0:T(8,128)(2,1)}), bf16[64,40,128]{2,1,0:T(8,128)(2,1)S(1)}, u32[]{:S(2)}, u32[]{:S(2)}) async-start(bf16[64,40,128]{2,1,0:T(8,128)(2,1)} %pack.1), calls=%async_computation | async-start | bytes 1310720 | tf_op jit(solution)/shard_map/all_to_all | solution.py:260
  18.6 23.5 %collective-permute-start = (bf16[320,640]{1,0:T(8,128)(2,1)S(1)}, bf16[320,640]{1,0:T(8,128)(2,1)S(1)}, u32[]{:S(2)}, u32[]{:S(2)}) collective-permute-start(bf16[320,640]{1,0:T(8,128)(2,1)S(1)} %bitcast.3), channel_id=1, source_target_pairs={{0,16},{16,0},{1,17},{17,1},{2,18},{18,2},{3,19},{19,3},{4,20},{20... | collective-permute-start | bytes 1228808 | tf_op jit(solution)/shard_map/ppermute | solution.py:237
  20.5 25.7 %collective-permute-start.1 = (bf16[320,640]{1,0:T(8,128)(2,1)S(1)}, bf16[320,640]{1,0:T(8,128)(2,1)S(1)}, u32[]{:S(2)}, u32[]{:S(2)}) collective-permute-start(bf16[320,640]{1,0:T(8,128)(2,1)S(1)} %bitcast.4), channel_id=1, source_target_pairs={{0,2},{2,0},{1,3},{3,1},{4,6},{6,4},{5,7},{7,5},{8,10},{10,8},{9,1... | collective-permute-start | bytes 1228808 | tf_op jit(solution)/shard_map/ppermute | solution.py:233
  23.9 0.7 copy-start.3
  27.1 13.2 %copy-start.2 = (s32[4]{0:T(128)S(1)}, s32[4]{0:T(128)}, u32[]{:S(2)}) copy-start(s32[4]{0:T(128)} %param.13) | copy-start | bytes 52
  42.2 12.2 %all-to-all-start.1 = ((bf16[8,136,128]{2,1,0:T(8,128)(2,1)}), bf16[8,136,128]{2,1,0:T(8,128)(2,1)S(1)}, u32[]{:S(2)}, u32[]{:S(2)}) async-start(bf16[8,136,128]{2,1,0:T(8,128)(2,1)} %attend.1), calls=%async_computation.1 | async-start | bytes 557056 | tf_op jit(solution)/shard_map/all_to_all | solution.py:271
  46.2 3.6 %collective-permute-start.2 = (bf16[320,640]{1,0:T(8,128)(2,1)S(1)}, bf16[320,640]{1,0:T(8,128)(2,1)S(1)}, u32[]{:S(2)}, u32[]{:S(2)}) collective-permute-start(bf16[320,640]{1,0:T(8,128)(2,1)S(1)} %collective-permute-done.1.theirs_ref), channel_id=1, source_target_pairs={{0,16},{16,0},{1,17},{17,1},{2,18},{18,2},{3,19},{19,3},{4,20},{20... | collective-permute-start | bytes 1228808 | tf_op jit(solution)/shard_map/ppermute | solution.py:237

commit v13 on v10

--- a/solution.py
+++ b/solution.py
@@ -77,7 +77,7 @@
     return high, middle, low
 
 
-def attend_kernel(order_ref, rows_ref, out_ref, keys_ref, values_ref):
+def attend_kernel(order_ref, rows_ref, out_hbm, keys_ref, values_ref, out_ref, sems):
     line = order_ref[...]
     order = [line[0, i] for i in range(SPANS)]
     spans = []
@@ -94,7 +94,7 @@
             values_ref[target : target + KROWS, :] = both[KROWS:]
     keys = keys_ref[...].astype(jnp.bfloat16)
     values = values_ref[...].astype(jnp.bfloat16)
-    state = []
+    state, copies = [], []
     for turn, span in enumerate(spans):
         seen = (turn + 1) * KBLOCK
         own = jnp.concatenate(
@@ -125,10 +125,20 @@
         for core in range(CORES):
             for ring in range(RING):
                 source = (ring * CORES + core) * CHUNK
-                out_ref[core * SPANS + span, ring * CHUNK : (ring + 1) * CHUNK, :] = mixed[
+                out_ref[turn * CORES + core, ring * CHUNK : (ring + 1) * CHUNK, :] = mixed[
                     source : source + CHUNK
                 ]
-            out_ref[core * SPANS + span, RING * CHUNK :, :] = stat.astype(jnp.bfloat16)
+            out_ref[turn * CORES + core, RING * CHUNK :, :] = stat.astype(jnp.bfloat16)
+            copies.append(
+                pltpu.make_async_copy(
+                    out_ref.at[turn * CORES + core],
+                    out_hbm.at[core * SPANS + span],
+                    sems.at[turn * CORES + core],
+                )
+            )
+            copies[-1].start()
+    for copy in copies:
+        copy.wait()
 
 
 def berth(place):
@@ -262,8 +272,12 @@
         attend_kernel,
         out_shape=jax.ShapeDtypeStruct((SPANS * CORES, RING * CHUNK + STATS, HEAD_DIM), jnp.bfloat16),
         in_specs=[VMEM, VMEM],
-        out_specs=VMEM,
-        scratch_shapes=[pltpu.VMEM((SPANS * KBLOCK, HEAD_DIM), jnp.float32)] * 2,
+        out_specs=HBM,
+        scratch_shapes=[pltpu.VMEM((SPANS * KBLOCK, HEAD_DIM), jnp.float32)] * 2
+        + [
+            pltpu.VMEM((SPANS * CORES, RING * CHUNK + STATS, HEAD_DIM), jnp.bfloat16),
+            pltpu.SemaphoreType.DMA((SPANS * CORES,)),
+        ],
         compiler_params=params(),
         name="attend",
     )(span_order.reshape(1, SPANS), rows)

time: 94 us -> 94 us (level)
  no operation moved by 1% of the time
where the time goes in v13:
time: 94 us; the launch traced here: 93.4 us
  blocking collectives  37.5 us (40%)
  starting transfers between devices  28.6 us (30%)
  waiting for transfers between devices  18.1 us (19%)
  Pallas kernels  5.83 us (6%)
  between operations  2.07 us (2%)
  local copies, waits for them, and re-layouts  1.26 us (1%)
    all_to_all x1, blocking collectives, shards(): merged = lax.all_to_all(merged, ('far', 'part', 'side'), 0, 0, tiled=True)  26 us
    all_to_all x1, starting transfers between devices, shards(): lax.all_to_all(packed, ('span', 'part', 'far', 'side'), 0, 0, tiled=True)  16.7 us
    all_to_all x1, waiting for transfers between devices, shards(): lax.all_to_all(packed, ('span', 'part', 'far', 'side'), 0, 0, tiled=True)  12.6 us
    all_to_all x1, blocking collectives, shards(): sums = lax.all_to_all(sums, ('side', 'ring'), 0, 0, tiled=True)  11.6 us
    all_to_all x1, starting transfers between devices, shards(): parts = lax.all_to_all(parts, ('core', 'span'), 0, 0, tiled=True)  4.57 us
    ppermute x2, starting transfers between devices, swap_cores(): return lax.ppermute(x, 'core', [(0, 1), (1, 0)])  3.97 us
    all_to_all x1, waiting for transfers between devices, shards(): parts = lax.all_to_all(parts, ('core', 'span'), 0, 0, tiled=True)  3.9 us
    ppermute x1, starting transfers between devices, swap_sides(): return lax.ppermute(x, 'side', [(0, 1), (1, 0)])  3.38 us
  transfers between devices with their start and end apart: 5, of which 3 were waited for; matrix products, arithmetic and copies ran while one was open for 1% of the time, Pallas kernels for 2%

profile of v13, /device:TPU:16, one launch (start us, length us, event | category | flops | bytes accessed | tf_op | source)
XLA Modules:
  0.0 93.4 jit_solution(2365082483711043405)
XLA Ops:
  0.0 0.0 copy-start
  0.0 1.8 %pack.1 = bf16[64,40,128]{2,1,0:T(8,128)(2,1)} custom-call(bf16[48,640]{1,0:T(8,128)(2,1)} %q_hbm.1, bf16[48,640]{1,0:T(8,128)(2,1)} %k_hbm.1, bf16[48,640]{1,0:T(8,128)(2,1)} %v_hbm.1), custom_call_target="tpu_custom_call" | custom-call | tf_op jit(solution)/shard_map/pack/pallas_call | solution.py:252
  1.9 0.0 copy-start.1
  1.9 16.7 %all-to-all-start = ((bf16[64,40,128]{2,1,0:T(8,128)(2,1)}), bf16[64,40,128]{2,1,0:T(8,128)(2,1)S(1)}, u32[]{:S(2)}, u32[]{:S(2)}) async-start(bf16[64,40,128]{2,1,0:T(8,128)(2,1)} %pack.1), calls=%async_computation | async-start | bytes 1310720 | tf_op jit(solution)/shard_map/all_to_all | solution.py:270
  18.6 0.0 copy-done.1
  18.6 1.9 %collective-permute-start = (bf16[320,640]{1,0:T(8,128)(2,1)S(1)}, bf16[320,640]{1,0:T(8,128)(2,1)S(1)}, u32[]{:S(2)}, u32[]{:S(2)}) collective-permute-start(bf16[320,640]{1,0:T(8,128)(2,1)S(1)} %bitcast.3), channel_id=1, source_target_pairs={{0,16},{16,0},{1,17},{17,1},{2,18},{18,2},{3,19},{19,3},{4,20},{20... | collective-permute-start | bytes 1228808 | tf_op jit(solution)/shard_map/ppermute | solution.py:247
  20.5 3.4 %collective-permute-start.1 = (bf16[320,640]{1,0:T(8,128)(2,1)S(1)}, bf16[320,640]{1,0:T(8,128)(2,1)S(1)}, u32[]{:S(2)}, u32[]{:S(2)}) collective-permute-start(bf16[320,640]{1,0:T(8,128)(2,1)S(1)} %bitcast.4), channel_id=1, source_target_pairs={{0,2},{2,0},{1,3},{3,1},{4,6},{6,4},{5,7},{7,5},{8,10},{10,8},{9,1... | collective-permute-start | bytes 1228808 | tf_op jit(solution)/shard_map/ppermute | solution.py:243
  23.9 0.0 copy-start.3
  23.9 0.6 copy-done.3
  24.6 0.6 dynamic_slice.7
  27.1 0.0 copy-done
  27.1 0.0 copy-start.2
  27.1 12.6 %all-to-all-done.rows_ref = bf16[64,40,128]{2,1,0:T(8,128)(2,1)S(1)} async-done(((bf16[64,40,128]{2,1,0:T(8,128)(2,1)}), bf16[64,40,128]{2,1,0:T(8,128)(2,1)S(1)}, u32[]{:S(2)}, u32[]{:S(2)}) %all-to-all-start) | async-done | bytes 655392 | tf_op jit(solution)/shard_map/all_to_all | solution.py:270
  39.8 0.0 copy-done.2
  39.8 1.8 %attend.1 = bf16[8,136,128]{2,1,0:T(8,128)(2,1)} custom-call(s32[1,4]{1,0:T(1,128)S(1)} %bitcast.6, bf16[64,40,128]{2,1,0:T(8,128)(2,1)S(1)} %all-to-all-done.rows_ref), custom_call_target="tpu_custom_call" | custom-call | tf_op jit(solution)/shard_map/attend/pallas_call | solution.py:271
  41.5 0.0 collective-permute-done.other_ref
  41.6 4.6 %all-to-all-start.1 = ((bf16[8,136,128]{2,1,0:T(8,128)(2,1)}), bf16[8,136,128]{2,1,0:T(8,128)(2,1)S(1)}, u32[]{:S(2)}, u32[]{:S(2)}) async-start(bf16[8,136,128]{2,1,0:T(8,128)(2,1)} %attend.1), calls=%async_computation.1 | async-start | bytes 557056 | tf_op jit(solution)/shard_map/all_to_all | solution.py:285
  46.1 0.0 collective-permute-done.1.theirs_ref
  46.1 2.0 %collective-permute-start.2 = (bf16[320,640]{1,0:T(8,128)(2,1)S(1)}, bf16[320,640]{1,0:T(8,128)(2,1)S(1)}, u32[]{:S(2)}, u32[]{:S(2)}) collective-permute-start(bf16[320,640]{1,0:T(8,128)(2,1)S(1)} %collective-permute-done.1.theirs_ref), channel_id=1, source_target_pairs={{0,16},{16,0},{1,17},{17,1},{2,18},{18,2},{3,19},{19,3},{4,20},{20... | collective-permute-start | bytes 1228808 | tf_op jit(solution)/shard_map/ppermute | solution.py:247
  48.2 1.6 %collective-permute-done.2.theirs_other_ref = bf16[320,640]{1,0:T(8,128)(2,1)S(1)} collective-permute-done((bf16[320,640]{1,0:T(8,128)(2,1)S(1)}, bf16[320,640]{1,0:T(8,128)(2,1)S(1)}, u32[]{:S(2)}, u32[]{:S(2)}) %collective-permute-start.2) | collective-permute-done | bytes 409632 | tf_op jit(solution)/shard_map/ppermute | solution.py:247
  49.8 3.9 %all-to-all-done.1.parts_ref = bf16[8,136,128]{2,1,0:T(8,128)(2,1)S(1)} async-done(((bf16[8,136,128]{2,1,0:T(8,128)(2,1)}), bf16[8,136,128]{2,1,0:T(8,128)(2,1)S(1)}, u32[]{:S(2)}, u32[]{:S(2)}) %all-to-all-start.1) | async-done | bytes 278560 | tf_op jit(solution)/shard_map/all_to_all | solution.py:285
  53.7 0.6 merge.1
  54.3 26.0 %all_to_all.20.rows_ref = bf16[16,64,256]{2,1,0:T(8,128)(2,1)S(1)} all-to-all(bf16[16,64,256]{2,1,0:T(8,128)(2,1)S(1)} %merge.1), channel_id=1, replica_groups=mesh['span'=4,'ring'=4,'core'=2,'far'=4,'side'=2,'part'=2] {'far','part'..., dimensions={0} | all-to-all | bytes 1048576 | tf_op jit(solution)/shard_map/all_to_all | solution.py:296
  80.3 0.8 project.1
  81.1 11.6 %all_to_all.21.parts_ref = bf16[8,120,128]{2,1,0:T(8,128)(2,1)S(1)} all-to-all(bf16[8,120,128]{2,1,0:T(8,128)(2,1)S(1)} %project.1), channel_id=1, replica_groups=mesh['span'=4,'ring'=4,'core'=2,'far'=4,'side'=2,'part'=2] {'side','ring'}, dimensions={0} | all-to-all | bytes 491520 | tf_op jit(solution)/shard_map/all_to_all | solution.py:305
  92.7 0.7 finish.1
  (1 shorter events, 0.0 us)
Async XLA Ops:
  0.0 27.1 %copy-start = (f32[50,320]{1,0:T(8,128)S(1)}, f32[50,320]{1,0:T(8,128)}, u32[]{:S(2)}) copy-start(f32[50,320]{1,0:T(8,128)} %param.11) | copy-start | bytes 192004
  1.9 16.7 %copy-start.1 = (bf16[640,320]{0,1:T(8,128)(2,1)S(1)}, bf16[640,320]{0,1:T(8,128)(2,1)}, u32[]{:S(2)}) copy-start(bf16[640,320]{0,1:T(8,128)(2,1)} %param.10) | copy-start | bytes 1228804
  1.9 37.9 %all-to-all-start = ((bf16[64,40,128]{2,1,0:T(8,128)(2,1)}), bf16[64,40,128]{2,1,0:T(8,128)(2,1)S(1)}, u32[]{:S(2)}, u32[]{:S(2)}) async-start(bf16[64,40,128]{2,1,0:T(8,128)(2,1)} %pack.1), calls=%async_computation | async-start | bytes 1310720 | tf_op jit(solution)/shard_map/all_to_all | solution.py:270
  18.6 23.0 %collective-permute-start = (bf16[320,640]{1,0:T(8,128)(2,1)S(1)}, bf16[320,640]{1,0:T(8,128)(2,1)S(1)}, u32[]{:S(2)}, u32[]{:S(2)}) collective-permute-start(bf16[320,640]{1,0:T(8,128)(2,1)S(1)} %bitcast.3), channel_id=1, source_target_pairs={{0,16},{16,0},{1,17},{17,1},{2,18},{18,2},{3,19},{19,3},{4,20},{20... | collective-permute-start | bytes 1228808 | tf_op jit(solution)/shard_map/ppermute | solution.py:247
  20.5 25.6 %collective-permute-start.1 = (bf16[320,640]{1,0:T(8,128)(2,1)S(1)}, bf16[320,640]{1,0:T(8,128)(2,1)S(1)}, u32[]{:S(2)}, u32[]{:S(2)}) collective-permute-start(bf16[320,640]{1,0:T(8,128)(2,1)S(1)} %bitcast.4), channel_id=1, source_target_pairs={{0,2},{2,0},{1,3},{3,1},{4,6},{6,4},{5,7},{7,5},{8,10},{10,8},{9,1... | collective-permute-start | bytes 1228808 | tf_op jit(solution)/shard_map/ppermute | solution.py:243
  23.9 0.7 copy-start.3
  27.1 12.6 %copy-start.2 = (s32[4]{0:T(128)S(1)}, s32[4]{0:T(128)}, u32[]{:S(2)}) copy-start(s32[4]{0:T(128)} %param.13) | copy-start | bytes 52
  41.6 12.1 %all-to-all-start.1 = ((bf16[8,136,128]{2,1,0:T(8,128)(2,1)}), bf16[8,136,128]{2,1,0:T(8,128)(2,1)S(1)}, u32[]{:S(2)}, u32[]{:S(2)}) async-start(bf16[8,136,128]{2,1,0:T(8,128)(2,1)} %attend.1), calls=%async_computation.1 | async-start | bytes 557056 | tf_op jit(solution)/shard_map/all_to_all | solution.py:285
  46.1 3.6 %collective-permute-start.2 = (bf16[320,640]{1,0:T(8,128)(2,1)S(1)}, bf16[320,640]{1,0:T(8,128)(2,1)S(1)}, u32[]{:S(2)}, u32[]{:S(2)}) collective-permute-start(bf16[320,640]{1,0:T(8,128)(2,1)S(1)} %collective-permute-done.1.theirs_ref), channel_id=1, source_target_pairs={{0,16},{16,0},{1,17},{17,1},{2,18},{18,2},{3,19},{19,3},{4,20},{20... | collective-permute-start | bytes 1228808 | tf_op jit(solution)/shard_map/ppermute | solution.py:247
